TPU v7x, 32 devices: a whole 2x2x4 slice. The times are simulated.
32 devices in a mesh: rows: 8 (over y, x, core), mem: 4 (over z).
Axes of the slice: x: 2, y: 2, z: 4, core: 2. Of those that a mesh axis runs over, the one named last changes fastest.
Arguments:
- questions: bfloat16 [16, 1024, 768], P('rows', 'mem'), may hold values from -6 to 6
- answers: bfloat16 [16, 1024, 768], P('rows', 'mem'), may hold values from -6 to 6
- q_segments: int32 [16, 1024], P('rows'), may hold values from 0 to 7, never falling along the last dimension, each value on 1 to 769 neighbouring positions
- a_segments: int32 [16, 1024], P('rows'), may hold values from 0 to 7, never falling along the last dimension, each value on 1 to 769 neighbouring positions
- entry_ids: int32 [16, 8, 12], P('rows', None, 'mem'), may hold values from 0 to 4095
- entry_alive_flags: int32 [16, 8, 12], P('rows'), may hold values from 0 to 1, as said below
- memory_table: bfloat16 [4096, 2, 768], replicated, may hold values from -6 to 6
- enc_params: bfloat16 [768, 9216], P(None, ('rows', 'mem')), as said below
- dec_params: bfloat16 [768, 12288], P(None, ('rows', 'mem')), as said below
- norm_gains: float32 [6, 768], replicated, may hold values from 0.1 to 1.9
- cotangent: float32 [16, 1024, 768], P('rows', 'mem'), may hold values from -6 to 6
Outputs:
- decoded: bfloat16 [16, 1024, 768], P('rows', 'mem')
- grad_questions: float32 [16, 1024, 768], P('rows', 'mem')
- grad_answers: float32 [16, 1024, 768], P('rows', 'mem')
- grad_encoder: float32 [768, 9216], P(None, ('rows', 'mem'))
- grad_decoder: float32 [768, 12288], P(None, ('rows', 'mem'))
- grad_gains: float32 [6, 768], replicated
Inputs may be any that keep to these rules, and one draw needn't show every extreme that they name: `entry_alive_flags`: each question has exactly 10 live slots of its 12. `enc_params`: entries lie within 9 / sqrt(768) in magnitude. `dec_params`: entries lie within 9 / sqrt(768) in magnitude.
All inputs are finite; a program needn't handle non-finite values.
Results may differ from a plain program's by a relative error of at most 0.025.
Values may be sent and summed in bfloat16 or wider, within the bound.
A program may use at most 384 MiB of HBM per device.

v0:
```python
import jax
import jax.numpy as jnp
from jax import lax
from jax.sharding import PartitionSpec as P

D = 768
H = 12
HD = 64
FF = 3072


epsilon = 1e-06
masked_score = -1e30


def rms_norm(values, gain):
    return values * lax.rsqrt(jnp.mean(values * values, -1, keepdims=True) + epsilon) * gain


def norm_back(values, gain, grad):
    unused, pull = jax.vjp(rms_norm, values, gain)
    return pull(grad)


def project(left, weight):
    return jnp.einsum("...d,de->...e", left, weight, preferred_element_type=jnp.float32)


def project_back(left, weight):
    return jnp.einsum("...e,de->...d", left, weight, preferred_element_type=jnp.float32)


def outer_sum(left, right):
    flat_left = left.reshape(-1, left.shape[-1])
    flat_right = right.reshape(-1, right.shape[-1])
    return jnp.einsum("nd,ne->de", flat_left, flat_right, preferred_element_type=jnp.float32)


def split_heads(values):
    return values.reshape(values.shape[0], values.shape[1], H, HD)


def scores_of(queries, keys, mask):
    raw = jnp.einsum(
        "rqhd,rkhd->rhqk",
        split_heads(queries),
        split_heads(keys),
        preferred_element_type=jnp.float32,
    ) * HD ** (-0.5)
    return jnp.where(mask[:, None], raw, masked_score)


def attend(queries, keys, values, mask):
    scores = scores_of(queries, keys, mask)
    largest = jnp.max(scores, -1, keepdims=True)
    layer_weight_tree = jnp.exp(scores - largest)
    total = jnp.sum(layer_weight_tree, -1, keepdims=True)
    probs = (layer_weight_tree / total).astype(jnp.bfloat16)
    mixed = jnp.einsum(
        "rhqk,rkhd->rqhd", probs, split_heads(values), preferred_element_type=jnp.float32
    )
    return (mixed.reshape(queries.shape), largest + jnp.log(total))


def attend_back(queries, keys, values, mask, logsum, grad_out):
    probs = jnp.exp(scores_of(queries, keys, mask) - logsum)
    gradient_per_head = split_heads(grad_out)
    grad_probs = jnp.einsum(
        "rqhd,rkhd->rhqk",
        gradient_per_head,
        split_heads(values),
        preferred_element_type=jnp.float32,
    )
    inner = jnp.sum(probs * grad_probs, -1, keepdims=True)
    grad_scores = (probs * (grad_probs - inner)).astype(jnp.bfloat16)
    grad_q = jnp.einsum(
        "rhqk,rkhd->rqhd", grad_scores, split_heads(keys), preferred_element_type=jnp.float32
    ) * HD ** (-0.5)
    grad_k = jnp.einsum(
        "rhqk,rqhd->rkhd", grad_scores, split_heads(queries), preferred_element_type=jnp.float32
    ) * HD ** (-0.5)
    grad_v = jnp.einsum(
        "rhqk,rqhd->rkhd",
        probs.astype(jnp.bfloat16),
        gradient_per_head,
        preferred_element_type=jnp.float32,
    )
    return (grad_q.reshape(queries.shape), grad_k.reshape(keys.shape), grad_v.reshape(keys.shape))


def output_back(grad, mixed_b, w_out):
    grad_b = grad.astype(jnp.bfloat16)
    return (outer_sum(grad_b, mixed_b), project(grad_b, w_out).astype(jnp.bfloat16))


def feed_back(grad, normed_b, pre_act, act_b, w_in, w_out):
    grad_b = grad.astype(jnp.bfloat16)
    grad_wout = outer_sum(grad_b, act_b)
    grad_act = project(grad_b, w_out)
    unused, pull = jax.vjp(jax.nn.gelu, pre_act)
    grad_pre = pull(grad_act)[0].astype(jnp.bfloat16)
    return (outer_sum(normed_b, grad_pre), grad_wout, project_back(grad_pre, w_in))


def on_device(
    questions,
    answers,
    q_segments,
    a_segments,
    entry_ids,
    entry_alive_flags,
    memory_table,
    enc_params,
    dec_params,
    norm_gains,
    cotangent,
):
    enc_weights, dec_weights = (
        lax.all_gather(enc_params, ("rows", "mem"), axis=1, tiled=True),
        lax.all_gather(dec_params, ("rows", "mem"), axis=1, tiled=True),
    )
    rows_here, own_len = (questions.shape[0], questions.shape[1])
    row_len = q_segments.shape[1]
    per_row, slots_dev = (entry_ids.shape[1], entry_ids.shape[2])
    n_mem = lax.axis_size("mem")
    start = lax.axis_index("mem") * own_len
    own_pos = start + jnp.arange(own_len, dtype=jnp.int32)
    q_own = lax.dynamic_slice_in_dim(q_segments, start, own_len, 1)
    a_own = lax.dynamic_slice_in_dim(a_segments, start, own_len, 1)
    x_question = questions.astype(jnp.float32)
    normed_q = rms_norm(x_question, norm_gains[0]).astype(jnp.bfloat16)
    qkv_enc = project(normed_q, enc_weights[:, : 3 * D]).astype(jnp.bfloat16)
    entry_vals = memory_table[entry_ids].astype(jnp.float32)
    prefix_b = rms_norm(entry_vals, norm_gains[0]).astype(jnp.bfloat16)
    prefix_kv = (
        project(prefix_b, enc_weights[:, D : 3 * D])
        .astype(jnp.bfloat16)
        .reshape(rows_here, per_row * slots_dev * 2, 2 * D)
    )
    token_kv, gathered_pre = (
        lax.all_gather(qkv_enc[..., D:], "mem", axis=1, tiled=True),
        lax.all_gather(prefix_kv, "mem", axis=1, tiled=True),
    )
    enc_keys = jnp.concatenate([token_kv[..., :D], gathered_pre[..., :D]], 1)
    enc_vals = jnp.concatenate([token_kv[..., D:], gathered_pre[..., D:]], 1)
    places = jnp.arange(n_mem * per_row * slots_dev * 2, dtype=jnp.int32)
    owner = places // (per_row * slots_dev * 2)
    question = places // (slots_dev * 2) % per_row
    slot_num = owner * slots_dev + places % (slots_dev * 2) // 2
    live_pre = entry_alive_flags[:, question, slot_num]
    prefix_mask = (q_own[:, :, None] == question[None, None, :]) & (live_pre[:, None, :] == 1)
    enc_mask = jnp.concatenate([q_own[:, :, None] == q_segments[:, None, :], prefix_mask], 2)
    query_enc = qkv_enc[..., :D]
    mixed_enc, logsum_enc = attend(query_enc, enc_keys, enc_vals, enc_mask)
    mixed_enc_b = mixed_enc.astype(jnp.bfloat16)
    hidden_one = x_question + project_back(mixed_enc_b, enc_weights[:, 3 * D : 4 * D])
    normed_f1 = rms_norm(hidden_one, norm_gains[1]).astype(jnp.bfloat16)
    pre_enc = project(normed_f1, enc_weights[:, 4 * D : 4 * D + FF])
    act_enc = jax.nn.gelu(pre_enc).astype(jnp.bfloat16)
    hidden_two = hidden_one + project_back(act_enc, enc_weights[:, 4 * D + FF :])
    encoded = rms_norm(hidden_two, norm_gains[5]).astype(jnp.bfloat16)
    x_answer = answers.astype(jnp.float32)
    normed_a = rms_norm(x_answer, norm_gains[2]).astype(jnp.bfloat16)
    qkv_self = project(normed_a, dec_weights[:, : 3 * D]).astype(jnp.bfloat16)
    cross_kv = project(encoded, dec_weights[:, 5 * D : 7 * D]).astype(jnp.bfloat16)
    self_all, cross_all = (
        lax.all_gather(qkv_self[..., D:], "mem", axis=1, tiled=True),
        lax.all_gather(cross_kv, "mem", axis=1, tiled=True),
    )
    all_pos = jnp.arange(row_len, dtype=jnp.int32)
    self_mask = (a_own[:, :, None] == a_segments[:, None, :]) & (
        all_pos[None, None, :] <= own_pos[None, :, None]
    )
    self_query_rows = qkv_self[..., :D]
    mixed_self, logsum_self = attend(
        self_query_rows, self_all[..., :D], self_all[..., D:], self_mask
    )
    mixed_self_b = mixed_self.astype(jnp.bfloat16)
    dec_one = x_answer + project_back(mixed_self_b, dec_weights[:, 3 * D : 4 * D])
    normed_c = rms_norm(dec_one, norm_gains[3]).astype(jnp.bfloat16)
    query_cross = project(normed_c, dec_weights[:, 4 * D : 5 * D]).astype(jnp.bfloat16)
    cross_mask = a_own[:, :, None] == q_segments[:, None, :]
    mixed_cross, logsum_cross = attend(
        query_cross, cross_all[..., :D], cross_all[..., D:], cross_mask
    )
    mixed_cross_b = mixed_cross.astype(jnp.bfloat16)
    dec_two = dec_one + project_back(mixed_cross_b, dec_weights[:, 7 * D : 8 * D])
    normed_f2 = rms_norm(dec_two, norm_gains[4]).astype(jnp.bfloat16)
    pre_dec = project(normed_f2, dec_weights[:, 8 * D : 8 * D + FF])
    act_dec = jax.nn.gelu(pre_dec).astype(jnp.bfloat16)
    dec_three = dec_two + project_back(act_dec, dec_weights[:, 8 * D + FF :])
    decoded = dec_three.astype(jnp.bfloat16)
    grad_w1d, grad_w2d, grad_nf2 = feed_back(
        cotangent,
        normed_f2,
        pre_dec,
        act_dec,
        dec_weights[:, 8 * D : 8 * D + FF],
        dec_weights[:, 8 * D + FF :],
    )
    grad_x, grad_gain4 = norm_back(dec_two, norm_gains[4], grad_nf2)
    grad_two = cotangent + grad_x
    grad_woc, grad_mixc = output_back(grad_two, mixed_cross_b, dec_weights[:, 7 * D : 8 * D])
    grad_qc, grad_kc, grad_vc = attend_back(
        query_cross, cross_all[..., :D], cross_all[..., D:], cross_mask, logsum_cross, grad_mixc
    )
    grad_ckv = lax.psum_scatter(
        jnp.concatenate([grad_kc, grad_vc], -1).astype(jnp.bfloat16),
        "mem",
        scatter_dimension=1,
        tiled=True,
    )
    grad_qc_b = grad_qc.astype(jnp.bfloat16)
    grad_wqc = outer_sum(normed_c, grad_qc_b)
    grad_x, grad_gain3 = norm_back(
        dec_one, norm_gains[3], project_back(grad_qc_b, dec_weights[:, 4 * D : 5 * D])
    )
    grad_one = grad_two + grad_x
    grad_wckv = outer_sum(encoded, grad_ckv)
    grad_encoded, grad_gain5 = norm_back(
        hidden_two, norm_gains[5], project_back(grad_ckv, dec_weights[:, 5 * D : 7 * D])
    )
    grad_wos, grad_mixs = output_back(grad_one, mixed_self_b, dec_weights[:, 3 * D : 4 * D])
    gradient_self_queries, grad_ks, grad_vs = attend_back(
        self_query_rows, self_all[..., :D], self_all[..., D:], self_mask, logsum_self, grad_mixs
    )
    gradient_self_key_value = lax.psum_scatter(
        jnp.concatenate([grad_ks, grad_vs], -1).astype(jnp.bfloat16),
        "mem",
        scatter_dimension=1,
        tiled=True,
    ).astype(jnp.float32)
    gradient_self_query_key_value = jnp.concatenate(
        [gradient_self_queries, gradient_self_key_value], -1
    ).astype(jnp.bfloat16)
    grad_wsqkv = outer_sum(normed_a, gradient_self_query_key_value)
    grad_x, grad_gain2 = norm_back(
        x_answer,
        norm_gains[2],
        project_back(gradient_self_query_key_value, dec_weights[:, : 3 * D]),
    )
    grad_answers = grad_one + grad_x
    dec_full = jnp.concatenate(
        [grad_wsqkv, grad_wos, grad_wqc, grad_wckv, grad_woc, grad_w1d, grad_w2d], 1
    )
    grad_w1e, grad_w2e, grad_nf1 = feed_back(
        grad_encoded,
        normed_f1,
        pre_enc,
        act_enc,
        enc_weights[:, 4 * D : 4 * D + FF],
        enc_weights[:, 4 * D + FF :],
    )
    grad_x, grad_gain1 = norm_back(hidden_one, norm_gains[1], grad_nf1)
    grad_hidden = grad_encoded + grad_x
    grad_woe, grad_mixe = output_back(grad_hidden, mixed_enc_b, enc_weights[:, 3 * D : 4 * D])
    grad_qe, grad_keys, grad_vals = attend_back(
        query_enc, enc_keys, enc_vals, enc_mask, logsum_enc, grad_mixe
    )
    grad_tok, grad_pre = (
        lax.psum_scatter(
            jnp.concatenate([grad_keys[:, :row_len], grad_vals[:, :row_len]], -1).astype(
                jnp.bfloat16
            ),
            "mem",
            scatter_dimension=1,
            tiled=True,
        ).astype(jnp.float32),
        lax.psum_scatter(
            jnp.concatenate([grad_keys[:, row_len:], grad_vals[:, row_len:]], -1).astype(
                jnp.bfloat16
            ),
            "mem",
            scatter_dimension=1,
            tiled=True,
        ).astype(jnp.float32),
    )
    grad_qkv = jnp.concatenate([grad_qe, grad_tok], -1).astype(jnp.bfloat16)
    grad_wqkv = outer_sum(normed_q, grad_qkv)
    grad_pre_b = grad_pre.astype(jnp.bfloat16).reshape(rows_here, per_row, slots_dev, 2, 2 * D)
    grad_wpre = outer_sum(prefix_b, grad_pre_b)
    unused, grad_gain0b = norm_back(
        entry_vals, norm_gains[0], project_back(grad_pre_b, enc_weights[:, D : 3 * D])
    )
    grad_x, grad_gain0 = norm_back(
        x_question, norm_gains[0], project_back(grad_qkv, enc_weights[:, : 3 * D])
    )
    grad_questions = grad_hidden + grad_x
    grad_attn_in = grad_wqkv + jnp.pad(grad_wpre, ((0, 0), (D, 0)))
    enc_full = jnp.concatenate([grad_attn_in, grad_woe, grad_w1e, grad_w2e], 1)
    gain_terms = jnp.stack(
        [grad_gain0 + grad_gain0b, grad_gain1, grad_gain2, grad_gain3, grad_gain4, grad_gain5]
    )
    grad_gains = lax.psum(gain_terms, ("rows", "mem"))
    grad_encoder, grad_decoder = (
        lax.psum_scatter(enc_full, ("rows", "mem"), scatter_dimension=1, tiled=True),
        lax.psum_scatter(dec_full, ("rows", "mem"), scatter_dimension=1, tiled=True),
    )
    return (decoded, grad_questions, grad_answers, grad_encoder, grad_decoder, grad_gains)


def solution(mesh):
    return jax.shard_map(
        on_device,
        mesh=mesh,
        in_specs=(
            P("rows", "mem", None),
            P("rows", "mem", None),
            P("rows", None),
            P("rows", None),
            P("rows", None, "mem"),
            P("rows", None, None),
            P(),
            P(None, ("rows", "mem")),
            P(None, ("rows", "mem")),
            P(),
            P("rows", "mem", None),
        ),
        out_specs=(
            P("rows", "mem", None),
            P("rows", "mem", None),
            P("rows", "mem", None),
            P(None, ("rows", "mem")),
            P(None, ("rows", "mem")),
            P(),
        ),
        check_vma=False,
    )
```

profile of v0, /device:TPU:0, one launch (start us, length us, event | category | flops | bytes accessed | tf_op | source)
XLA Modules:
  0.0 1783.3 jit_solution(1994056367633672591)
XLA Ops:
  16.5 100.2 %all-gather.11.cloned.1.call-done = bf16[768,9216]{0,1:T(8,128)(2,1)} async-done(((bf16[768,288]{0,1:T(8,128)(2,1)}), bf16[768,9216]{0,1:T(8,128)(2,1)}) %all-gather.11.cloned.1.call-update) | async-done | bytes 14155792 | tf_op jit(solution)/shard_map/all_gather | solution.py:119
  135.2 13.9 all-gather.15.cloned.1.call-done
  150.4 131.1 %all-gather.7.cloned.1.call-done = bf16[768,12288]{1,0:T(8,128)(2,1)} async-done(((bf16[768,384]{1,0:T(8,128)(2,1)}), bf16[768,12288]{1,0:T(8,128)(2,1)}) %all-gather.7.cloned.1.call-update) | async-done | bytes 18874384 | tf_op jit(solution)/shard_map/all_gather | solution.py:120
  288.9 108.2 %all-gather.13.cloned.1.call-done = bf16[2,1024,1536]{2,1,0:T(8,128)(2,1)} async-done(((bf16[2,256,1536]{2,1,0:T(8,128)(2,1)}), bf16[2,1024,1536]{2,1,0:T(8,128)(2,1)}) %all-gather.13.cloned.1.call-update) | async-done | bytes 6291472 | tf_op jit(solution)/shard_map/all_gather | solution.py:141
  416.2 13.9 fusion.125
  430.1 12.5 fusion
  442.6 12.4 fusion.75
  478.1 34.5 %all-gather.9.cloned.1.call-done = bf16[2,1024,1536]{2,1,0:T(8,128)(2,1)} async-done(((bf16[2,256,1536]{2,1,0:T(8,128)(2,1)}), bf16[2,1024,1536]{2,1,0:T(8,128)(2,1)}) %all-gather.9.cloned.1.call-update) | async-done | bytes 6291472 | tf_op jit(solution)/shard_map/all_gather | solution.py:167
  527.6 12.1 fusion.18
  539.7 12.0 fusion.2
  551.7 11.8 fusion.74
  570.5 57.7 %all-gather.17.cloned.1.call-done = bf16[2,1024,1536]{2,1,0:T(8,128)(2,1)} async-done(((bf16[2,256,1536]{2,1,0:T(8,128)(2,1)}), bf16[2,1024,1536]{2,1,0:T(8,128)(2,1)}) %all-gather.17.cloned.1.call-update) | async-done | bytes 6291472 | tf_op jit(solution)/shard_map/all_gather | solution.py:168
  637.3 12.1 fusion.19
  649.4 12.0 fusion.3
  666.1 12.6 fusion.73
  710.8 19.4 %multiply_reduce_fusion.2 = (f32[2,12,256]{2,1,0:T(8,128)S(1)}, f32[2,12,256,1024]{3,2,1,0:T(8,128)}) fusion(f32[2,12,256]{2,1,0:T(8,128)S(1)} %log_add_fusion.2, f32[2,12,256,1024]{3,2,1,0:T(8,128)} %get-tuple-element.70, pred[2,256,1024]{2,1,0:T(8,128)(4,1)} %get-tuple-element.56, bf16[2,256,12,64]{1,3,2,0:T(8,128)(2,1)} %bitcast.258, ...), kind=kOutput, calls=%fused_computation.14 | convolution fusion | flops 836757504 | bytes 54837248 | tf_op jit(solution)/shard_map/rqhd,rkhd->rhqk/dot_general | solution.py:68
  730.2 15.7 fusion.47
  745.9 17.0 multiply_convert_fusion.2
  801.7 19.5 %multiply_reduce_fusion.1 = (f32[2,12,256]{2,1,0:T(8,128)S(1)}, f32[2,12,256,1024]{3,2,1,0:T(8,128)}) fusion(f32[2,12,256]{2,1,0:T(8,128)S(1)} %log_add_fusion, f32[2,12,256,1024]{3,2,1,0:T(8,128)} %get-tuple-element.60, pred[2,256,1024]{2,1,0:T(8,128)(4,1)S(1)} %copy-done.20, bf16[2,256,12,64]{1,3,2,0:T(8,128)(2,1)S(1)} %bitcast.256, ...), kind=kOutput, calls=%fused_computation.11 | convolution fusion | flops 836757504 | bytes 54837248 | tf_op jit(solution)/shard_map/rqhd,rkhd->rhqk/dot_general | solution.py:68
  821.2 17.0 multiply_convert_fusion.1
  845.6 12.9 fusion.50
  868.5 24.5 %reduce-scatter.9.cloned.1.call-done = bf16[2,256,1536]{2,1,0:T(8,128)(2,1)} async-done(((bf16[2,1024,1536]{2,1,0:T(8,128)(2,1)}), bf16[2,256,1536]{2,1,0:T(8,128)(2,1)}) %reduce-scatter.9.cloned.1.call-update) | async-done | bytes 1572880 | tf_op jit(solution)/shard_map/reduce_scatter | solution.py:207
  918.0 21.8 %multiply_reduce_fusion = (f32[2,12,256]{2,1,0:T(8,128)S(1)}, f32[2,12,256,1216]{2,3,1,0:T(8,128)}) fusion(f32[2,12,256,1216]{2,3,1,0:T(8,128)} %get-tuple-element.62, f32[2,12,256]{2,1,0:T(8,128)S(1)} %log_add_fusion.1, bf16[2,256,12,64]{1,3,2,0:T(8,128)(2,1)S(1)} %bitcast.244, bf16[2,1216,12,64]{1,3,2,0:T(8,128)(2,1)} %bitcast.233), kind=kOutput, calls=%fused_computation.3 | convolution fusion | flops 978708480 | bytes 64339968 | tf_op jit(solution)/shard_map/rqhd,rkhd->rhqk/dot_general | solution.py:68
  939.8 25.1 %multiply_convert_fusion = bf16[2,12,256,1216]{2,3,1,0:T(8,128)(2,1)} fusion(f32[2,12,256,1216]{2,3,1,0:T(8,128)} %get-tuple-element.79, f32[2,12,256,1216]{2,3,1,0:T(8,128)} %get-tuple-element.62, f32[2,12,256]{2,1,0:T(8,128)S(1)} %get-tuple-element.78, f32[2,12,256]{2,1,0:T(8,128)S(1)} %log_add_fusion.1), kind=kLoop, calls=%fused_computation.2 | loop fusion | flops 29884416 | bytes 74760192 | tf_op jit(solution)/shard_map/convert_element_type | solution.py:75
  964.9 11.5 multiply_convert_fusion.3
  977.9 14.1 fusion.34
  1090.1 60.1 %reduce-scatter.11.cloned.1.call-done = bf16[2,256,1536]{2,1,0:T(8,128)(2,1)} async-done(((bf16[2,1024,1536]{2,1,0:T(8,128)(2,1)}), bf16[2,256,1536]{2,1,0:T(8,128)(2,1)}) %reduce-scatter.11.cloned.1.call-update) | async-done | bytes 1572880 | tf_op jit(solution)/shard_map/reduce_scatter | solution.py:261
  1158.6 22.0 %pad_maximum_fusion = f32[768,9216]{1,0:T(8,128)} fusion(f32[768,3072]{1,0:T(8,128)} %convolution_bitcast_fusion, f32[768,3072]{1,0:T(8,128)} %convolution_bitcast_fusion.1, f32[768,768]{1,0:T(8,128)} %convolution_bitcast_fusion.2, f32[768,2304]{1,0:T(8,128)} %bitcast_add_fusion), kind=kLoop, calls=%fused_computation.8 | loop fusion | flops 21233664 | bytes 56623104 | tf_op jit(solution)/shard_map/concatenate | solution.py:290
  1180.6 30.4 %copy.251 = f32[768,9216]{0,1:T(8,128)} copy(f32[768,9216]{1,0:T(8,128)} %pad_maximum_fusion) | data formatting | bytes 56623104
  1236.3 43.8 %psum.7 = f32[6,768]{1,0:T(8,128)} all-reduce(f32[6,768]{1,0:T(8,128)S(1)} %stack.24), channel_id=1, replica_groups=mesh['rows'=8,'mem'=4] {'rows','mem'}, use_global_device_ids=true, to_apply=%region_35.36 | all-reduce | flops 4608 | bytes 36864 | tf_op jit(solution)/shard_map/psum | solution.py:294
  1283.0 222.5 %reduce-scatter.17.cloned.1.call-done = f32[768,384]{1,0:T(8,128)} async-done(((f32[768,12288]{1,0:T(8,128)}), f32[768,384]{1,0:T(8,128)}) %reduce-scatter.17.cloned.1.call-update) | async-done | bytes 1179664 | tf_op jit(solution)/shard_map/reduce_scatter | solution.py:297
  1505.6 270.7 %reduce-scatter.19.cloned.1.call-done = f32[288,768]{1,0:T(8,128)} async-done(((f32[9216,768]{1,0:T(8,128)}), f32[288,768]{1,0:T(8,128)}) %reduce-scatter.19.cloned.1.call-update) | async-done | bytes 884752
  (409 shorter events, 362.2 us)
Async XLA Ops:
  7.2 109.6 %all-gather.11.cloned.1.call-start = ((), (), s32[]{:S(2)}) async-start(), calls=%async_computation.8 | async-start | bytes 14598144 | tf_op jit(solution)/shard_map/all_gather | solution.py:119
  7.9 141.2 %all-gather.15.cloned.1.call-start = ((), (), s32[]{:S(2)}) async-start(), calls=%async_computation.10 | async-start | bytes 1474560 | tf_op jit(solution)/shard_map/all_gather | solution.py:142
  14.4 106.7 %copy-start.64 = (f32[2,8,3,2,768]{4,3,2,1,0:T(2,128)}, f32[2,8,3,2,768]{4,3,2,1,0:T(2,128)S(1)}, u32[]{:S(2)}) copy-start(f32[2,8,3,2,768]{4,3,2,1,0:T(2,128)S(1)} %convert.56) | copy-start | bytes 884740
  14.4 106.7 %copy-start.28 = (bf16[2,256,768]{2,1,0:T(8,128)(2,1)S(1)}, bf16[2,256,768]{2,1,0:T(8,128)(2,1)}, u32[]{:S(2)}) copy-start(bf16[2,256,768]{2,1,0:T(8,128)(2,1)} %param.11) | copy-start | bytes 2359300
  16.4 105.0 %copy-start.79 = (f32[768]{0:T(1024)}, f32[768]{0:T(1024)S(1)}, u32[]{:S(2)}) copy-start(f32[768]{0:T(1024)S(1)} %get-tuple-element.45) | copy-start | bytes 9220
  16.4 265.1 %copy-start.77 = (f32[768]{0:T(1024)}, f32[768]{0:T(1024)S(1)}, u32[]{:S(2)}) copy-start(f32[768]{0:T(1024)S(1)} %get-tuple-element.46) | copy-start | bytes 9220
  16.4 441.2 %copy-start.73 = (f32[768]{0:T(1024)}, f32[768]{0:T(1024)S(1)}, u32[]{:S(2)}) copy-start(f32[768]{0:T(1024)S(1)} %get-tuple-element.44) | copy-start | bytes 9220
  16.4 455.5 %copy-start.81 = (f32[768]{0:T(1024)}, f32[768]{0:T(1024)S(1)}, u32[]{:S(2)}) copy-start(f32[768]{0:T(1024)S(1)} %get-tuple-element.43) | copy-start | bytes 9220
  16.4 100.3 %copy-start.97 = (f32[2,8,3,2]{1,3,2,0:T(2,128)}, f32[2,8,3,2]{1,3,2,0:T(2,128)S(1)}, u32[]{:S(2)}) copy-start(f32[2,8,3,2]{1,3,2,0:T(2,128)S(1)} %add_rsqrt_fusion) | copy-start | bytes 1156
  16.5 104.9 %copy-start.69 = (bf16[2,8,3,2,768]{4,1,3,2,0:T(8,128)(2,1)}, bf16[2,8,3,2,768]{4,1,3,2,0:T(8,128)(2,1)S(1)}, u32[]{:S(2)}) copy-start(bf16[2,8,3,2,768]{4,1,3,2,0:T(8,128)(2,1)S(1)} %multiply_convert_fusion.15) | copy-start | bytes 442372
  120.4 161.2 %all-gather.7.cloned.1.call-start = ((), (), s32[]{:S(2)}) async-start(), calls=%async_computation.6 | async-start | bytes 19464192 | tf_op jit(solution)/shard_map/all_gather | solution.py:120
  121.1 276.0 %all-gather.13.cloned.1.call-start = ((), (), s32[]{:S(2)}) async-start(), calls=%async_computation.9 | async-start | bytes 7864320 | tf_op jit(solution)/shard_map/all_gather | solution.py:141
  128.3 384.3 %all-gather.9.cloned.1.call-start = ((), (), s32[]{:S(2)}) async-start(), calls=%async_computation.7 | async-start | bytes 7864320 | tf_op jit(solution)/shard_map/all_gather | solution.py:167
  134.6 151.0 %copy-start.83 = (f32[2,256]{1,0:T(2,128)}, f32[2,256]{1,0:T(2,128)S(1)}, u32[]{:S(2)}) copy-start(f32[2,256]{1,0:T(2,128)S(1)} %fusion.94) | copy-start | bytes 6148
  135.2 281.0 %copy-start.30 = (bf16[2,256,768]{1,2,0:T(8,128)(2,1)}, bf16[2,256,768]{1,2,0:T(8,128)(2,1)S(1)}, u32[]{:S(2)}) copy-start(bf16[2,256,768]{1,2,0:T(8,128)(2,1)S(1)} %copy.189) | copy-start | bytes 2359300
  288.4 339.9 %all-gather.17.cloned.1.call-start = ((), (), s32[]{:S(2)}) async-start(), calls=%async_computation.11 | async-start | bytes 7864320 | tf_op jit(solution)/shard_map/all_gather | solution.py:168
  476.9 416.0 %reduce-scatter.9.cloned.1.call-start = ((), (), s32[]{:S(2)}) async-start(), calls=%async_computation.12 | async-start | bytes 7864320 | tf_op jit(solution)/shard_map/reduce_scatter | solution.py:207
  566.1 231.6 %copy-start.99 = (f32[2,256]{1,0:T(2,128)}, f32[2,256]{1,0:T(2,128)S(1)}, u32[]{:S(2)}) copy-start(f32[2,256]{1,0:T(2,128)S(1)} %fusion.98) | copy-start | bytes 6148
  783.8 241.5 %reduce-scatter.13.cloned.1.call-start = ((), (), s32[]{:S(2)}) async-start(), calls=%async_computation.14 | async-start | bytes 7864320 | tf_op jit(solution)/shard_map/reduce_scatter | solution.py:227
  868.4 24.6 %copy-start.39 = (f32[2,256,768]{2,1,0:T(8,128)S(1)}, f32[2,256,768]{2,1,0:T(8,128)}, u32[]{:S(2)}) copy-start(f32[2,256,768]{2,1,0:T(8,128)} %copy-done.38) | copy-start | bytes 4718596
  868.4 24.6 %copy-start.82 = (f32[768]{0:T(1024)S(1)}, f32[768]{0:T(1024)}, u32[]{:S(2)}) copy-start(f32[768]{0:T(1024)} %copy-done.81) | copy-start | bytes 9220
  868.4 24.6 %copy-start.94 = (f32[2,256]{1,0:T(2,128)S(1)}, f32[2,256]{1,0:T(2,128)}, u32[]{:S(2)}) copy-start(f32[2,256]{1,0:T(2,128)} %copy-done.93) | copy-start | bytes 6148
  868.4 28.8 %copy-start.111 = (f32[2,256]{1,0:T(2,128)S(1)}, f32[2,256]{1,0:T(2,128)}, u32[]{:S(2)}) copy-start(f32[2,256]{1,0:T(2,128)} %copy-done.110) | copy-start | bytes 6148
  868.4 217.8 %reduce-scatter.15.cloned.1.call-start = ((), (), s32[]{:S(2)}) async-start(), calls=%async_computation.15 | async-start | bytes 1474560 | tf_op jit(solution)/shard_map/reduce_scatter | solution.py:269
  939.8 25.1 %copy-start.31 = (bf16[2,256,768]{1,2,0:T(8,128)(2,1)S(1)}, bf16[2,256,768]{1,2,0:T(8,128)(2,1)}, u32[]{:S(2)}) copy-start(bf16[2,256,768]{1,2,0:T(8,128)(2,1)} %copy-done.30) | copy-start | bytes 2359300
  994.6 155.6 %reduce-scatter.11.cloned.1.call-start = ((), (), s32[]{:S(2)}) async-start(), calls=%async_computation.13 | async-start | bytes 7864320 | tf_op jit(solution)/shard_map/reduce_scatter | solution.py:261
  1012.4 493.1 %reduce-scatter.17.cloned.1.call-start = ((), (), s32[]{:S(2)}) async-start(), calls=%async_computation.16 | async-start | bytes 38928384 | tf_op jit(solution)/shard_map/reduce_scatter | solution.py:297
  1054.3 722.0 %reduce-scatter.19.cloned.1.call-start = ((), (), s32[]{:S(2)}) async-start(), calls=%async_computation.17 | async-start | bytes 29196288
  1086.2 64.1 %copy-start.80 = (f32[768]{0:T(1024)S(1)}, f32[768]{0:T(1024)}, u32[]{:S(2)}) copy-start(f32[768]{0:T(1024)} %copy-done.79) | copy-start | bytes 9220
  1086.2 64.1 %copy-start.96 = (f32[2,256]{1,0:T(2,128)S(1)}, f32[2,256]{1,0:T(2,128)}, u32[]{:S(2)}) copy-start(f32[2,256]{1,0:T(2,128)} %copy-done.95) | copy-start | bytes 6148
  1230.8 49.2 %copy-start.102 = (f32[2,256]{1,0:T(2,128)S(1)}, f32[2,256]{1,0:T(2,128)}, u32[]{:S(2)}) copy-start(f32[2,256]{1,0:T(2,128)} %copy-done.101) | copy-start | bytes 6148
  1230.8 49.3 %copy-start.15 = (f32[2,256,768]{2,1,0:T(8,128)S(1)}, f32[2,256,768]{2,1,0:T(8,128)}, u32[]{:S(2)}) copy-start(f32[2,256,768]{2,1,0:T(8,128)} %copy-done.14) | copy-start | bytes 4718596
  (102 other events, 667.2 us)
Sparse Core Ops, SparseCore 0:
  10.8 105.8 all-gather.10
  120.5 28.5 all-gather.14
  152.0 129.4 all-gather.6
  283.5 113.5 all-gather.12
  399.1 113.5 all-gather.8
  514.6 113.5 all-gather.16
  783.9 108.9 reduce-scatter.8
  895.2 111.2 reduce-scatter.12
  1008.9 29.6 reduce-scatter.14
  1040.7 109.4 reduce-scatter.10
  1157.2 348.2 reduce-scatter.16
  1513.5 262.6 reduce-scatter.18
where the time goes:
time: 1790 us; the launch traced here: 1780 us
  waiting for transfers between devices  1030 us (58%)
  matrix products  397 us (22%)
  local copies, waits for them, and re-layouts  152 us (8%)
  other arithmetic  148 us (8%)
  blocking collectives  43.8 us (2%)
    unnamed x13, waiting for transfers between devices  272 us
    reduce_scatter x1, waiting for transfers between devices, on_device(): lax.psum_scatter(dec_full, ('rows', 'mem'), scatter_dimension=1, tiled=True)  223 us
    all_gather x1, waiting for transfers between devices, on_device(): lax.all_gather(dec_params, ('rows', 'mem'), axis=1, tiled=True)  131 us
    all_gather x1, waiting for transfers between devices, on_device(): lax.all_gather(qkv_enc[..., D:], 'mem', axis=1, tiled=True)  108 us
    all_gather x1, waiting for transfers between devices, on_device(): lax.all_gather(enc_params, ('rows', 'mem'), axis=1, tiled=True)  100 us
    dot_general x3, matrix products, attend_back(): jnp.einsum('rqhd,rkhd->rhqk', gradient_per_head, split_heads(values), pre...  60.7 us
    reduce_scatter x1, waiting for transfers between devices, on_device(): lax.psum_scatter(jnp.concatenate([grad_keys[:, :row_len], grad_vals[:, :r...  60.1 us
    dot_general x12, matrix products, project_back(): jnp.einsum('...e,de->...d', left, weight, preferred_element_type=jnp.floa...  59.8 us
  transfers between devices with their start and end apart: 12, of which 10 were waited for; matrix products, arithmetic and copies ran while one was open for 29% of the time, Pallas kernels for 0%

commit v1 on v0

v1 whole, which is shorter than its diff:
```python
import functools
import jax
import jax.numpy as jnp
from jax import lax
from jax.experimental import pallas as pl
from jax.experimental.pallas import tpu as pltpu
from jax.sharding import PartitionSpec as P

D = 768
H = 12
HD = 64
FF = 3072
QB = 256
masked_score = -1e30


def key_chunks(own_len, extra):
    chunks = []
    for side in (0, 1):
        for at in range(own_len // QB):
            chunks.append((side, at * QB, QB))
        if extra:
            chunks.append((side, own_len, extra))
    return chunks


def attend_kernel(causal, own_len, extra, act, q_ref, qaug_ref, own_k, own_v, oth_k, oth_v, kaug_ref, o_ref, lse_ref, s_ref, m_ref, l_ref, acc_ref):
    low = lax.broadcasted_iota(jnp.int32, (1, 128), 1) < HD
    chunks = key_chunks(own_len, extra)
    nk = own_len + extra
    for qb in range(own_len // QB):
        rows = pl.ds(qb * QB, QB)
        q = q_ref[rows, :] * jnp.bfloat16(HD ** (-0.5))
        qaug = qaug_ref[rows, :]
        queries = (jnp.where(low, q, qaug), jnp.where(low, qaug, q))
        m_ref[...] = jnp.full(m_ref.shape, -3e30, jnp.float32)
        l_ref[...] = jnp.zeros(l_ref.shape, jnp.float32)
        acc_ref[...] = jnp.zeros(acc_ref.shape, jnp.float32)
        for ci, (side, at, size) in enumerate(chunks):

            def score(side=side, at=at, size=size):
                k = (own_k, oth_k)[side][at : at + size, :]
                place = slice(side * nk + at, side * nk + at + size)
                kaug = kaug_ref[place, :]
                for h in (0, 1):
                    cols = slice(h * QB, (h + 1) * QB)
                    keys = jnp.where(low, k, kaug) if h == 0 else jnp.where(low, kaug, k)
                    s = lax.dot_general(keys, queries[h], (((1,), (1,)), ((), ())), preferred_element_type=jnp.float32)
                    if causal and side == 0 and at == qb * QB:
                        tri = lax.broadcasted_iota(jnp.int32, (size, QB), 0) <= lax.broadcasted_iota(jnp.int32, (size, QB), 1)
                        s = jnp.where(tri, s, masked_score)
                    s_ref[place, cols] = s
                    m_ref[:, cols] = jnp.maximum(m_ref[:, cols], jnp.max(s.reshape(size // 8, 8, QB), 0))

            pl.when(act[qb, ci] != 0)(score)
        m = jnp.max(m_ref[...], 0, keepdims=True)
        for ci, (side, at, size) in enumerate(chunks):

            def mix(side=side, at=at, size=size):
                v = (own_v, oth_v)[side][at : at + size, :]
                zero = jnp.zeros_like(v)
                place = slice(side * nk + at, side * nk + at + size)
                p = jnp.exp(s_ref[place, :] - m)
                l_ref[...] += jnp.sum(p.reshape(size // 8, 8, 2 * QB), 0)
                pb = p.astype(jnp.bfloat16)
                pb = jnp.concatenate([pb[:, :QB], pb[:, QB:]], 0)
                v_split = jnp.concatenate([jnp.where(low, v, zero), jnp.where(low, zero, v)], 0)
                acc_ref[...] += lax.dot_general(pb, v_split, (((0,), (0,)), ((), ())), preferred_element_type=jnp.float32)

            pl.when(act[qb, ci] != 0)(mix)
        total = jnp.sum(l_ref[...], 0, keepdims=True)
        lse = m + jnp.log(total)
        rec = 1.0 / total
        wide = lambda row, h: jnp.broadcast_to(row[:, h * QB : (h + 1) * QB], (HD, QB))
        o_ref[rows, :] = (acc_ref[...] * jnp.concatenate([wide(rec, 0), wide(rec, 1)], 0).T).astype(jnp.bfloat16)
        lse_ref[rows, :] = jnp.concatenate([wide(lse, 1), wide(lse, 0)], 0).T


def attend(causal, act, q, qaug, own_kv, oth_kv, kaug):
    t = q.shape[0]
    nk = own_kv.shape[0]
    col = lambda first: pl.BlockSpec((nk, 128), lambda i, a: (0, first + i))
    return pl.pallas_call(
        functools.partial(attend_kernel, causal, t, nk - t),
        grid_spec=pltpu.PrefetchScalarGridSpec(
            num_scalar_prefetch=1,
            grid=(H // 2,),
            in_specs=[
                pl.BlockSpec((t, 128), lambda i, a: (0, i)),
                pl.BlockSpec((t, 128), lambda i, a: (0, 0)),
                col(0), col(H // 2), col(0), col(H // 2),
                pl.BlockSpec((2 * nk, 128), lambda i, a: (0, 0)),
            ],
            out_specs=[pl.BlockSpec((t, 128), lambda i, a: (0, i))] * 2,
            scratch_shapes=[pltpu.VMEM((2 * nk, 2 * QB), jnp.float32), pltpu.VMEM((8, 2 * QB), jnp.float32), pltpu.VMEM((8, 2 * QB), jnp.float32), pltpu.VMEM((QB, 128), jnp.float32)],
        ),
        out_shape=[jax.ShapeDtypeStruct((t, D), jnp.bfloat16), jax.ShapeDtypeStruct((t, D), jnp.float32)],
        compiler_params=pltpu.CompilerParams(vmem_limit_bytes=40 * 1024 * 1024),
        cost_estimate=pl.CostEstimate(flops=4 * t * 2 * nk * D, bytes_accessed=8 * nk * D, transcendentals=t * 2 * nk * H),
        name="attend",
    )(act, q, qaug, own_kv, own_kv, oth_kv, oth_kv, kaug)


def three_parts(value):
    hi = value.astype(jnp.bfloat16).astype(jnp.float32)
    mid = (value - hi).astype(jnp.bfloat16).astype(jnp.float32)
    return hi, mid, value - hi - mid


def spread(base, lane64, value):
    hi, mid, lo = three_parts(value)
    return jnp.where(lane64 == 8, hi, jnp.where(lane64 == 9, mid, jnp.where(lane64 == 10, lo, base)))


def back_kernel(causal, own_len, extra, act, q_ref, qaug_ref, own_k, own_v, oth_k, oth_v, kaug_ref, o_ref, lse_ref, g_ref, dq_ref, dko_ref, dvo_ref, dkt_ref, dvt_ref, dk_acc, dv_acc, dq_acc):
    lane = lax.broadcasted_iota(jnp.int32, (1, 128), 1)
    low = lane < HD
    lane64 = lane % HD
    chunks = key_chunks(own_len, extra)
    nk = own_len + extra
    dk_acc[...] = jnp.zeros(dk_acc.shape, jnp.float32)
    dv_acc[...] = jnp.zeros(dv_acc.shape, jnp.float32)
    ones_aug = jnp.where((lane64 >= 8) & (lane64 <= 10), 1.0, 0.0).astype(jnp.bfloat16)
    for qb in range(own_len // QB):
        rows = pl.ds(qb * QB, QB)
        q = q_ref[rows, :] * jnp.bfloat16(HD ** (-0.5))
        g = g_ref[rows, :]
        qaug = spread(qaug_ref[rows, :].astype(jnp.float32), lane64, -lse_ref[rows, :]).astype(jnp.bfloat16)
        prod = g.astype(jnp.float32) * o_ref[rows, :].astype(jnp.float32)
        d_even = jnp.sum(jnp.where(low, prod, 0.0), -1, keepdims=True)
        d_odd = jnp.sum(jnp.where(low, 0.0, prod), -1, keepdims=True)
        gaug = spread(jnp.zeros((QB, 128), jnp.float32), lane64, -jnp.where(low, d_odd, d_even)).astype(jnp.bfloat16)
        queries = (jnp.where(low, q, qaug), jnp.where(low, qaug, q))
        grads = (jnp.where(low, g, gaug), jnp.where(low, gaug, g))
        zero = jnp.zeros_like(q)
        q_split = jnp.concatenate([jnp.where(low, q, zero), jnp.where(low, zero, q)], 0)
        g_split = jnp.concatenate([jnp.where(low, g, zero), jnp.where(low, zero, g)], 0)
        dq_acc[...] = jnp.zeros(dq_acc.shape, jnp.float32)
        for ci, (side, at, size) in enumerate(chunks):

            def work(side=side, at=at, size=size):
                k = (own_k, oth_k)[side][at : at + size, :]
                v = (own_v, oth_v)[side][at : at + size, :]
                place = slice(side * nk + at, side * nk + at + size)
                kaug = kaug_ref[place, :]
                vaug = jnp.broadcast_to(ones_aug, v.shape)
                zk = jnp.zeros_like(k)
                probs, dscores = [], []
                for h in (0, 1):
                    keys = jnp.where(low, k, kaug) if h == 0 else jnp.where(low, kaug, k)
                    vals = jnp.where(low, v, vaug) if h == 0 else jnp.where(low, vaug, v)
                    s = lax.dot_general(keys, queries[h], (((1,), (1,)), ((), ())), preferred_element_type=jnp.float32)
                    if causal and side == 0 and at == qb * QB:
                        tri = lax.broadcasted_iota(jnp.int32, (size, QB), 0) <= lax.broadcasted_iota(jnp.int32, (size, QB), 1)
                        s = jnp.where(tri, s, masked_score)
                    p = jnp.exp(s)
                    dp = lax.dot_general(vals, grads[h], (((1,), (1,)), ((), ())), preferred_element_type=jnp.float32)
                    dscores.append((p * dp).astype(jnp.bfloat16))
                    probs.append(p.astype(jnp.bfloat16))
                ds = jnp.concatenate(dscores, 1)
                pb = jnp.concatenate(probs, 1)
                dk_acc[place, :] += jnp.dot(ds, q_split, preferred_element_type=jnp.float32)
                dv_acc[place, :] += jnp.dot(pb, g_split, preferred_element_type=jnp.float32)
                k_split = jnp.concatenate([jnp.where(low, k, zk), jnp.where(low, zk, k)], 0)
                dst = jnp.concatenate(dscores, 0)
                dq_acc[...] += lax.dot_general(dst, k_split, (((0,), (0,)), ((), ())), preferred_element_type=jnp.float32)

            pl.when(act[qb, ci] != 0)(work)
        dq_ref[rows, :] = (dq_acc[...] * HD ** (-0.5)).astype(jnp.bfloat16)
    dko_ref[...] = dk_acc[:nk, :]
    dvo_ref[...] = dv_acc[:nk, :]
    dkt_ref[...] = dk_acc[nk:, :].astype(jnp.bfloat16)
    dvt_ref[...] = dv_acc[nk:, :].astype(jnp.bfloat16)


def attend_back(causal, act, q, qaug, own_kv, oth_kv, kaug, mixed, lse, grad):
    t = q.shape[0]
    nk = own_kv.shape[0]
    col = lambda first: pl.BlockSpec((nk, 128), lambda i, a: (0, first + i))
    tok = pl.BlockSpec((t, 128), lambda i, a: (0, i))
    return pl.pallas_call(
        functools.partial(back_kernel, causal, t, nk - t),
        grid_spec=pltpu.PrefetchScalarGridSpec(
            num_scalar_prefetch=1,
            grid=(H // 2,),
            in_specs=[
                tok,
                pl.BlockSpec((t, 128), lambda i, a: (0, 0)),
                col(0), col(H // 2), col(0), col(H // 2),
                pl.BlockSpec((2 * nk, 128), lambda i, a: (0, 0)),
                tok, tok, tok,
            ],
            out_specs=[tok, col(0), col(0), col(0), col(0)],
            scratch_shapes=[pltpu.VMEM((2 * nk, 128), jnp.float32), pltpu.VMEM((2 * nk, 128), jnp.float32), pltpu.VMEM((QB, 128), jnp.float32)],
        ),
        out_shape=[
            jax.ShapeDtypeStruct((t, D), jnp.bfloat16),
            jax.ShapeDtypeStruct((nk, D), jnp.float32),
            jax.ShapeDtypeStruct((nk, D), jnp.float32),
            jax.ShapeDtypeStruct((nk, D), jnp.bfloat16),
            jax.ShapeDtypeStruct((nk, D), jnp.bfloat16),
        ],
        compiler_params=pltpu.CompilerParams(vmem_limit_bytes=40 * 1024 * 1024),
        cost_estimate=pl.CostEstimate(flops=10 * t * 2 * nk * D, bytes_accessed=24 * nk * D, transcendentals=t * 2 * nk * H),
        name="attend_back",
    )(act, q, qaug, own_kv, own_kv, oth_kv, oth_kv, kaug, mixed, lse, grad)


def seg_aug_q(seg):
    j = jnp.arange(128, dtype=jnp.int32) % HD
    return ((j[None, :] < 8) & (j[None, :] == seg[:, None])).astype(jnp.bfloat16)


def seg_aug_k(seg):
    j = jnp.arange(128, dtype=jnp.int32)[None, :] % HD
    bad = (j < 8) & (j != seg[:, None])
    return jnp.where(bad, masked_score, jnp.where((j >= 8) & (j <= 10), 1.0, 0.0)).astype(jnp.bfloat16)


epsilon = 1e-06


def rms_norm(values, gain):
    return values * lax.rsqrt(jnp.mean(values * values, -1, keepdims=True) + epsilon) * gain


def norm_back(values, gain, grad):
    unused, pull = jax.vjp(rms_norm, values, gain)
    return pull(grad)


def project(left, weight_t):
    return jnp.einsum("nd,ed->ne", left, weight_t, preferred_element_type=jnp.float32)


def project_back(left, weight_t):
    return jnp.einsum("ne,ed->nd", left, weight_t, preferred_element_type=jnp.float32)


def outer_sum(wide, narrow):
    return jnp.einsum("ne,nd->ed", wide, narrow, preferred_element_type=jnp.float32).astype(jnp.bfloat16)


def output_back(grad, mixed_b, w_out):
    grad_b = grad.astype(jnp.bfloat16)
    return (outer_sum(mixed_b, grad_b), project(grad_b, w_out).astype(jnp.bfloat16))


def feed_back(grad, normed_b, pre_act, act_b, w_in, w_out):
    grad_b = grad.astype(jnp.bfloat16)
    grad_wout = outer_sum(act_b, grad_b)
    grad_act = project(grad_b, w_out)
    unused, pull = jax.vjp(jax.nn.gelu, pre_act)
    grad_pre = pull(grad_act)[0].astype(jnp.bfloat16)
    return (outer_sum(grad_pre, normed_b), grad_wout, project_back(grad_pre, w_in))


def partner(values):
    n_rows = lax.axis_size("rows")
    return lax.ppermute(values, "rows", [(i, i ^ 1) for i in range(n_rows)])


def my_row(values):
    core = lax.axis_index("rows") % 2
    mem = lax.axis_index("mem")
    chosen = jnp.where(mem // 2 == core, values, partner(values))
    return lax.dynamic_index_in_dim(chosen, mem % 2, 0, keepdims=False)


def quarters_of(core):
    return (jnp.where(core == 0, 0, 1), jnp.where(core == 0, 3, 2))


def own_quarters(row, core, quarter):
    return jnp.concatenate(
        [lax.dynamic_slice_in_dim(row, place * quarter, quarter, 0) for place in quarters_of(core)], 0
    )


def to_rows(values):
    quarter = values.shape[1]
    row = my_row(lax.all_gather(values, "mem", axis=1, tiled=True))
    return own_quarters(row, lax.axis_index("rows") % 2, quarter)


def from_rows(values):
    quarter = values.shape[0] // 2
    core = lax.axis_index("rows") % 2
    mem = lax.axis_index("mem")
    gathered = lax.all_gather(values, "mem", axis=0)
    other = partner(gathered)
    holder = jnp.where((mem == 0) | (mem == 3), 0, 1)
    chosen = jnp.where(holder == core, gathered, other)
    return lax.dynamic_slice(
        chosen, (2 * core, jnp.where(mem < 2, 0, quarter), 0), (2, quarter, values.shape[1])
    )


def gather_weights(params):
    return lax.all_gather(params.T, ("rows", "mem"), axis=0, tiled=True)


def reduce_weights(grads):
    return lax.psum_scatter(grads, ("rows", "mem"), scatter_dimension=0, tiled=True)


def flags_of(q_row, k_row, core, quarter, extra, causal):
    n = q_row.shape[0] // quarter
    ends_q = q_row.reshape(n, quarter)
    ends_k = k_row.reshape(n, quarter)
    meets = (ends_k[None, :, 0] <= ends_q[:, None, -1]) & (ends_q[:, None, 0] <= ends_k[None, :, -1])
    if causal:
        meets &= jnp.arange(n)[None, :] <= jnp.arange(n)[:, None]
    mine = jnp.stack(quarters_of(core))
    others = jnp.stack(quarters_of(1 - core))
    meets = meets[mine]
    always = [jnp.ones((2, 1), bool)] if extra else []
    return jnp.concatenate([meets[:, mine]] + always + [meets[:, others]] + always, 1).astype(jnp.int32)


def both_parts(own, other):
    return jnp.concatenate([own, other], 0)


def on_device(
    questions,
    answers,
    q_segments,
    a_segments,
    entry_ids,
    entry_alive_flags,
    memory_table,
    enc_params,
    dec_params,
    norm_gains,
    cotangent,
):
    quarter = questions.shape[1]
    core = lax.axis_index("rows") % 2
    per_row, slots = entry_alive_flags.shape[1], entry_alive_flags.shape[2]
    half = per_row // 2
    enc_w = gather_weights(enc_params)
    dec_w = gather_weights(dec_params)
    all_ids = lax.all_gather(entry_ids, "mem", axis=2, tiled=True)
    rows_here = questions.shape[0]
    numbers = my_row(
        jnp.concatenate(
            [
                q_segments,
                a_segments,
                entry_alive_flags.reshape(rows_here, -1),
                all_ids.reshape(rows_here, -1),
            ],
            1,
        )
    )
    row_len = q_segments.shape[1]
    q_row = numbers[:row_len]
    a_row = numbers[row_len : 2 * row_len]
    alive = numbers[2 * row_len : 2 * row_len + per_row * slots]
    ids = numbers[2 * row_len + per_row * slots :]
    x_question = to_rows(questions).astype(jnp.float32)
    x_answer = to_rows(answers).astype(jnp.float32)
    grad_top = to_rows(cotangent.astype(jnp.bfloat16)).astype(jnp.float32)

    own_ids = lax.dynamic_slice_in_dim(ids, core * half * slots, half * slots, 0)
    entry_vals = memory_table[own_ids].reshape(half * slots * 2, D).astype(jnp.float32)
    n_prefix = entry_vals.shape[0]
    extra = -(-n_prefix // 128) * 128
    place = jnp.arange(extra, dtype=jnp.int32)

    def prefix_segments(which):
        question = which * half + place // (2 * slots)
        live = lax.dynamic_slice_in_dim(alive, which * half * slots, half * slots, 0)
        live = jnp.pad(jnp.repeat(live, 2), (0, extra - n_prefix))
        return jnp.where(live == 1, question, -1)

    tokens = 2 * quarter
    own_q = own_quarters(q_row, core, quarter)
    other_q = own_quarters(q_row, 1 - core, quarter)
    own_a = own_quarters(a_row, core, quarter)
    other_a = own_quarters(a_row, 1 - core, quarter)
    q_aug, a_aug = seg_aug_q(own_q), seg_aug_q(own_a)
    enc_aug = seg_aug_k(
        jnp.concatenate([own_q, prefix_segments(core), other_q, prefix_segments(1 - core)])
    )
    self_aug = seg_aug_k(jnp.concatenate([own_a, other_a]))
    cross_aug = seg_aug_k(jnp.concatenate([own_q, other_q]))
    enc_act = flags_of(q_row, q_row, core, quarter, extra, False)
    self_act = flags_of(a_row, a_row, core, quarter, 0, True)
    cross_act = flags_of(a_row, q_row, core, quarter, 0, False)

    enc_in = jnp.concatenate([x_question, jnp.pad(entry_vals, ((0, extra - n_prefix), (0, 0)))], 0)
    normed_q = rms_norm(enc_in, norm_gains[0]).astype(jnp.bfloat16)
    query_enc = project(normed_q[:tokens], enc_w[:D]).astype(jnp.bfloat16)
    enc_kv = project(normed_q, enc_w[D : 3 * D]).astype(jnp.bfloat16)
    enc_kv_other = partner(enc_kv)

    normed_a = rms_norm(x_answer, norm_gains[2]).astype(jnp.bfloat16)
    qkv_self = project(normed_a, dec_w[: 3 * D]).astype(jnp.bfloat16)
    query_self, self_kv = qkv_self[:, :D], qkv_self[:, D:]
    self_kv_other = partner(self_kv)

    mixed_enc, logsum_enc = attend(False, enc_act, query_enc, q_aug, enc_kv, enc_kv_other, enc_aug)
    hidden_one = x_question + project_back(mixed_enc, enc_w[3 * D : 4 * D])
    normed_f1 = rms_norm(hidden_one, norm_gains[1]).astype(jnp.bfloat16)
    pre_enc = project(normed_f1, enc_w[4 * D : 4 * D + FF])
    act_enc = jax.nn.gelu(pre_enc).astype(jnp.bfloat16)
    hidden_two = hidden_one + project_back(act_enc, enc_w[4 * D + FF :])
    encoded = rms_norm(hidden_two, norm_gains[5]).astype(jnp.bfloat16)
    cross_kv = project(encoded, dec_w[5 * D : 7 * D]).astype(jnp.bfloat16)
    cross_kv_other = partner(cross_kv)

    mixed_self, logsum_self = attend(True, self_act, query_self, a_aug, self_kv, self_kv_other, self_aug)
    dec_one = x_answer + project_back(mixed_self, dec_w[3 * D : 4 * D])
    normed_c = rms_norm(dec_one, norm_gains[3]).astype(jnp.bfloat16)
    query_cross = project(normed_c, dec_w[4 * D : 5 * D]).astype(jnp.bfloat16)
    mixed_cross, logsum_cross = attend(
        False, cross_act, query_cross, a_aug, cross_kv, cross_kv_other, cross_aug
    )
    dec_two = dec_one + project_back(mixed_cross, dec_w[7 * D : 8 * D])
    normed_f2 = rms_norm(dec_two, norm_gains[4]).astype(jnp.bfloat16)
    pre_dec = project(normed_f2, dec_w[8 * D : 8 * D + FF])
    act_dec = jax.nn.gelu(pre_dec).astype(jnp.bfloat16)
    dec_three = dec_two + project_back(act_dec, dec_w[8 * D + FF :])
    decoded = from_rows(dec_three.astype(jnp.bfloat16))

    grad_w1d, grad_w2d, grad_nf2 = feed_back(
        grad_top, normed_f2, pre_dec, act_dec, dec_w[8 * D : 8 * D + FF], dec_w[8 * D + FF :]
    )
    grad_x, grad_gain4 = norm_back(dec_two, norm_gains[4], grad_nf2)
    grad_two = grad_top + grad_x
    grad_woc, grad_mixc = output_back(grad_two, mixed_cross, dec_w[7 * D : 8 * D])
    grad_qc, dk_own, dv_own, dk_other, dv_other = attend_back(
        False, cross_act, query_cross, a_aug, cross_kv, cross_kv_other, cross_aug,
        mixed_cross, logsum_cross, grad_mixc,
    )
    more = partner(jnp.concatenate([dk_other, dv_other], 1)).astype(jnp.float32)
    grad_ckv = (jnp.concatenate([dk_own, dv_own], 1) + more).astype(jnp.bfloat16)
    grad_wqc = outer_sum(grad_qc, normed_c)
    grad_x, grad_gain3 = norm_back(
        dec_one, norm_gains[3], project_back(grad_qc, dec_w[4 * D : 5 * D])
    )
    grad_one = grad_two + grad_x
    grad_wckv = outer_sum(grad_ckv, encoded)
    grad_encoded, grad_gain5 = norm_back(
        hidden_two, norm_gains[5], project_back(grad_ckv, dec_w[5 * D : 7 * D])
    )
    grad_wos, grad_mixs = output_back(grad_one, mixed_self, dec_w[3 * D : 4 * D])
    grad_qs, dk_own, dv_own, dk_other, dv_other = attend_back(
        True, self_act, query_self, a_aug, self_kv, self_kv_other, self_aug,
        mixed_self, logsum_self, grad_mixs,
    )
    more = partner(jnp.concatenate([dk_other, dv_other], 1)).astype(jnp.float32)
    grad_skv = (jnp.concatenate([dk_own, dv_own], 1) + more).astype(jnp.bfloat16)
    grad_self = jnp.concatenate([grad_qs, grad_skv], 1)
    grad_wself = outer_sum(grad_self, normed_a)
    grad_x, grad_gain2 = norm_back(x_answer, norm_gains[2], project_back(grad_self, dec_w[: 3 * D]))
    grad_answers = from_rows((grad_one + grad_x).astype(jnp.bfloat16)).astype(jnp.float32)
    dec_full = jnp.concatenate(
        [grad_wself, grad_wos, grad_wqc, grad_wckv, grad_woc, grad_w1d, grad_w2d], 0
    )
    grad_decoder = reduce_weights(dec_full).astype(jnp.float32).T

    grad_w1e, grad_w2e, grad_nf1 = feed_back(
        grad_encoded, normed_f1, pre_enc, act_enc, enc_w[4 * D : 4 * D + FF], enc_w[4 * D + FF :]
    )
    grad_x, grad_gain1 = norm_back(hidden_one, norm_gains[1], grad_nf1)
    grad_hidden = grad_encoded + grad_x
    grad_woe, grad_mixe = output_back(grad_hidden, mixed_enc, enc_w[3 * D : 4 * D])
    grad_qe, dk_own, dv_own, dk_other, dv_other = attend_back(
        False, enc_act, query_enc, q_aug, enc_kv, enc_kv_other, enc_aug,
        mixed_enc, logsum_enc, grad_mixe,
    )
    more = partner(jnp.concatenate([dk_other, dv_other], 1)).astype(jnp.float32)
    grad_ekv = (jnp.concatenate([dk_own, dv_own], 1) + more).astype(jnp.bfloat16)
    grad_wqe = outer_sum(grad_qe, normed_q[:tokens])
    grad_wkve = outer_sum(grad_ekv, normed_q)
    grad_in = project_back(grad_ekv, enc_w[D : 3 * D])
    grad_in = grad_in + jnp.pad(project_back(grad_qe, enc_w[:D]), ((0, extra), (0, 0)))
    grad_x, grad_gain0 = norm_back(enc_in, norm_gains[0], grad_in)
    grad_questions = from_rows((grad_hidden + grad_x[:tokens]).astype(jnp.bfloat16)).astype(jnp.float32)
    enc_full = jnp.concatenate([grad_wqe, grad_wkve, grad_woe, grad_w1e, grad_w2e], 0)
    gain_terms = jnp.stack(
        [grad_gain0, grad_gain1, grad_gain2, grad_gain3, grad_gain4, grad_gain5]
    )
    grad_gains = lax.psum(gain_terms, ("rows", "mem"))
    grad_encoder = reduce_weights(enc_full).astype(jnp.float32).T
    return (decoded, grad_questions, grad_answers, grad_encoder, grad_decoder, grad_gains)


def solution(mesh):
    return jax.shard_map(
        on_device,
        mesh=mesh,
        in_specs=(
            P("rows", "mem", None),
            P("rows", "mem", None),
            P("rows", None),
            P("rows", None),
            P("rows", None, "mem"),
            P("rows", None, None),
            P(),
            P(None, ("rows", "mem")),
            P(None, ("rows", "mem")),
            P(),
            P("rows", "mem", None),
        ),
        out_specs=(
            P("rows", "mem", None),
            P("rows", "mem", None),
            P("rows", "mem", None),
            P(None, ("rows", "mem")),
            P(None, ("rows", "mem")),
            P(),
        ),
        check_vma=False,
    )
```

time: 1790 us -> 1170 us (0.65)
  waiting for transfers between devices: 1030 us -> 692 us
  matrix products: 397 us -> 158 us
  Pallas kernels: 0 us -> 173 us
  local copies, waits for them, and re-layouts: 152 us -> 32 us
  other arithmetic: 148 us -> 30.6 us
    unnamed x13 -> x10, waiting for transfers between devices: 272 us -> 2.53 us
    dot_general x54 -> x36, matrix products: 397 us -> 158 us  [the longest x12 56.4 us: project_back(): jnp.einsum('ne,ed->nd', left, weight_t, preferred_element_type=jnp.float32)]
    pallas_call x0 -> x6, Pallas kernels: none -> 173 us  [the longest x3 94.1 us: attend_back(): pl.pallas_call(functools.partial(back_kernel, causal, t, nk - t), grid_sp...]
    all_gather x6 -> x8, waiting for transfers between devices: 446 us -> 357 us  [the longest x3 164 us: to_rows(): row = my_row(lax.all_gather(values, 'mem', axis=1, tiled=True))]
    convert_element_type x5 -> x14, other arithmetic: 59.3 us -> 13.2 us  [the longest x1 2.79 us: on_device(): from_rows((grad_hidden + grad_x[:tokens]).astype(jnp.bfloat16))]
    unnamed x246 -> x255, local copies, waits for them, and re-layouts: 58 us -> 13.7 us
    slice x20 -> x8, local copies, waits for them, and re-layouts: 44 us -> 0.42 us  [the longest x2 0.16 us: on_device(): query_self, self_kv = (qkv_self[:, :D], qkv_self[:, D:])]
    concatenate x8 -> x6, other arithmetic: 42.5 us -> 0.4 us  [the longest x3 0.37 us: on_device(): more = partner(jnp.concatenate([dk_other, dv_other], 1)).astype(jnp.float32)]
  transfers between devices with their start and end apart: 12 -> 23, of which waited for: 10 -> 10; matrix products, arithmetic and copies ran while one was open for 29% -> 16% of each run, Pallas kernels for 0% -> 13%
where the time goes in v1:
time: 1170 us; the launch traced here: 1160 us
  waiting for transfers between devices  692 us (59%)
  Pallas kernels  173 us (15%)
  matrix products  158 us (14%)
  blocking collectives  54.2 us (5%)
  local copies, waits for them, and re-layouts  32 us (3%)
  other arithmetic  30.6 us (3%)
  between operations  16.6 us (1%)
    reduce_scatter x2, waiting for transfers between devices, reduce_weights(): lax.psum_scatter(grads, ('rows', 'mem'), scatter_dimension=0, tiled=True)  330 us
    all_gather x3, waiting for transfers between devices, to_rows(): row = my_row(lax.all_gather(values, 'mem', axis=1, tiled=True))  164 us
    all_gather x2, waiting for transfers between devices, gather_weights(): return lax.all_gather(params.T, ('rows', 'mem'), axis=0, tiled=True)  162 us
    pallas_call x3, Pallas kernels, attend_back(): pl.pallas_call(functools.partial(back_kernel, causal, t, nk - t), grid_sp...  94.1 us
    pallas_call x3, Pallas kernels, attend(): pl.pallas_call(functools.partial(attend_kernel, causal, t, nk - t), grid_...  79.4 us
    dot_general x12, matrix products, project_back(): jnp.einsum('ne,ed->nd', left, weight_t, preferred_element_type=jnp.float32)  56.4 us
    dot_general x12, matrix products, project(): jnp.einsum('nd,ed->ne', left, weight_t, preferred_element_type=jnp.float32)  54.9 us
    dot_general x12, matrix products, outer_sum(): jnp.einsum('ne,nd->ed', wide, narrow, preferred_element_type=jnp.float32)  46.9 us
  transfers between devices with their start and end apart: 23, of which 10 were waited for; matrix products, arithmetic and copies ran while one was open for 16% of the time, Pallas kernels for 13%

profile of v1, /device:TPU:0, one launch (start us, length us, event | category | flops | bytes accessed | tf_op | source)
XLA Modules:
  0.0 1160.6 jit_solution(7389589851178942067)
XLA Ops:
  12.4 14.9 %all_gather.37 = s32[2,8,12]{1,0,2:T(2,128)S(1)} all-gather(s32[2,8,3]{1,0,2:T(2,128)S(1)} %copy-done.107), channel_id=1, replica_groups=mesh['rows'=8,'mem'=4] {'mem'}, dimensions={2}, use_global_device_ids=true | all-gather | bytes 960 | tf_op jit(solution)/shard_map/all_gather | solution.py:344
  27.8 48.6 %all-gather.20.cloned.1.call-done = bf16[2,1024,768]{2,1,0:T(8,128)(2,1)} async-done(((bf16[2,256,768]{2,1,0:T(8,128)(2,1)}), bf16[2,1024,768]{2,1,0:T(8,128)(2,1)}) %all-gather.20.cloned.1.call-update) | async-done | bytes 3145744 | tf_op jit(solution)/shard_map/all_gather | solution.py:282
  76.4 63.8 %all-gather.16.cloned.1.call-done = bf16[2,1024,768]{2,1,0:T(8,128)(2,1)} async-done(((bf16[2,256,768]{2,1,0:T(8,128)(2,1)}), bf16[2,1024,768]{2,1,0:T(8,128)(2,1)}) %all-gather.16.cloned.1.call-update) | async-done | bytes 3145744 | tf_op jit(solution)/shard_map/all_gather | solution.py:282
  145.6 6.3 gather_fusion.9
  152.7 51.2 %all-gather.12.cloned.1.call-done = bf16[2,1024,768]{2,1,0:T(8,128)(2,1)} async-done(((bf16[2,256,768]{2,1,0:T(8,128)(2,1)}), bf16[2,1024,768]{2,1,0:T(8,128)(2,1)}) %all-gather.12.cloned.1.call-update) | async-done | bytes 3145744 | tf_op jit(solution)/shard_map/all_gather | solution.py:282
  204.0 5.3 broadcast_select_fusion
  212.7 95.7 %all-gather.18.cloned.1.call-done = bf16[9216,768]{1,0:T(8,128)(2,1)} async-done(((bf16[288,768]{1,0:T(8,128)(2,1)}), bf16[9216,768]{1,0:T(8,128)(2,1)}) %all-gather.18.cloned.1.call-update) | async-done | bytes 14155792 | tf_op jit(solution)/shard_map/all_gather | solution.py:300
  322.4 40.0 %attend.4 = (bf16[512,768]{1,0:T(8,128)(2,1)S(1)}, f32[512,768]{1,0:T(8,128)S(1)}) custom-call(s32[2,6]{1,0:T(2,128)S(1)} %add_convert_fusion.3.act, bf16[512,768]{1,0:T(8,128)(2,1)S(1)} %convolution_convert_fusion.18.q_ref, bf16[512,128]{1,0:T(8,128)(2,1)S(1)} %get-tuple-element.111.qaug_ref, bf16[640,1536]{1,0:T(8,128)(2,1)S(1)} %convolution_convert_fusion.8.own_k.own_v, ...), custom_call_target="tpu_custom_call" | custom-call | flops 2013265920 | bytes 3932160 | tf_op jit(solution)/shard_map/attend/pallas_call | solution.py:83
  366.3 7.3 fusion.33
  373.7 66.2 %all-gather.14.cloned.1.call-done = bf16[12288,768]{0,1:T(8,128)(2,1)} async-done(((bf16[384,768]{0,1:T(8,128)(2,1)}), bf16[12288,768]{0,1:T(8,128)(2,1)}) %all-gather.14.cloned.1.call-update) | async-done | bytes 18874384 | tf_op jit(solution)/shard_map/all_gather | solution.py:300
  445.5 6.2 multiply_reduce_fusion.12
  459.3 19.6 %attend.3 = (bf16[512,768]{1,0:T(8,128)(2,1)S(1)}, f32[512,768]{1,0:T(8,128)S(1)}) custom-call(s32[2,4]{1,0:T(2,128)S(1)} %add_convert_fusion.1.act, bf16[512,768]{1,0:T(8,128)(2,1)S(1)} %slice.175.q_ref, bf16[512,128]{1,0:T(8,128)(2,1)S(1)} %get-tuple-element.112.qaug_ref, bf16[512,1536]{1,0:T(8,128)(2,1)S(1)} %slice.176.own_k.own_v, ...), custom_call_target="tpu_custom_call" | custom-call | flops 1610612736 | bytes 3145728 | tf_op jit(solution)/shard_map/attend/pallas_call | solution.py:83
  484.7 19.9 %attend.5 = (bf16[512,768]{1,0:T(8,128)(2,1)S(1)}, f32[512,768]{1,0:T(8,128)S(1)}) custom-call(s32[2,4]{1,0:T(2,128)S(1)} %add_convert_fusion.2.act, bf16[512,768]{1,0:T(8,128)(2,1)S(1)} %convolution_convert_fusion.19.q_ref, bf16[512,128]{1,0:T(8,128)(2,1)S(1)} %copy-done.12, bf16[512,1536]{1,0:T(8,128)(2,1)S(1)} %convolution_convert_fusion.9.own_k.own_v, ...), custom_call_target="tpu_custom_call" | custom-call | flops 1610612736 | bytes 3145728 | tf_op jit(solution)/shard_map/attend/pallas_call | solution.py:83
  507.4 5.2 fusion.25
  515.2 7.1 add_convert_fusion
  522.3 8.8 fusion.13
  531.2 6.3 multiply_reduce_fusion.4
  541.4 23.8 %attend_back.3 = (bf16[512,768]{1,0:T(8,128)(2,1)S(1)}, f32[512,768]{1,0:T(8,128)S(1)}, f32[512,768]{1,0:T(8,128)S(1)}, bf16[512,768]{1,0:T(8,128)(2,1)S(1)}, bf16[512,768]{1,0:T(8,128)(2,1)S(1)}) custom-call(s32[2,4]{1,0:T(2,128)S(1)} %add_convert_fusion.2.act, bf16[512,768]{1,0:T(8,128)(2,1)S(1)} %copy-done.23, bf16[512,128]{1,0:T(8,128)(2,1)S(1)} %copy-done.13, ...), custom_call_target="tpu_custom_call" | custom-call | flops 4026531840 | bytes 9437184 | tf_op jit(solution)/shard_map/attend_back/pallas_call | solution.py:181
  571.9 23.7 %attend_back.5 = (bf16[512,768]{1,0:T(8,128)(2,1)S(1)}, f32[512,768]{1,0:T(8,128)S(1)}, f32[512,768]{1,0:T(8,128)S(1)}, bf16[512,768]{1,0:T(8,128)(2,1)S(1)}, bf16[512,768]{1,0:T(8,128)(2,1)S(1)}) custom-call(s32[2,4]{1,0:T(2,128)S(1)} %add_convert_fusion.1.act, bf16[512,768]{1,0:T(8,128)(2,1)S(1)} %copy-done.4, bf16[512,128]{1,0:T(8,128)(2,1)S(1)} %copy-done.13, ...), custom_call_target="tpu_custom_call" | custom-call | flops 4026531840 | bytes 9437184 | tf_op jit(solution)/shard_map/attend_back/pallas_call | solution.py:181
  600.3 4.9 fusion.56
  605.3 5.5 multiply_reduce_fusion.3
  614.1 9.3 fusion.6
  623.4 6.3 multiply_reduce_fusion.6
  633.0 46.6 %attend_back.4 = (bf16[512,768]{1,0:T(8,128)(2,1)S(1)}, f32[640,768]{1,0:T(8,128)S(1)}, f32[640,768]{1,0:T(8,128)S(1)}, bf16[640,768]{1,0:T(8,128)(2,1)S(1)}, bf16[640,768]{1,0:T(8,128)(2,1)S(1)}) custom-call(s32[2,6]{1,0:T(2,128)S(1)} %add_convert_fusion.3.act, bf16[512,768]{1,0:T(8,128)(2,1)S(1)} %copy-done.27, bf16[512,128]{1,0:T(8,128)(2,1)S(1)} %copy-done.10, ...), custom_call_target="tpu_custom_call" | custom-call | flops 5033164800 | bytes 11796480 | tf_op jit(solution)/shard_map/attend_back/pallas_call | solution.py:181
  683.8 5.1 multiply_reduce_fusion
  693.7 5.4 fusion.37
  705.6 8.3 fusion.16
  715.4 5.6 fusion.18
  740.3 31.2 %all-gather.24.cloned.1.call-done = bf16[2048,768]{1,0:T(8,128)(2,1)} async-done(((bf16[512,768]{1,0:T(8,128)(2,1)}), bf16[2048,768]{1,0:T(8,128)(2,1)}) %all-gather.24.cloned.1.call-update) | async-done | bytes 3145744 | tf_op jit(solution)/shard_map/all_gather | solution.py:290
  771.6 39.4 %psum.7 = f32[6,768]{1,0:T(8,128)} all-reduce(f32[6,768]{1,0:T(8,128)S(1)} %stack.20), channel_id=1, replica_groups=mesh['rows'=8,'mem'=4] {'rows','mem'}, use_global_device_ids=true, to_apply=%region_20.21 | all-reduce | flops 4608 | bytes 36864 | tf_op jit(solution)/shard_map/psum | solution.py:487
  818.8 120.2 %reduce-scatter.3.cloned.1.call-done = bf16[288,768]{1,0:T(8,128)(2,1)} async-done(((bf16[9216,768]{1,0:T(8,128)(2,1)}), bf16[288,768]{1,0:T(8,128)(2,1)}) %reduce-scatter.3.cloned.1.call-update) | async-done | bytes 442384 | tf_op jit(solution)/shard_map/reduce_scatter | solution.py:304
  941.0 209.8 %reduce-scatter.5.cloned.1.call-done = bf16[384,768]{1,0:T(8,128)(2,1)} async-done(((bf16[12288,768]{1,0:T(8,128)(2,1)}), bf16[384,768]{1,0:T(8,128)(2,1)}) %reduce-scatter.5.cloned.1.call-update) | async-done | bytes 589840 | tf_op jit(solution)/shard_map/reduce_scatter | solution.py:304
  (432 shorter events, 127.0 us)
Async XLA Ops:
  7.2 69.2 %all-gather.20.cloned.1.call-start = ((), (), s32[]{:S(2)}) async-start(), calls=%async_computation.6 | async-start | bytes 3932160 | tf_op jit(solution)/shard_map/all_gather | solution.py:282
  9.6 130.5 %all-gather.16.cloned.1.call-start = ((), (), s32[]{:S(2)}) async-start(), calls=%async_computation.4 | async-start | bytes 3932160 | tf_op jit(solution)/shard_map/all_gather | solution.py:282
  10.4 193.5 %all-gather.12.cloned.1.call-start = ((), (), s32[]{:S(2)}) async-start(), calls=%async_computation.2 | async-start | bytes 3932160 | tf_op jit(solution)/shard_map/all_gather | solution.py:282
  11.1 297.4 %all-gather.18.cloned.1.call-start = ((), (), s32[]{:S(2)}) async-start(), calls=%async_computation.5 | async-start | bytes 14598144 | tf_op jit(solution)/shard_map/all_gather | solution.py:300
  11.7 428.1 %all-gather.14.cloned.1.call-start = ((), (), s32[]{:S(2)}) async-start(), calls=%async_computation.3 | async-start | bytes 19464192 | tf_op jit(solution)/shard_map/all_gather | solution.py:300
  12.3 727.4 %all-gather.22.cloned.1.call-start = ((), (), s32[]{:S(2)}) async-start(), calls=%async_computation.9 | async-start | bytes 3932160 | tf_op jit(solution)/shard_map/all_gather | solution.py:290
  27.5 112.7 %collective-permute-start.1 = (s32[2,2240]{1,0:T(2,128)S(1)}, s32[2,2240]{1,0:T(2,128)S(1)}, u32[]{:S(2)}, u32[]{:S(2)}) collective-permute-start(s32[2,2240]{1,0:T(2,128)S(1)} %concatenate.109), channel_id=1, source_target_pairs={{0,4},{4,0},{8,12},{12,8},{16,20},{20,16},{24,28},{28,24},{1,5},{5... | collective-permute-start | bytes 53768 | tf_op jit(solution)/shard_map/ppermute | solution.py:260
  76.3 127.7 %collective-permute-start.7 = (bf16[2,1024,768]{2,1,0:T(8,128)(2,1)}, bf16[2,1024,768]{2,1,0:T(8,128)(2,1)}, u32[]{:S(2)}, u32[]{:S(2)}) collective-permute-start(bf16[2,1024,768]{2,1,0:T(8,128)(2,1)} %all-gather.20.cloned.1.call-done), channel_id=1, source_target_pairs={{0,4},{4,0},{8,12},{12,8},{16,20},{20,16},{24,28},{28,24},{1,5},{5... | collective-permute-start | bytes 9437192 | tf_op jit(solution)/shard_map/ppermute | solution.py:260
  140.1 63.9 %collective-permute-start.3 = (bf16[2,1024,768]{2,1,0:T(8,128)(2,1)}, bf16[2,1024,768]{2,1,0:T(8,128)(2,1)}, u32[]{:S(2)}, u32[]{:S(2)}) collective-permute-start(bf16[2,1024,768]{2,1,0:T(8,128)(2,1)} %all-gather.16.cloned.1.call-done), channel_id=1, source_target_pairs={{0,4},{4,0},{8,12},{12,8},{16,20},{20,16},{24,28},{28,24},{1,5},{5... | collective-permute-start | bytes 9437192 | tf_op jit(solution)/shard_map/ppermute | solution.py:260
  140.1 175.8 %copy-start.100 = (pred[128]{0:T(512)(128)(4,1)}, pred[128]{0:T(512)(128)(4,1)S(1)}, u32[]{:S(2)}) copy-start(pred[128]{0:T(512)(128)(4,1)S(1)} %broadcast_compare_fusion) | copy-start | bytes 388
  140.1 175.8 %copy-start.108 = (bf16[128]{0:T(256)(128)(2,1)}, bf16[128]{0:T(256)(128)(2,1)S(1)}, u32[]{:S(2)}) copy-start(bf16[128]{0:T(256)(128)(2,1)S(1)} %and_select_fusion.1) | copy-start | bytes 772
  203.9 112.3 %collective-permute-start = (bf16[2,1024,768]{2,1,0:T(8,128)(2,1)}, bf16[2,1024,768]{2,1,0:T(8,128)(2,1)}, u32[]{:S(2)}, u32[]{:S(2)}) collective-permute-start(bf16[2,1024,768]{2,1,0:T(8,128)(2,1)} %all-gather.12.cloned.1.call-done), channel_id=1, source_target_pairs={{0,4},{4,0},{8,12},{12,8},{16,20},{20,16},{24,28},{28,24},{1,5},{5... | collective-permute-start | bytes 9437192 | tf_op jit(solution)/shard_map/ppermute | solution.py:260
  312.2 10.2 collective-permute-start.4
  315.9 143.4 %copy-start.11 = (bf16[512,128]{1,0:T(8,128)(2,1)}, bf16[512,128]{1,0:T(8,128)(2,1)S(1)}, u32[]{:S(2)}) copy-start(bf16[512,128]{1,0:T(8,128)(2,1)S(1)} %get-tuple-element.112.qaug_ref) | copy-start | bytes 393220
  322.3 40.0 %copy-start.26 = (bf16[512,768]{1,0:T(8,128)(2,1)}, bf16[512,768]{1,0:T(8,128)(2,1)S(1)}, u32[]{:S(2)}) copy-start(bf16[512,768]{1,0:T(8,128)(2,1)S(1)} %convolution_convert_fusion.18.q_ref) | copy-start | bytes 2359300
  366.3 73.5 %copy-start.63 = (bf16[256,768]{1,0:T(8,128)(2,1)S(1)}, bf16[256,768]{1,0:T(8,128)(2,1)}, u32[]{:S(2)}) copy-start(bf16[256,768]{1,0:T(8,128)(2,1)} %copy-done.62) | copy-start | bytes 1179652
  366.3 73.5 %copy-start.67 = (bf16[256,768]{1,0:T(8,128)(2,1)S(1)}, bf16[256,768]{1,0:T(8,128)(2,1)}, u32[]{:S(2)}) copy-start(bf16[256,768]{1,0:T(8,128)(2,1)} %copy-done.66) | copy-start | bytes 1179652
  444.2 15.0 %collective-permute-start.2 = (bf16[512,1536]{1,0:T(8,128)(2,1)S(1)}, bf16[512,1536]{1,0:T(8,128)(2,1)S(1)}, u32[]{:S(2)}, u32[]{:S(2)}) collective-permute-start(bf16[512,1536]{1,0:T(8,128)(2,1)S(1)} %slice.176.own_k.own_v), channel_id=1, source_target_pairs={{0,4},{4,0},{8,12},{12,8},{16,20},{20,16},{24,28},{28,24},{1,5},{5... | collective-permute-start | bytes 4718600 | tf_op jit(solution)/shard_map/ppermute | solution.py:260
  456.0 28.7 %collective-permute-start.5 = (bf16[512,1536]{1,0:T(8,128)(2,1)S(1)}, bf16[512,1536]{1,0:T(8,128)(2,1)S(1)}, u32[]{:S(2)}, u32[]{:S(2)}) collective-permute-start(bf16[512,1536]{1,0:T(8,128)(2,1)S(1)} %convolution_convert_fusion.9.own_k.own_v), channel_id=1, source_target_pairs={{0,4},{4,0},{8,12},{12,8},{16,20},{20,16},{24,28},{28,24},{1,5},{5... | collective-permute-start | bytes 4718600 | tf_op jit(solution)/shard_map/ppermute | solution.py:260
  522.3 217.6 %all-gather.26.cloned.1.call-start = ((), (), s32[]{:S(2)}) async-start(), calls=%async_computation.11 | async-start | bytes 3932160 | tf_op jit(solution)/shard_map/all_gather | solution.py:290
  565.3 40.0 %copy-start.28 = (f32[512,768]{1,0:T(8,128)}, f32[512,768]{1,0:T(8,128)S(1)}, u32[]{:S(2)}) copy-start(f32[512,768]{1,0:T(8,128)S(1)} %get-tuple-element.31) | copy-start | bytes 4718596
  568.9 42.0 %copy-start.48 = (f32[512,768]{1,0:T(8,128)}, f32[512,768]{1,0:T(8,128)S(1)}, u32[]{:S(2)}) copy-start(f32[512,768]{1,0:T(8,128)S(1)} %fusion.63) | copy-start | bytes 4718596
  595.7 3.5 collective-permute-start.11
  595.9 9.3 collective-permute-start.8
  612.2 159.2 %all-gather.24.cloned.1.call-start = ((), (), s32[]{:S(2)}) async-start(), calls=%async_computation.10 | async-start | bytes 3932160 | tf_op jit(solution)/shard_map/all_gather | solution.py:290
  630.2 58.8 %copy-start.50 = (f32[512,768]{1,0:T(8,128)}, f32[512,768]{1,0:T(8,128)S(1)}, u32[]{:S(2)}) copy-start(f32[512,768]{1,0:T(8,128)S(1)} %fusion.60) | copy-start | bytes 4718596
  679.8 4.0 collective-permute-start.9
  690.3 248.7 %reduce-scatter.3.cloned.1.call-start = ((), (), s32[]{:S(2)}) async-start(), calls=%async_computation.7 | async-start | bytes 14598144 | tf_op jit(solution)/shard_map/reduce_scatter | solution.py:304
  714.0 436.9 %reduce-scatter.5.cloned.1.call-start = ((), (), s32[]{:S(2)}) async-start(), calls=%async_computation.8 | async-start | bytes 19464192 | tf_op jit(solution)/shard_map/reduce_scatter | solution.py:304
  739.7 71.3 %collective-permute-start.6 = (bf16[4,512,768]{2,1,0:T(8,128)(2,1)}, bf16[4,512,768]{2,1,0:T(8,128)(2,1)S(1)}, u32[]{:S(2)}, u32[]{:S(2)}) collective-permute-start(bf16[4,512,768]{2,1,0:T(8,128)(2,1)} %bitcast.75), channel_id=1, source_target_pairs={{0,4},{4,0},{8,12},{12,8},{16,20},{20,16},{24,28},{28,24},{1,5},{5... | collective-permute-start | bytes 9437192 | tf_op jit(solution)/shard_map/ppermute | solution.py:260
  739.9 73.4 %collective-permute-start.12 = (bf16[4,512,768]{2,1,0:T(8,128)(2,1)}, bf16[4,512,768]{2,1,0:T(8,128)(2,1)}, u32[]{:S(2)}, u32[]{:S(2)}) collective-permute-start(bf16[4,512,768]{2,1,0:T(8,128)(2,1)} %bitcast.77), channel_id=1, source_target_pairs={{0,4},{4,0},{8,12},{12,8},{16,20},{20,16},{24,28},{28,24},{1,5},{5... | collective-permute-start | bytes 9437192 | tf_op jit(solution)/shard_map/ppermute | solution.py:260
  771.5 44.6 %collective-permute-start.10 = (bf16[4,512,768]{2,1,0:T(8,128)(2,1)}, bf16[4,512,768]{2,1,0:T(8,128)(2,1)}, u32[]{:S(2)}, u32[]{:S(2)}) collective-permute-start(bf16[4,512,768]{2,1,0:T(8,128)(2,1)} %bitcast.79), channel_id=1, source_target_pairs={{0,4},{4,0},{8,12},{12,8},{16,20},{20,16},{24,28},{28,24},{1,5},{5... | collective-permute-start | bytes 9437192 | tf_op jit(solution)/shard_map/ppermute | solution.py:260
  (114 other events, 908.8 us)
Sparse Core Ops, SparseCore 0:
  10.1 66.1 all-gather.19
  77.9 62.1 all-gather.15
  141.7 62.1 all-gather.11
  206.5 101.8 all-gather.17
  311.2 128.5 all-gather.13
  522.4 70.9 all-gather.21
  612.4 81.0 all-gather.25
  695.6 75.8 all-gather.23
  777.5 161.4 reduce-scatter.2
  945.3 205.5 reduce-scatter.4

commit v2 on v1

--- a/solution.py
+++ b/solution.py
@@ -217,6 +217,385 @@
     return jnp.where(bad, masked_score, jnp.where((j >= 8) & (j <= 10), 1.0, 0.0)).astype(jnp.bfloat16)
 
 
+MESH = pl.DeviceIdType.MESH
+
+
+def position():
+    r, m = lax.axis_index("rows"), lax.axis_index("mem")
+    core = lax.rem(r, 2)
+    x_at = lax.rem(lax.div(r, 2), 2)
+    y_at = lax.div(r, 4)
+    near = r + 1 - 2 * core
+    x_near = r + 2 - 4 * x_at
+    y_near = r + 4 - 8 * y_at
+    first = x_near + core * (y_near - x_near)
+    second = y_near + core * (x_near - y_near)
+    both = first + second - r
+    return r, m, core, near, first, second, both
+
+
+def greet(r, m, core, first, second):
+    barrier = pltpu.get_barrier_semaphore()
+    base = r - core
+    count = 0
+    for c in (0, 1):
+        for step in range(4):
+            if c == 0 and step == 0:
+                continue
+            to = r if c == 0 else base + 1 - core
+            pl.semaphore_signal(barrier, inc=1, device_id=(to, lax.rem(m + step, 4)), device_id_type=MESH)
+            count += 1
+    for to in (first, second):
+        pl.semaphore_signal(barrier, inc=1, device_id=(to, m), device_id_type=MESH)
+        count += 1
+    pl.semaphore_wait(barrier, count)
+
+
+def remote(src, dst, send, recv, to):
+    return pltpu.make_async_remote_copy(
+        src_ref=src, dst_ref=dst, send_sem=send, recv_sem=recv, device_id=to, device_id_type=MESH
+    )
+
+
+def gather_kernel(
+    enc_in, dec_in, q_in, a_in, g_in, seg_in, ids_in,
+    enc_out, dec_out, q_out, a_out, g_out, seg_out, ids_out,
+    z_s, z_r, a_s, a_r, b_s, b_r, c_s, c_r, t_s, t_r, t_l, i_s, i_r, i_l, w_l, n_s, n_r,
+):
+    r, m, core, near, first, second, both = position()
+    base = r - core
+    ins, outs = (enc_in, dec_in), (enc_out, dec_out)
+    greet(r, m, core, first, second)
+
+    def at(which, row, mem):
+        size = ins[which].shape[0]
+        return outs[which].at[pl.ds(pl.multiple_of((row * 4 + mem) * size, 32), size)]
+
+    waits = []
+    locals_ = []
+    for w in (0, 1):
+        copy = pltpu.make_async_copy(ins[w], at(w, r, m), w_l.at[w])
+        copy.start()
+        locals_.append(copy)
+
+    def send(src, dst, s, v, to):
+        copy = remote(src, dst, s, v, to)
+        copy.start()
+        waits.append(copy)
+
+    send(seg_in.at[lax.rem(m, 2)], seg_out, n_s, n_r, (near, m))
+    holder = lax.div(m * (3 - m), 2)
+    slot = lax.div(m, 2)
+    cond_sends = []
+    for i in (0, 1):
+        for e in (0, 1):
+            to = (r if e == 0 else near, 2 * core + i)
+            copy = remote(ids_in.at[i], ids_out.at[m], i_s.at[i, e], i_r.at[m], to)
+            if e == 1:
+                copy.start()
+                waits.append(copy)
+                continue
+            here = 2 * core + i == m
+            mine = pltpu.make_async_copy(ids_in.at[i], ids_out.at[m], i_l)
+            pl.when(here)(mine.start)
+            pl.when(jnp.logical_not(here))(copy.start)
+            cond_sends.append((here, copy))
+
+    def tokens(n, src, dst):
+        for i in (0, 1):
+            here = jnp.logical_and(2 * core + i == m, holder == core)
+            place = dst.at[pl.ds(pl.multiple_of(slot * 256, 256), 256)]
+            copy = remote(src.at[i], place, t_s.at[n, i], t_r.at[n, slot], (base + holder, 2 * core + i))
+            mine = pltpu.make_async_copy(src.at[i], place, t_l.at[n])
+            pl.when(here)(mine.start)
+            pl.when(jnp.logical_not(here))(copy.start)
+            cond_sends.append((here, copy))
+
+    def forward(step, which):
+        mem = lax.rem(m - step + 4, 4)
+        for w in (0, 1):
+            here = at(w, r, mem)
+            src = ins[w] if step == 0 else here
+            if step < 3:
+                send(src, here, z_s.at[step, w], z_r.at[step, w], (r, lax.rem(m + 1, 4)))
+            send(src, here, b_s.at[step, 0, w], b_r.at[step, 0, w], (second, m))
+            send(src, here, a_s.at[step, w], a_r.at[step, w], (first, m))
+            send(src, here, c_s.at[step, 0, w], c_r.at[step, 0, w], (near, m))
+
+    def stage_a(step):
+        if step > 0:
+            mem = lax.rem(m - step + 4, 4)
+            for w in (0, 1):
+                here = at(w, r, mem)
+                remote(here, here, z_s.at[step - 1, w], z_r.at[step - 1, w], (near, m)).wait_recv()
+        forward(step, 0)
+
+    def stage_b(step):
+        mem = lax.rem(m - step + 4, 4)
+        for w in (0, 1):
+            here = at(w, first, mem)
+            remote(here, here, a_s.at[step, w], a_r.at[step, w], (near, m)).wait_recv()
+            send(here, here, b_s.at[step, 1, w], b_r.at[step, 1, w], (second, m))
+            send(here, here, c_s.at[step, 1, w], c_r.at[step, 1, w], (near, m))
+
+    def stage_c(step):
+        mem = lax.rem(m - step + 4, 4)
+        for k, row in ((0, second), (1, both)):
+            for w in (0, 1):
+                here = at(w, row, mem)
+                remote(here, here, b_s.at[step, k, w], b_r.at[step, k, w], (near, m)).wait_recv()
+                send(here, here, c_s.at[step, 2 + k, w], c_r.at[step, 2 + k, w], (near, m))
+
+    tokens(0, q_in, q_out)
+    stage_a(0)
+    tokens(1, a_in, a_out)
+    stage_a(1)
+    stage_b(0)
+    tokens(2, g_in, g_out)
+    stage_a(2)
+    stage_b(1)
+    stage_c(0)
+    stage_a(3)
+    stage_b(2)
+    stage_c(1)
+    stage_b(3)
+    stage_c(2)
+    stage_c(3)
+
+    turn = 1 - 2 * core
+    others = (r + turn, first_of(r, core), second_of(r, core), both + turn)
+    for step in range(4):
+        mem = lax.rem(m - step + 4, 4)
+        for k in range(4):
+            for w in (0, 1):
+                here = at(w, others[k], mem)
+                remote(here, here, c_s.at[step, k, w], c_r.at[step, k, w], (near, m)).wait_recv()
+    remote(seg_out, seg_out, n_s, n_r, (near, m)).wait_recv()
+    mine_row = lax.div(m, 2) == core
+    for mem in range(4):
+        here = jnp.logical_and(mine_row, m == mem)
+        got = remote(ids_out.at[mem], ids_out.at[mem], i_s.at[0, 0], i_r.at[mem], (near, m))
+        mine = pltpu.make_async_copy(ids_in.at[0], ids_out.at[mem], i_l)
+        pl.when(here)(mine.wait)
+        pl.when(jnp.logical_not(here))(got.wait_recv)
+    for n, dst in enumerate((q_out, a_out, g_out)):
+        for li in (0, 1):
+            source = core if li == 0 else 3 - core
+            here = jnp.logical_and(mine_row, m == source)
+            place = dst.at[pl.ds(li * 256, 256)]
+            got = remote(place, place, t_s.at[n, 0], t_r.at[n, li], (near, m))
+            mine = pltpu.make_async_copy(place, place, t_l.at[n])
+            pl.when(here)(mine.wait)
+            pl.when(jnp.logical_not(here))(got.wait_recv)
+    for copy in locals_:
+        copy.wait()
+    for copy in waits:
+        copy.wait_send()
+    for here, copy in cond_sends:
+        pl.when(jnp.logical_not(here))(copy.wait_send)
+
+
+def first_of(r, core):
+    turn = 1 - 2 * core
+    x_step = 2 - 4 * lax.rem(lax.div(r, 2), 2)
+    y_step = 4 - 8 * lax.div(r, 4)
+    return r + turn + y_step + core * (x_step - y_step)
+
+
+def second_of(r, core):
+    turn = 1 - 2 * core
+    x_step = 2 - 4 * lax.rem(lax.div(r, 2), 2)
+    y_step = 4 - 8 * lax.div(r, 4)
+    return r + turn + x_step + core * (y_step - x_step)
+
+
+def gather_fast(enc_t, dec_t, q, a, g, seg, ids):
+    dma = pltpu.SemaphoreType.DMA
+    tokens = 2 * q.shape[1]
+    any_ = pl.BlockSpec(memory_space=pl.ANY)
+    out = lambda shape, kind=jnp.bfloat16: jax.ShapeDtypeStruct(shape, kind)
+    return pl.pallas_call(
+        gather_kernel,
+        in_specs=[any_] * 7,
+        out_specs=[any_] * 7,
+        out_shape=[
+            out((32 * enc_t.shape[0], D)),
+            out((32 * dec_t.shape[0], D)),
+            out((tokens, D)), out((tokens, D)), out((tokens, D)),
+            out(seg.shape[1:], jnp.int32),
+            out((4,) + ids.shape[1:], jnp.int32),
+        ],
+        scratch_shapes=[
+            dma((3, 2)), dma((3, 2)), dma((4, 2)), dma((4, 2)), dma((4, 2, 2)), dma((4, 2, 2)),
+            dma((4, 4, 2)), dma((4, 4, 2)), dma((3, 2)), dma((3, 2)), dma((3,)), dma((2, 2)), dma((4,)), dma,
+            dma((2,)), dma, dma,
+        ],
+        compiler_params=pltpu.CompilerParams(collective_id=0, has_side_effects=True),
+        name="gather_fast",
+    )(enc_t, dec_t, q, a, g, seg, ids)
+
+
+def add_to(total, more):
+    def step(i, unused):
+        rows = pl.ds(pl.multiple_of(i * 32, 32), 32)
+        total[rows, :] = total[rows, :] + more[rows, :]
+        return unused
+
+    lax.fori_loop(0, total.shape[0] // 32, step, 0)
+
+
+def reduce_kernel(
+    enc_in, dec_in, y_in, q_in, a_in, gain_in,
+    enc_out, dec_out, y_out, q_out, a_out, gain_out,
+    held_e, held_d, rc_e, rc_d, rb_e, rb_d, ra_e, ra_d, rz_e, rz_d, rg, gs, gz,
+    l_l, c_s, c_r, b_s, b_r, a_s, a_r, z_s, z_r, t_s, t_r, t_l, g_s, g_r, gz_s, gz_r, o_l,
+):
+    r, m, core, near, first, second, both = position()
+    base = r - core
+    ins, outs = (enc_in, dec_in), (enc_out, dec_out)
+    held, rc, rb, ra, rz = (held_e, held_d), (rc_e, rc_d), (rb_e, rb_d), (ra_e, ra_d), (rz_e, rz_d)
+    greet(r, m, core, first, second)
+    turn = 1 - 2 * core
+    mine_rows = (r, first, second, both)
+    others = (r + turn, first_of(r, core), second_of(r, core), both + turn)
+    x_near = first + core * (second - first)
+    y_near = second + core * (first - second)
+    waits = []
+    cond_sends = []
+
+    def send(src, dst, s, v, to):
+        copy = remote(src, dst, s, v, to)
+        copy.start()
+        waits.append(copy)
+
+    def arrived(dst, s, v):
+        remote(dst, dst, s, v, (near, m)).wait_recv()
+
+    def at(w, row, mem):
+        size = outs[w].shape[0]
+        return ins[w].at[pl.ds(pl.multiple_of((row * 4 + mem) * size, 32), size)]
+
+    send(gain_in, rg.at[0], g_s.at[0], g_r.at[0], (near, m))
+
+    order = (3, 2, 1, 0)
+    loads = {}
+    for j in range(4):
+        mem = lax.rem(m - 1 - j + 8, 4)
+        for k in order:
+            for w in (0, 1):
+                send(at(w, others[k], mem), rc[w].at[j, k], c_s.at[j, k, w], c_r.at[j, k, w], (near, m))
+                loads[j, k, w] = pltpu.make_async_copy(at(w, mine_rows[k], mem), held[w].at[j, k], l_l.at[j, k, w])
+                loads[j, k, w].start()
+
+    def tokens(n, src, dst):
+        for li in (0, 1):
+            to_mem = core if li == 0 else 3 - core
+            here = jnp.logical_and(to_mem == m, lax.div(m, 2) == core)
+            place = src.at[pl.ds(li * 256, 256)]
+            target = dst.at[lax.rem(m, 2)]
+            copy = remote(place, target, t_s.at[n, li], t_r.at[n, lax.rem(m, 2)], (base + lax.div(m, 2), to_mem))
+            mine = pltpu.make_async_copy(place, target, t_l.at[n])
+            pl.when(here)(mine.start)
+            pl.when(jnp.logical_not(here))(copy.start)
+            cond_sends.append((here, copy))
+
+    def from_core(j):
+        for k in order:
+            for w in (0, 1):
+                loads[j, k, w].wait()
+                arrived(rc[w].at[j, k], c_s.at[j, k, w], c_r.at[j, k, w])
+                add_to(held[w].at[j, k], rc[w].at[j, k])
+                if k >= 2:
+                    send(held[w].at[j, k], rb[w].at[j, k - 2], b_s.at[j, k - 2, w], b_r.at[j, k - 2, w], (second, m))
+
+    def from_second(j):
+        for k in (1, 0):
+            for w in (0, 1):
+                arrived(rb[w].at[j, k], b_s.at[j, k, w], b_r.at[j, k, w])
+                add_to(held[w].at[j, k], rb[w].at[j, k])
+                if k == 1:
+                    send(held[w].at[j, 1], ra[w].at[j], a_s.at[j, w], a_r.at[j, w], (first, m))
+
+    def from_first(j):
+        for w in (0, 1):
+            arrived(ra[w].at[j], a_s.at[j, w], a_r.at[j, w])
+            add_to(held[w].at[j, 0], ra[w].at[j])
+            if j > 0:
+                arrived(rz[w].at[j - 1], z_s.at[j - 1, w], z_r.at[j - 1, w])
+                add_to(held[w].at[j, 0], rz[w].at[j - 1])
+            if j < 3:
+                send(held[w].at[j, 0], rz[w].at[j], z_s.at[j, w], z_r.at[j, w], (r, lax.rem(m + 1, 4)))
+            else:
+                pltpu.make_async_copy(held[w].at[3, 0], outs[w], o_l.at[w]).start()
+
+    tokens(0, y_in, y_out)
+    from_core(0)
+    arrived(rg.at[0], g_s.at[0], g_r.at[0])
+    gs[0] = gain_in[...] + rg[0]
+    send(gs.at[0], rg.at[1], g_s.at[1], g_r.at[1], (x_near, m))
+    from_core(1)
+    tokens(1, q_in, q_out)
+    arrived(rg.at[1], g_s.at[1], g_r.at[1])
+    gs[1] = gs[0] + rg[1]
+    send(gs.at[1], rg.at[2], g_s.at[2], g_r.at[2], (y_near, m))
+    from_second(0)
+    from_core(2)
+    from_second(1)
+    tokens(2, a_in, a_out)
+    from_first(0)
+    arrived(rg.at[2], g_s.at[2], g_r.at[2])
+    gs[2] = gs[1] + rg[2]
+    gz[m] = gs[2]
+    for hop in (1, 2, 3):
+        send(gs.at[2], gz.at[m], gz_s.at[hop - 1], gz_r.at[m], (r, lax.rem(m + hop, 4)))
+    from_core(3)
+    from_second(2)
+    from_first(1)
+    from_second(3)
+    from_first(2)
+    from_first(3)
+    for mem in range(4):
+        pl.when(m != mem)(remote(gz.at[mem], gz.at[mem], gz_s.at[0], gz_r.at[mem], (near, m)).wait_recv)
+    gain_out[...] = (gz[0] + gz[1]) + (gz[2] + gz[3])
+    holder = lax.div(m * (3 - m), 2)
+    for n, dst in enumerate((y_out, q_out, a_out)):
+        for i in (0, 1):
+            here = jnp.logical_and(2 * core + i == m, holder == core)
+            got = remote(dst.at[i], dst.at[i], t_s.at[n, 0], t_r.at[n, i], (near, m))
+            mine = pltpu.make_async_copy(dst.at[i], dst.at[i], t_l.at[n])
+            pl.when(here)(mine.wait)
+            pl.when(jnp.logical_not(here))(got.wait_recv)
+    for w in (0, 1):
+        pltpu.make_async_copy(held[w].at[3, 0], outs[w], o_l.at[w]).wait()
+    for copy in waits:
+        copy.wait_send()
+    for here, copy in cond_sends:
+        pl.when(jnp.logical_not(here))(copy.wait_send)
+
+
+def reduce_fast(enc_g, dec_g, y, q, a, gains):
+    dma = pltpu.SemaphoreType.DMA
+    any_ = pl.BlockSpec(memory_space=pl.ANY)
+    vmem = pl.BlockSpec(memory_space=pltpu.VMEM)
+    out = lambda shape, kind=jnp.bfloat16: jax.ShapeDtypeStruct(shape, kind)
+    n_e, n_d = enc_g.shape[0] // 32, dec_g.shape[0] // 32
+    quarter = y.shape[0] // 2
+    held = lambda *lead: [pltpu.VMEM(lead + (n, D), jnp.bfloat16) for n in (n_e, n_d)]
+    small = lambda n: pltpu.VMEM((n,) + gains.shape, jnp.float32)
+    return pl.pallas_call(
+        reduce_kernel,
+        in_specs=[any_] * 5 + [vmem],
+        out_specs=[any_] * 5 + [vmem],
+        out_shape=[out((n_e, D)), out((n_d, D))] + [out((2, quarter, D))] * 3 + [out(gains.shape, jnp.float32)],
+        scratch_shapes=held(4, 4) + held(4, 4) + held(4, 2) + held(4) + held(3) + [small(3), small(3), small(4)] + [
+            dma((4, 4, 2)), dma((4, 4, 2)), dma((4, 4, 2)), dma((4, 2, 2)), dma((4, 2, 2)), dma((4, 2)), dma((4, 2)),
+            dma((3, 2)), dma((3, 2)), dma((3, 2)), dma((3, 2)), dma((3,)), dma((3,)), dma((3,)), dma((3,)), dma((4,)), dma((2,)),
+        ],
+        compiler_params=pltpu.CompilerParams(collective_id=1, has_side_effects=True, vmem_limit_bytes=56 * 1024 * 1024),
+        name="reduce_fast",
+    )(enc_g, dec_g, y, q, a, gains)
+
+
 epsilon = 1e-06
 
 
@@ -323,6 +702,7 @@
 
 
 def on_device(
+    fast,
     questions,
     answers,
     q_segments,
@@ -339,29 +719,33 @@
     core = lax.axis_index("rows") % 2
     per_row, slots = entry_alive_flags.shape[1], entry_alive_flags.shape[2]
     half = per_row // 2
-    enc_w = gather_weights(enc_params)
-    dec_w = gather_weights(dec_params)
-    all_ids = lax.all_gather(entry_ids, "mem", axis=2, tiled=True)
-    rows_here = questions.shape[0]
-    numbers = my_row(
-        jnp.concatenate(
-            [
-                q_segments,
-                a_segments,
-                entry_alive_flags.reshape(rows_here, -1),
-                all_ids.reshape(rows_here, -1),
-            ],
-            1,
+    rows_here, row_len = q_segments.shape
+    segs = jnp.concatenate([q_segments, a_segments, entry_alive_flags.reshape(rows_here, -1)], 1)
+    if fast:
+        segs = jnp.pad(segs, ((0, 0), (0, -segs.shape[1] % 1024))).reshape(rows_here, -1, 128)
+        own_ids = entry_ids.reshape(rows_here, -1)
+        n_ids = own_ids.shape[1]
+        own_ids = jnp.pad(own_ids, ((0, 0), (0, 1024 - n_ids))).reshape(rows_here, 8, 128)
+        enc_w, dec_w, x_question, x_answer, grad_top, other_segs, ids = gather_fast(
+            enc_params.T, dec_params.T, questions, answers, cotangent.astype(jnp.bfloat16), segs, own_ids
         )
-    )
-    row_len = q_segments.shape[1]
+        mem = lax.axis_index("mem")
+        numbers = jnp.where(
+            mem // 2 == core, lax.dynamic_index_in_dim(segs, mem % 2, 0, keepdims=False), other_segs
+        ).reshape(-1)
+        ids = ids.reshape(ids.shape[0], -1)[:, :n_ids].reshape(ids.shape[0], per_row, -1)
+        ids = ids.transpose(1, 0, 2).reshape(-1)
+    else:
+        enc_w, dec_w = gather_weights(enc_params), gather_weights(dec_params)
+        ids = my_row(lax.all_gather(entry_ids, "mem", axis=2, tiled=True)).reshape(-1)
+        numbers = my_row(segs)
+        x_question, x_answer = to_rows(questions), to_rows(answers)
+        grad_top = to_rows(cotangent.astype(jnp.bfloat16))
+    x_question, x_answer = x_question.astype(jnp.float32), x_answer.astype(jnp.float32)
+    grad_top = grad_top.astype(jnp.float32)
     q_row = numbers[:row_len]
     a_row = numbers[row_len : 2 * row_len]
     alive = numbers[2 * row_len : 2 * row_len + per_row * slots]
-    ids = numbers[2 * row_len + per_row * slots :]
-    x_question = to_rows(questions).astype(jnp.float32)
-    x_answer = to_rows(answers).astype(jnp.float32)
-    grad_top = to_rows(cotangent.astype(jnp.bfloat16)).astype(jnp.float32)
 
     own_ids = lax.dynamic_slice_in_dim(ids, core * half * slots, half * slots, 0)
     entry_vals = memory_table[own_ids].reshape(half * slots * 2, D).astype(jnp.float32)
@@ -423,7 +807,7 @@
     pre_dec = project(normed_f2, dec_w[8 * D : 8 * D + FF])
     act_dec = jax.nn.gelu(pre_dec).astype(jnp.bfloat16)
     dec_three = dec_two + project_back(act_dec, dec_w[8 * D + FF :])
-    decoded = from_rows(dec_three.astype(jnp.bfloat16))
+    decoded = dec_three.astype(jnp.bfloat16)
 
     grad_w1d, grad_w2d, grad_nf2 = feed_back(
         grad_top, normed_f2, pre_dec, act_dec, dec_w[8 * D : 8 * D + FF], dec_w[8 * D + FF :]
@@ -456,11 +840,10 @@
     grad_self = jnp.concatenate([grad_qs, grad_skv], 1)
     grad_wself = outer_sum(grad_self, normed_a)
     grad_x, grad_gain2 = norm_back(x_answer, norm_gains[2], project_back(grad_self, dec_w[: 3 * D]))
-    grad_answers = from_rows((grad_one + grad_x).astype(jnp.bfloat16)).astype(jnp.float32)
+    grad_answers = (grad_one + grad_x).astype(jnp.bfloat16)
     dec_full = jnp.concatenate(
         [grad_wself, grad_wos, grad_wqc, grad_wckv, grad_woc, grad_w1d, grad_w2d], 0
     )
-    grad_decoder = reduce_weights(dec_full).astype(jnp.float32).T
 
     grad_w1e, grad_w2e, grad_nf1 = feed_back(
         grad_encoded, normed_f1, pre_enc, act_enc, enc_w[4 * D : 4 * D + FF], enc_w[4 * D + FF :]
@@ -479,19 +862,36 @@
     grad_in = project_back(grad_ekv, enc_w[D : 3 * D])
     grad_in = grad_in + jnp.pad(project_back(grad_qe, enc_w[:D]), ((0, extra), (0, 0)))
     grad_x, grad_gain0 = norm_back(enc_in, norm_gains[0], grad_in)
-    grad_questions = from_rows((grad_hidden + grad_x[:tokens]).astype(jnp.bfloat16)).astype(jnp.float32)
+    grad_questions = (grad_hidden + grad_x[:tokens]).astype(jnp.bfloat16)
     enc_full = jnp.concatenate([grad_wqe, grad_wkve, grad_woe, grad_w1e, grad_w2e], 0)
     gain_terms = jnp.stack(
         [grad_gain0, grad_gain1, grad_gain2, grad_gain3, grad_gain4, grad_gain5]
     )
-    grad_gains = lax.psum(gain_terms, ("rows", "mem"))
-    grad_encoder = reduce_weights(enc_full).astype(jnp.float32).T
-    return (decoded, grad_questions, grad_answers, grad_encoder, grad_decoder, grad_gains)
+    if fast:
+        grad_encoder, grad_decoder, decoded, grad_questions, grad_answers, grad_gains = reduce_fast(
+            enc_full, dec_full, decoded, grad_questions, grad_answers, jnp.pad(gain_terms, ((0, 2), (0, 0)))
+        )
+        grad_gains = grad_gains[:6]
+    else:
+        decoded, grad_questions, grad_answers = (
+            from_rows(values) for values in (decoded, grad_questions, grad_answers)
+        )
+        grad_gains = lax.psum(gain_terms, ("rows", "mem"))
+        grad_encoder, grad_decoder = reduce_weights(enc_full), reduce_weights(dec_full)
+    return (
+        decoded,
+        grad_questions.astype(jnp.float32),
+        grad_answers.astype(jnp.float32),
+        grad_encoder.astype(jnp.float32).T,
+        grad_decoder.astype(jnp.float32).T,
+        grad_gains,
+    )
 
 
 def solution(mesh):
+    fast = mesh.shape["rows"] == 8 and mesh.shape["mem"] == 4
     return jax.shard_map(
-        on_device,
+        functools.partial(on_device, fast),
         mesh=mesh,
         in_specs=(
             P("rows", "mem", None),

time: 1170 us -> 753 us (0.64)
  waiting for transfers between devices: 692 us -> 0.02 us
  Pallas kernels: 173 us -> 528 us
  blocking collectives: 54.2 us -> 0 us
  between operations: 16.6 us -> 1.97 us
    all_gather x8 -> x0, waiting for transfers between devices: 357 us -> none  [the longest x3 164 us: to_rows(): row = my_row(lax.all_gather(values, 'mem', axis=1, tiled=True))]
    pallas_call x0 -> x2, Pallas kernels: none -> 354 us  [the longest x1 199 us: reduce_fast(): pl.pallas_call(reduce_kernel, in_specs=[any_] * 5 + [vmem], out_specs=[an...]
    reduce_scatter x2 -> x0, waiting for transfers between devices: 330 us -> none  [reduce_weights(): lax.psum_scatter(grads, ('rows', 'mem'), scatter_dimension=0, tiled=True)]
    psum x1 -> x0, blocking collectives: 39.4 us -> none  [on_device(): grad_gains = lax.psum(gain_terms, ('rows', 'mem'))]
    all_gather x1 -> x0, blocking collectives: 14.9 us -> none  [on_device(): all_ids = lax.all_gather(entry_ids, 'mem', axis=2, tiled=True)]
  transfers between devices with their start and end apart: 23 -> 6, of which waited for: 10 -> 0; matrix products, arithmetic and copies ran while one was open for 16% -> 14% of each run, Pallas kernels for 13% -> 18%
where the time goes in v2:
time: 753 us; the launch traced here: 747 us
  Pallas kernels  528 us (70%)
  matrix products  157 us (21%)
  local copies, waits for them, and re-layouts  35.5 us (5%)
  other arithmetic  21.4 us (3%)
    pallas_call x1, Pallas kernels, reduce_fast(): pl.pallas_call(reduce_kernel, in_specs=[any_] * 5 + [vmem], out_specs=[an...  199 us
    pallas_call x1, Pallas kernels, gather_fast(): pl.pallas_call(gather_kernel, in_specs=[any_] * 7, out_specs=[any_] * 7,...  154 us
    pallas_call x3, Pallas kernels, attend_back(): pl.pallas_call(functools.partial(back_kernel, causal, t, nk - t), grid_sp...  94.6 us
    pallas_call x3, Pallas kernels, attend(): pl.pallas_call(functools.partial(attend_kernel, causal, t, nk - t), grid_...  80.2 us
    dot_general x12, matrix products, project_back(): jnp.einsum('ne,ed->nd', left, weight_t, preferred_element_type=jnp.float32)  56.5 us
    dot_general x12, matrix products, project(): jnp.einsum('nd,ed->ne', left, weight_t, preferred_element_type=jnp.float32)  53.2 us
    dot_general x12, matrix products, outer_sum(): jnp.einsum('ne,nd->ed', wide, narrow, preferred_element_type=jnp.float32)  47.7 us
  transfers between devices with their start and end apart: 6, of which 0 were waited for; matrix products, arithmetic and copies ran while one was open for 14% of the time, Pallas kernels for 18%

profile of v2, /device:TPU:0, one launch (start us, length us, event | category | flops | bytes accessed | tf_op | source)
XLA Modules:
  0.0 746.6 jit_solution(13833259985349462457)
XLA Ops:
  9.8 154.4 %gather_fast.1 = (bf16[9216,768]{1,0:T(8,128)(2,1)}, bf16[12288,768]{1,0:T(8,128)(2,1)}, bf16[512,768]{1,0:T(8,128)(2,1)}, bf16[512,768]{1,0:T(8,128)(2,1)}, bf1...) custom-call(bf16[288,768]{1,0:T(8,128)(2,1)} %bitcast.66, bf16[384,768]{1,0:T(8,128)(2,1)} %bitcast.65, ...), custom_call_target="tpu_custom_call" | custom-call | tf_op jit(solution)/shard_map/gather_fast/pallas_call | solution.py:417
  165.3 5.4 gather_fusion.3
  173.5 5.1 convolution_convert_fusion.8.own_k.own_v
  180.0 4.1 convolution_convert_fusion.5
  197.6 40.3 %attend.3 = (bf16[512,768]{1,0:T(8,128)(2,1)S(1)}, f32[512,768]{1,0:T(8,128)S(1)}) custom-call(s32[2,6]{1,0:T(2,128)S(1)} %add_convert_fusion.1.act, bf16[512,768]{1,0:T(8,128)(2,1)S(1)} %convolution_convert_fusion.19.q_ref, bf16[512,128]{1,0:T(8,128)(2,1)S(1)} %get-tuple-element.128.qaug_ref, bf16[640,1536]{1,0:T(8,128)(2,1)} %convolution_convert_fusion.8.own_k.own_v, ...), custom_call_target="tpu_custom_call" | custom-call | flops 2013265920 | bytes 3932160 | tf_op jit(solution)/shard_map/attend/pallas_call | solution.py:83
  240.7 5.2 fusion.33
  245.9 8.5 %multiply_reduce_fusion.12 = (f32[512]{0:T(512)S(1)}, f32[512,768]{1,0:T(8,128)S(1)}) fusion(f32[512,768]{1,0:T(8,128)S(1)} %get-tuple-element.135, bf16[9216,768]{1,0:T(8,128)(2,1)} %get-tuple-element.43, f32[512,3072]{1,0:T(8,128)S(1)} %fusion.33), kind=kOutput, calls=%fused_computation.129 | convolution fusion | flops 2431254016 | bytes 14157824 | tf_op jit(solution)/shard_map/ne,ed->nd/dot_general | solution.py:616
  254.4 3.7 convolution_convert_fusion.9.own_k.own_v
  259.1 20.4 %attend.4 = (bf16[512,768]{1,0:T(8,128)(2,1)S(1)}, f32[512,768]{1,0:T(8,128)S(1)}) custom-call(s32[2,4]{1,0:T(2,128)S(1)} %add_convert_fusion.3.act, bf16[512,768]{1,0:T(8,128)(2,1)S(1)} %slice.188.q_ref, bf16[512,128]{1,0:T(8,128)(2,1)S(1)} %get-tuple-element.127.qaug_ref, bf16[512,1536]{1,0:T(8,128)(2,1)S(1)} %slice.189.own_k.own_v, ...), custom_call_target="tpu_custom_call" | custom-call | flops 1610612736 | bytes 3145728 | tf_op jit(solution)/shard_map/attend/pallas_call | solution.py:83
  279.5 2.7 multiply_reduce_fusion.14
  285.0 19.5 %attend.5 = (bf16[512,768]{1,0:T(8,128)(2,1)S(1)}, f32[512,768]{1,0:T(8,128)S(1)}) custom-call(s32[2,4]{1,0:T(2,128)S(1)} %add_convert_fusion.2.act, bf16[512,768]{1,0:T(8,128)(2,1)S(1)} %convolution_convert_fusion.18.q_ref, bf16[512,128]{1,0:T(8,128)(2,1)S(1)} %get-tuple-element.127.qaug_ref, bf16[512,1536]{1,0:T(8,128)(2,1)S(1)} %convolution_convert_fusion.9.own_k.own_v, ...), custom_call_target="tpu_custom_call" | custom-call | flops 1610612736 | bytes 3145728 | tf_op jit(solution)/shard_map/attend/pallas_call | solution.py:83
  306.6 5.2 fusion.21
  311.8 9.6 %fusion.13 = bf16[512,3072]{1,0:T(8,128)(2,1)S(1)} fusion(f32[512,3072]{1,0:T(8,128)S(1)} %fusion.21, bf16[512,768]{1,0:T(8,128)(2,1)S(1)} %copy-done.37, bf16[12288,768]{1,0:T(8,128)(2,1)} %get-tuple-element.47), kind=kOutput, calls=%fused_computation.27 | convolution fusion | flops 2447376384 | bytes 14942208 | tf_op jit(solution)/shard_map/nd,ed->ne/dot_general | solution.py:612
  321.4 6.3 multiply_reduce_fusion.4
  330.3 23.4 %attend_back.3 = (bf16[512,768]{1,0:T(8,128)(2,1)S(1)}, f32[512,768]{1,0:T(8,128)S(1)}, f32[512,768]{1,0:T(8,128)S(1)}, bf16[512,768]{1,0:T(8,128)(2,1)S(1)}, bf16[512,768]{1,0:T(8,128)(2,1)S(1)}) custom-call(s32[2,4]{1,0:T(2,128)S(1)} %add_convert_fusion.2.act, bf16[512,768]{1,0:T(8,128)(2,1)S(1)} %convolution_convert_fusion.18.q_ref, ...), custom_call_target="tpu_custom_call" | custom-call | flops 4026531840 | bytes 9437184 | tf_op jit(solution)/shard_map/attend_back/pallas_call | solution.py:181
  353.8 3.1 multiply_reduce_fusion.5
  361.4 24.4 %attend_back.5 = (bf16[512,768]{1,0:T(8,128)(2,1)S(1)}, f32[512,768]{1,0:T(8,128)S(1)}, f32[512,768]{1,0:T(8,128)S(1)}, bf16[512,768]{1,0:T(8,128)(2,1)S(1)}, bf16[512,768]{1,0:T(8,128)(2,1)S(1)}) custom-call(s32[2,4]{1,0:T(2,128)S(1)} %add_convert_fusion.3.act, bf16[512,768]{1,0:T(8,128)(2,1)S(1)} %slice.188.q_ref, ...), custom_call_target="tpu_custom_call" | custom-call | flops 4026531840 | bytes 9437184 | tf_op jit(solution)/shard_map/attend_back/pallas_call | solution.py:181
  387.1 9.7 %add_convert_fusion.y_in = bf16[512,768]{1,0:T(8,128)(2,1)} fusion(f32[512,768]{1,0:T(8,128)S(1)} %get-tuple-element.141, bf16[12288,768]{1,0:T(8,128)(2,1)} %get-tuple-element.47, f32[512,3072]{1,0:T(8,128)} %copy-done.48), kind=kOutput, calls=%fused_computation.121 | convolution fusion | flops 2430861312 | bytes 13369344 | tf_op jit(solution)/shard_map/ne,ed->nd/dot_general | solution.py:616
  396.8 3.8 multiply_reduce_fusion.3
  401.0 8.5 %fusion.6 = bf16[512,3072]{1,0:T(8,128)(2,1)S(1)} fusion(f32[512,3072]{1,0:T(8,128)S(1)} %bitcast.86, bf16[9216,768]{1,0:T(8,128)(2,1)} %get-tuple-element.43, f32[512,768]{1,0:T(8,128)S(1)} %add_add_fusion.4), kind=kOutput, calls=%fused_computation.20 | convolution fusion | flops 2447769600 | bytes 15728640 | tf_op jit(solution)/shard_map/nd,ed->ne/dot_general | solution.py:612
  409.5 6.3 multiply_reduce_fusion.6
  418.6 46.8 %attend_back.4 = (bf16[512,768]{1,0:T(8,128)(2,1)S(1)}, f32[640,768]{1,0:T(8,128)S(1)}, f32[640,768]{1,0:T(8,128)S(1)}, bf16[640,768]{1,0:T(8,128)(2,1)S(1)}, bf16[640,768]{1,0:T(8,128)(2,1)S(1)}) custom-call(s32[2,6]{1,0:T(2,128)S(1)} %add_convert_fusion.1.act, bf16[512,768]{1,0:T(8,128)(2,1)S(1)} %copy-done.1, ...), custom_call_target="tpu_custom_call" | custom-call | flops 5033164800 | bytes 11796480 | tf_op jit(solution)/shard_map/attend_back/pallas_call | solution.py:181
  471.2 4.2 fusion.56
  475.4 3.9 fusion.18
  484.6 4.4 fusion.36
  495.3 4.9 fusion.15
  500.2 8.3 %fusion.14.dec_in = bf16[12288,768]{1,0:T(8,128)(2,1)} fusion(bf16[12288,768]{1,0:T(8,128)(2,1)} %fusion.15, bf16[512,768]{1,0:T(8,128)(2,1)S(1)} %copy-done.38, f32[512,3072]{1,0:T(8,128)} %copy-done.48), kind=kOutput, calls=%fused_computation.31 | convolution fusion | flops 2432434176 | bytes 11796480 | tf_op jit(solution)/shard_map/ne,nd->ed/dot_general | solution.py:620
  508.6 5.0 multiply_reduce_fusion
  514.7 3.6 fusion.37
  520.2 4.7 fusion.17
  524.9 8.4 %fusion.16.enc_in = bf16[9216,768]{1,0:T(8,128)(2,1)} fusion(bf16[9216,768]{1,0:T(8,128)(2,1)} %fusion.17, f32[512,768]{1,0:T(8,128)S(1)} %copy-done.19, f32[512,3072]{1,0:T(8,128)} %copy-done.47), kind=kOutput, calls=%fused_computation.36 | convolution fusion | flops 2432827392 | bytes 12582912 | tf_op jit(solution)/shard_map/ne,nd->ed/dot_general | solution.py:620
  538.7 199.1 %reduce_fast.1 = (bf16[288,768]{1,0:T(8,128)(2,1)}, bf16[384,768]{1,0:T(8,128)(2,1)}, bf16[2,256,768]{2,1,0:T(8,128)(2,1)}, bf16[2,256,768]{2,1,0:T(8,128)(2,1)}...) custom-call(bf16[9216,768]{1,0:T(8,128)(2,1)} %fusion.16.enc_in, bf16[12288,768]{1,0:T(8,128)(2,1)} %fusion.14.dec_in, ...), custom_call_target="tpu_custom_call" | custom-call | tf_op jit(solution)/shard_map/reduce_fast/pallas_call | solution.py:585
  (260 shorter events, 81.8 us)
Async XLA Ops:
  5.3 168.0 %copy-start.44 = (f32[768]{0:T(1024)}, f32[768]{0:T(1024)S(1)}, u32[]{:S(2)}) copy-start(f32[768]{0:T(1024)S(1)} %get-tuple-element.102) | copy-start | bytes 9220
  9.8 155.1 %copy-start.39 = (s32[1,2,24,128]{3,2,1,0:T(8,128)S(1)}, s32[1,2,24,128]{3,2,1,0:T(8,128)}, u32[]{:S(2)}) copy-start(s32[1,2,24,128]{3,2,1,0:T(8,128)} %copy.67) | copy-start | bytes 73732
  173.2 335.3 %copy-start.42 = (f32[640]{0:T(1024)}, f32[640]{0:T(1024)S(1)}, u32[]{:S(2)}) copy-start(f32[640]{0:T(1024)S(1)} %fusion.104) | copy-start | bytes 7684
  173.5 6.3 copy-start.22
  178.6 19.0 %collective-permute-start = (bf16[640,1536]{1,0:T(8,128)(2,1)}, bf16[640,1536]{1,0:T(8,128)(2,1)}, u32[]{:S(2)}, u32[]{:S(2)}) collective-permute-start(bf16[640,1536]{1,0:T(8,128)(2,1)} %convolution_convert_fusion.8.own_k.own_v), channel_id=1, source_target_pairs={{0,4},{4,0},{8,12},{12,8},{16,20},{20,16},{24,28},{28,24},{1,5},{5... | collective-permute-start | bytes 5898248 | tf_op jit(solution)/shard_map/ppermute | solution.py:639
  185.7 73.4 %collective-permute-start.1 = (bf16[512,1536]{1,0:T(8,128)(2,1)S(1)}, bf16[512,1536]{1,0:T(8,128)(2,1)}, u32[]{:S(2)}, u32[]{:S(2)}) collective-permute-start(bf16[512,1536]{1,0:T(8,128)(2,1)S(1)} %slice.189.own_k.own_v), channel_id=1, source_target_pairs={{0,4},{4,0},{8,12},{12,8},{16,20},{20,16},{24,28},{28,24},{1,5},{5... | collective-permute-start | bytes 4718600 | tf_op jit(solution)/shard_map/ppermute | solution.py:639
  197.3 40.6 %copy-start = (bf16[512,768]{1,0:T(8,128)(2,1)}, bf16[512,768]{1,0:T(8,128)(2,1)S(1)}, u32[]{:S(2)}) copy-start(bf16[512,768]{1,0:T(8,128)(2,1)S(1)} %convolution_convert_fusion.19.q_ref) | copy-start | bytes 2359300
  197.6 40.4 %copy-start.34 = (bf16[512,768]{1,0:T(8,128)(2,1)S(1)}, bf16[512,768]{1,0:T(8,128)(2,1)}, u32[]{:S(2)}) copy-start(bf16[512,768]{1,0:T(8,128)(2,1)} %get-tuple-element.41) | copy-start | bytes 2359300
  245.9 8.5 %copy-start.47 = (f32[512,3072]{1,0:T(8,128)}, f32[512,3072]{1,0:T(8,128)S(1)}, u32[]{:S(2)}) copy-start(f32[512,3072]{1,0:T(8,128)S(1)} %fusion.33) | copy-start | bytes 18874372
  258.1 26.8 %collective-permute-start.2 = (bf16[512,1536]{1,0:T(8,128)(2,1)S(1)}, bf16[512,1536]{1,0:T(8,128)(2,1)S(1)}, u32[]{:S(2)}, u32[]{:S(2)}) collective-permute-start(bf16[512,1536]{1,0:T(8,128)(2,1)S(1)} %convolution_convert_fusion.9.own_k.own_v), channel_id=1, source_target_pairs={{0,4},{4,0},{8,12},{12,8},{16,20},{20,16},{24,28},{28,24},{1,5},{5... | collective-permute-start | bytes 4718600 | tf_op jit(solution)/shard_map/ppermute | solution.py:639
  282.3 74.7 %copy-start.16 = (f32[512,768]{1,0:T(8,128)}, f32[512,768]{1,0:T(8,128)S(1)}, u32[]{:S(2)}) copy-start(f32[512,768]{1,0:T(8,128)S(1)} %get-tuple-element.137) | copy-start | bytes 4718596
  306.6 80.5 %copy-start.14 = (f32[512,768]{1,0:T(8,128)}, f32[512,768]{1,0:T(8,128)S(1)}, u32[]{:S(2)}) copy-start(f32[512,768]{1,0:T(8,128)S(1)} %get-tuple-element.141) | copy-start | bytes 4718596
  311.8 9.6 %copy-start.48 = (f32[512,3072]{1,0:T(8,128)}, f32[512,3072]{1,0:T(8,128)S(1)}, u32[]{:S(2)}) copy-start(f32[512,3072]{1,0:T(8,128)S(1)} %fusion.21) | copy-start | bytes 18874372
  321.4 6.3 copy-start.49
  353.7 43.1 %copy-start.2 = (f32[512,768]{1,0:T(8,128)}, f32[512,768]{1,0:T(8,128)S(1)}, u32[]{:S(2)}) copy-start(f32[512,768]{1,0:T(8,128)S(1)} %get-tuple-element.52) | copy-start | bytes 4718596
  353.7 43.1 %copy-start.4 = (f32[512,768]{1,0:T(8,128)}, f32[512,768]{1,0:T(8,128)S(1)}, u32[]{:S(2)}) copy-start(f32[512,768]{1,0:T(8,128)S(1)} %get-tuple-element.53) | copy-start | bytes 4718596
  360.2 36.7 %collective-permute-start.3 = (bf16[512,1536]{1,0:T(8,128)(2,1)S(1)}, bf16[512,1536]{1,0:T(8,128)(2,1)}, u32[]{:S(2)}, u32[]{:S(2)}) collective-permute-start(bf16[512,1536]{1,0:T(8,128)(2,1)S(1)} %pad_maximum_fusion.3), channel_id=1, source_target_pairs={{0,4},{4,0},{8,12},{12,8},{16,20},{20,16},{24,28},{28,24},{1,5},{5... | collective-permute-start | bytes 4718600 | tf_op jit(solution)/shard_map/ppermute | solution.py:639
  385.8 15.2 %slice-start.1 = ((s8[6291456]{0:T(1024)(128)(4,1)}), s8[4194304]{0:T(1024)(128)(4,1)S(1)}, s32[]{:S(2)}) async-start(s8[6291456]{0:T(1024)(128)(4,1)} %bitcast.85), calls=%async_computation.1 | async-start | bytes 8388608
  387.1 9.7 %copy-start.29 = (f32[512,768]{1,0:T(8,128)S(1)}, f32[512,768]{1,0:T(8,128)}, u32[]{:S(2)}) copy-start(f32[512,768]{1,0:T(8,128)} %copy-done.28) | copy-start | bytes 4718596
  387.1 13.9 %slice-start.2 = ((s8[6291456]{0:T(1024)(128)(4,1)}), s8[2097152]{0:T(1024)(128)(4,1)S(1)}, s32[]{:S(2)}) async-start(s8[6291456]{0:T(1024)(128)(4,1)} %bitcast.85), calls=%async_computation.2 | async-start | bytes 4194304
  387.1 82.2 %collective-permute-start.5 = (bf16[512,1536]{1,0:T(8,128)(2,1)}, bf16[512,1536]{1,0:T(8,128)(2,1)}, u32[]{:S(2)}, u32[]{:S(2)}) collective-permute-start(bf16[512,1536]{1,0:T(8,128)(2,1)} %pad_maximum_fusion.4), channel_id=1, source_target_pairs={{0,4},{4,0},{8,12},{12,8},{16,20},{20,16},{24,28},{28,24},{1,5},{5... | collective-permute-start | bytes 4718600 | tf_op jit(solution)/shard_map/ppermute | solution.py:639
  401.0 14.8 %copy-start.18 = (f32[512,768]{1,0:T(8,128)}, f32[512,768]{1,0:T(8,128)S(1)}, u32[]{:S(2)}) copy-start(f32[512,768]{1,0:T(8,128)S(1)} %add_add_fusion.4) | copy-start | bytes 4718596
  401.0 8.5 %copy-start.26 = (f32[512,768]{1,0:T(8,128)S(1)}, f32[512,768]{1,0:T(8,128)}, u32[]{:S(2)}) copy-start(f32[512,768]{1,0:T(8,128)} %copy-done.25) | copy-start | bytes 4718596
  409.5 6.3 copy-start.51
  418.5 46.8 %copy-start.32 = (bf16[640,768]{1,0:T(8,128)(2,1)S(1)}, bf16[640,768]{1,0:T(8,128)(2,1)}, u32[]{:S(2)}) copy-start(bf16[640,768]{1,0:T(8,128)(2,1)} %copy-done.31) | copy-start | bytes 2949124
  479.5 29.0 %collective-permute-start.4 = (bf16[640,1536]{1,0:T(8,128)(2,1)S(1)}, bf16[640,1536]{1,0:T(8,128)(2,1)S(1)}, u32[]{:S(2)}, u32[]{:S(2)}) collective-permute-start(bf16[640,1536]{1,0:T(8,128)(2,1)S(1)} %pad_maximum_fusion.2), channel_id=1, source_target_pairs={{0,4},{4,0},{8,12},{12,8},{16,20},{20,16},{24,28},{28,24},{1,5},{5... | collective-permute-start | bytes 5898248 | tf_op jit(solution)/shard_map/ppermute | solution.py:639
  500.2 8.4 %copy-start.11 = (f32[512,768]{1,0:T(8,128)S(1)}, f32[512,768]{1,0:T(8,128)}, u32[]{:S(2)}) copy-start(f32[512,768]{1,0:T(8,128)} %copy-done.10) | copy-start | bytes 4718596
  500.2 8.4 %copy-start.21 = (f32[128,768]{1,0:T(8,128)S(1)}, f32[128,768]{1,0:T(8,128)}, u32[]{:S(2)}) copy-start(f32[128,768]{1,0:T(8,128)} %copy-done.20) | copy-start | bytes 1179652
  500.2 8.4 %copy-start.45 = (f32[768]{0:T(1024)S(1)}, f32[768]{0:T(1024)}, u32[]{:S(2)}) copy-start(f32[768]{0:T(1024)} %copy-done.44) | copy-start | bytes 9220
  508.6 5.6 copy-start.41
  524.9 8.4 %copy-start.46 = (f32[1,768]{1,0:T(1,128)S(1)}, f32[1,768]{1,0:T(1,128)}, u32[]{:S(2)}) copy-start(f32[1,768]{1,0:T(1,128)} %reshape.408) | copy-start | bytes 9220
  524.9 11.1 %slice-start = ((f32[640]{0:T(1024)}), f32[512]{0:T(512)S(1)}, s32[]{:S(2)}) async-start(f32[640]{0:T(1024)} %copy-done.42), calls=%async_computation | async-start | bytes 4096 | tf_op jit(solution)/shard_map/slice | solution.py:865
  (30 other events, 84.4 us)

commit v3 on v1

--- a/solution.py
+++ b/solution.py
@@ -24,7 +24,7 @@
     return chunks
 
 
-def attend_kernel(causal, own_len, extra, act, q_ref, qaug_ref, own_k, own_v, oth_k, oth_v, kaug_ref, o_ref, lse_ref, s_ref, m_ref, l_ref, acc_ref):
+def attend_pair(causal, own_len, extra, when, q_ref, qaug_ref, own_k, own_v, oth_k, oth_v, kaug_ref, o_ref, lse_ref, s_ref, m_ref, l_ref, acc_ref):
     low = lax.broadcasted_iota(jnp.int32, (1, 128), 1) < HD
     chunks = key_chunks(own_len, extra)
     nk = own_len + extra
@@ -52,7 +52,7 @@
                     s_ref[place, cols] = s
                     m_ref[:, cols] = jnp.maximum(m_ref[:, cols], jnp.max(s.reshape(size // 8, 8, QB), 0))
 
-            pl.when(act[qb, ci] != 0)(score)
+            when(qb, ci)(score)
         m = jnp.max(m_ref[...], 0, keepdims=True)
         for ci, (side, at, size) in enumerate(chunks):
 
@@ -67,13 +67,29 @@
                 v_split = jnp.concatenate([jnp.where(low, v, zero), jnp.where(low, zero, v)], 0)
                 acc_ref[...] += lax.dot_general(pb, v_split, (((0,), (0,)), ((), ())), preferred_element_type=jnp.float32)
 
-            pl.when(act[qb, ci] != 0)(mix)
+            when(qb, ci)(mix)
         total = jnp.sum(l_ref[...], 0, keepdims=True)
         lse = m + jnp.log(total)
         rec = 1.0 / total
         wide = lambda row, h: jnp.broadcast_to(row[:, h * QB : (h + 1) * QB], (HD, QB))
         o_ref[rows, :] = (acc_ref[...] * jnp.concatenate([wide(rec, 0), wide(rec, 1)], 0).T).astype(jnp.bfloat16)
         lse_ref[rows, :] = jnp.concatenate([wide(lse, 1), wide(lse, 0)], 0).T
+
+
+def flagged(act):
+    return lambda qb, ci: pl.when(act[qb, ci] != 0)
+
+
+def always(qb, ci):
+    return lambda work: work()
+
+
+def attend_kernel(causal, own_len, extra, act, *refs):
+    attend_pair(causal, own_len, extra, flagged(act), *refs)
+
+
+def back_kernel(causal, own_len, extra, act, *refs):
+    back_pair(causal, own_len, extra, flagged(act), *refs)
 
 
 def attend(causal, act, q, qaug, own_kv, oth_kv, kaug):
@@ -112,7 +128,7 @@
     return jnp.where(lane64 == 8, hi, jnp.where(lane64 == 9, mid, jnp.where(lane64 == 10, lo, base)))
 
 
-def back_kernel(causal, own_len, extra, act, q_ref, qaug_ref, own_k, own_v, oth_k, oth_v, kaug_ref, o_ref, lse_ref, g_ref, dq_ref, dko_ref, dvo_ref, dkt_ref, dvt_ref, dk_acc, dv_acc, dq_acc):
+def back_pair(causal, own_len, extra, when, q_ref, qaug_ref, own_k, own_v, oth_k, oth_v, kaug_ref, o_ref, lse_ref, g_ref, dq_ref, dko_ref, dvo_ref, dkt_ref, dvt_ref, dk_acc, dv_acc, dq_acc):
     lane = lax.broadcasted_iota(jnp.int32, (1, 128), 1)
     low = lane < HD
     lane64 = lane % HD
@@ -165,7 +181,7 @@
                 dst = jnp.concatenate(dscores, 0)
                 dq_acc[...] += lax.dot_general(dst, k_split, (((0,), (0,)), ((), ())), preferred_element_type=jnp.float32)
 
-            pl.when(act[qb, ci] != 0)(work)
+            when(qb, ci)(work)
         dq_ref[rows, :] = (dq_acc[...] * HD ** (-0.5)).astype(jnp.bfloat16)
     dko_ref[...] = dk_acc[:nk, :]
     dvo_ref[...] = dv_acc[:nk, :]
@@ -218,6 +234,19 @@
 
 
 epsilon = 1e-06
+CHUNK = 512
+
+
+def dot_nt(left, right):
+    return lax.dot_general(left, right, (((1,), (1,)), ((), ())), preferred_element_type=jnp.float32)
+
+
+def dot_nn(left, right):
+    return lax.dot_general(left, right, (((1,), (0,)), ((), ())), preferred_element_type=jnp.float32)
+
+
+def dot_tn(left, right):
+    return lax.dot_general(left, right, (((0,), (0,)), ((), ())), preferred_element_type=jnp.float32)
 
 
 def rms_norm(values, gain):
@@ -225,8 +254,812 @@
 
 
 def norm_back(values, gain, grad):
-    unused, pull = jax.vjp(rms_norm, values, gain)
-    return pull(grad)
+    root = lax.rsqrt(jnp.mean(values * values, -1, keepdims=True) + epsilon)
+    unit = values * root
+    scaled = grad * gain
+    inner = jnp.mean(unit * scaled, -1, keepdims=True)
+    return root * (scaled - unit * inner), jnp.sum(grad * unit, 0, keepdims=True)
+
+
+def gelu_pair(pre):
+    root = 0.7978845608028654
+    square = pre * pre
+    bent = jnp.tanh(root * pre * (1.0 + 0.044715 * square))
+    half = 0.5 * (1.0 + bent)
+    slope = half + 0.5 * pre * (1.0 - bent * bent) * root * (1.0 + 0.134145 * square)
+    return pre * half, slope
+
+
+def feed_back_chunk(normed, grad_b, w1, w2, dw, total, first):
+    act, slope = gelu_pair(dot_nt(normed, w1))
+    act = act.astype(jnp.bfloat16)
+    grad_pre = (dot_nt(grad_b, w2) * slope).astype(jnp.bfloat16)
+    dw[0] = dot_tn(grad_pre, normed).astype(jnp.bfloat16)
+    dw[1] = dot_tn(act, grad_b).astype(jnp.bfloat16)
+    part = dot_nn(grad_pre, w1)
+
+    @pl.when(first)
+    def _():
+        total[...] = part
+
+    @pl.when(jnp.logical_not(first))
+    def _():
+        total[...] += part
+
+    return act
+
+
+class ChunkStore:
+    def __init__(self, slots, whole, places, sems):
+        self.slots, self.whole, self.places, self.sems = slots, whole, places, sems
+
+    def copy(self, i, which):
+        slot = lax.rem(i, 2)
+        rows = pl.ds(pl.multiple_of(self.places[which] + i * CHUNK, CHUNK), CHUNK)
+        return pltpu.make_async_copy(self.slots.at[slot, which], self.whole.at[rows], self.sems.at[slot, which])
+
+    def start(self, i):
+        for which in (0, 1):
+            self.copy(i, which).start()
+
+    def wait(self, i):
+        for which in (0, 1):
+            self.copy(i, which).wait()
+
+
+def whole_spec(shape):
+    return pl.BlockSpec(shape, lambda i: (0,) * len(shape))
+
+
+def decode_top_kernel(
+    d1_ref, mixed_ref, gains, grad_ref, wo_ref, w1_ref, w2_ref,
+    decoded_ref, grad_two_ref, grad_mix_ref, dgain_ref, whole,
+    d2_ref, normed_ref, acc_ref, total_ref, slots, dwo_ref, sems, sem_o,
+):
+    i = pl.program_id(0)
+    store = ChunkStore(slots, whole, (8 * D, 8 * D + FF), sems)
+
+    @pl.when(i == 0)
+    def _():
+        d2_ref[...] = d1_ref[...] + dot_nn(mixed_ref[...], wo_ref[...])
+        normed_ref[...] = rms_norm(d2_ref[...], gains[4:5, :]).astype(jnp.bfloat16)
+
+    pl.when(i >= 2)(lambda: store.wait(i - 2))
+    act = feed_back_chunk(
+        normed_ref[...], grad_ref[...], w1_ref[...], w2_ref[...], slots.at[lax.rem(i, 2)], total_ref, i == 0
+    )
+    store.start(i)
+    more = dot_nn(act, w2_ref[...])
+
+    @pl.when(i == 0)
+    def _():
+        acc_ref[...] = d2_ref[...] + more
+
+    @pl.when(i > 0)
+    def _():
+        acc_ref[...] += more
+
+    @pl.when(i == FF // CHUNK - 1)
+    def _():
+        decoded_ref[...] = acc_ref[...].astype(jnp.bfloat16)
+        grad_x, dgain = norm_back(d2_ref[...], gains[4:5, :], total_ref[...])
+        dgain_ref[...] = jnp.broadcast_to(dgain, dgain_ref.shape)
+        grad_two = grad_ref[...].astype(jnp.float32) + grad_x
+        grad_two_ref[...] = grad_two
+        grad_b = grad_two.astype(jnp.bfloat16)
+        dwo_ref[...] = dot_tn(mixed_ref[...], grad_b).astype(jnp.bfloat16)
+        last = pltpu.make_async_copy(dwo_ref, whole.at[pl.ds(7 * D, D)], sem_o)
+        last.start()
+        grad_mix_ref[...] = dot_nt(grad_b, wo_ref[...]).astype(jnp.bfloat16)
+        store.wait(i - 1)
+        store.wait(i)
+        last.wait()
+
+
+def decode_top(d1, mixed, gains, grad_top, dec_w):
+    t = d1.shape[0]
+    n = FF // CHUNK
+    tok = whole_spec((t, D))
+    return pl.pallas_call(
+        decode_top_kernel,
+        grid=(n,),
+        in_specs=[
+            tok, tok, whole_spec(gains.shape), tok,
+            pl.BlockSpec((D, D), lambda i: (7, 0)),
+            pl.BlockSpec((CHUNK, D), lambda i: (8 * D // CHUNK + i, 0)),
+            pl.BlockSpec((CHUNK, D), lambda i: (8 * D // CHUNK + n + i, 0)),
+        ],
+        out_specs=[tok, tok, tok, whole_spec((8, D)), pl.BlockSpec(memory_space=pl.ANY)],
+        out_shape=[
+            jax.ShapeDtypeStruct((t, D), jnp.bfloat16),
+            jax.ShapeDtypeStruct((t, D), jnp.float32),
+            jax.ShapeDtypeStruct((t, D), jnp.bfloat16),
+            jax.ShapeDtypeStruct((8, D), jnp.float32),
+            jax.ShapeDtypeStruct(dec_w.shape, jnp.bfloat16),
+        ],
+        scratch_shapes=[
+            pltpu.VMEM((t, D), jnp.float32),
+            pltpu.VMEM((t, D), jnp.bfloat16),
+            pltpu.VMEM((t, D), jnp.float32),
+            pltpu.VMEM((t, D), jnp.float32),
+            pltpu.VMEM((2, 2, CHUNK, D), jnp.bfloat16),
+            pltpu.VMEM((D, D), jnp.bfloat16),
+            pltpu.SemaphoreType.DMA((2, 2)),
+            pltpu.SemaphoreType.DMA,
+        ],
+        compiler_params=pltpu.CompilerParams(vmem_limit_bytes=48 * 1024 * 1024),
+        cost_estimate=pl.CostEstimate(flops=14 * t * FF * D, bytes_accessed=8 * FF * D, transcendentals=t * FF),
+        name="decode_top",
+    )(d1, mixed, gains, grad_top, dec_w, dec_w, dec_w)
+
+
+MESH = pl.DeviceIdType.MESH
+
+
+def position():
+    r, m = lax.axis_index("rows"), lax.axis_index("mem")
+    core = lax.rem(r, 2)
+    near = r + 1 - 2 * core
+    x_near = r + 2 - 4 * lax.rem(lax.div(r, 2), 2)
+    y_near = r + 4 - 8 * lax.div(r, 4)
+    first = x_near + core * (y_near - x_near)
+    second = y_near + core * (x_near - y_near)
+    both = first + second - r
+    turn = 1 - 2 * core
+    others = (near, second + turn, first + turn, both + turn)
+    return r, m, core, near, first, second, both, others
+
+
+def greet(pos):
+    r, m, core, near, first, second = pos[:6]
+    barrier = pltpu.get_barrier_semaphore()
+    count = 0
+    for to in (r, near):
+        for step in range(4):
+            if to is r and step == 0:
+                continue
+            pl.semaphore_signal(barrier, inc=1, device_id=(to, lax.rem(m + step, 4)), device_id_type=MESH)
+            count += 1
+    for to in (first, second):
+        pl.semaphore_signal(barrier, inc=1, device_id=(to, m), device_id_type=MESH)
+        count += 1
+    pl.semaphore_wait(barrier, count)
+
+
+def remote(src, dst, send, recv, to):
+    return pltpu.make_async_remote_copy(
+        src_ref=src, dst_ref=dst, send_sem=send, recv_sem=recv, device_id=to, device_id_type=MESH
+    )
+
+
+class Mail:
+    def __init__(self, pos):
+        self.pos = pos
+        self.started = []
+        self.maybe = []
+
+    def send(self, make):
+        make().start()
+        self.started.append(make)
+
+    def send_or_keep(self, here, make, keep):
+        pl.when(here())(lambda: keep().start())
+        pl.when(jnp.logical_not(here()))(lambda: make().start())
+        self.maybe.append((here, make))
+
+    def arrived(self, ref, sem):
+        near, m = self.pos[3], self.pos[1]
+        remote(ref, ref, sem, sem, (near, m)).wait_recv()
+
+    def finish(self):
+        for make in self.started:
+            make().wait_send()
+        for here, make in self.maybe:
+            pl.when(jnp.logical_not(here()))(lambda make=make: make().wait_send())
+
+
+def dma(*shape):
+    return pltpu.SemaphoreType.DMA(shape)
+
+
+def gather_sems(n):
+    return [dma(3, n), dma(3, n), dma(4, n), dma(4, n), dma(4, 2, n), dma(4, 2, n), dma(4, 4, n), dma(4, 4, n), dma(n)]
+
+
+class Gather:
+    def __init__(self, mail, ins, outs, sems):
+        self.mail, self.ins, self.outs = mail, ins, outs
+        self.z_s, self.z_r, self.a_s, self.a_r, self.b_s, self.b_r, self.c_s, self.c_r, self.l = sems
+
+    def at(self, w, row, step):
+        m = self.mail.pos[1]
+        size = self.ins[w].shape[0]
+        mem = lax.rem(m - step + 4, 4)
+        return self.outs[w].at[pl.ds(pl.multiple_of((row * 4 + mem) * size, 32), size)]
+
+    def own(self, w):
+        return pltpu.make_async_copy(self.ins[w], self.at(w, self.mail.pos[0], 0), self.l.at[w])
+
+    def ring(self, step):
+        r, m, core, near, first, second, both, others = self.mail.pos
+        for w in range(len(self.ins)):
+            if step == 0:
+                self.own(w).start()
+            else:
+                self.mail.arrived(self.at(w, r, step), self.z_r.at[step - 1, w])
+
+            def src(w=w):
+                return self.ins[w] if step == 0 else self.at(w, r, step)
+
+            def dst(w=w):
+                return self.at(w, r, step)
+
+            send = self.mail.send
+            if step < 3:
+                send(lambda w=w, src=src, dst=dst: remote(src(), dst(), self.z_s.at[step, w], self.z_r.at[step, w], (r, lax.rem(m + 1, 4))))
+            send(lambda w=w, src=src, dst=dst: remote(src(), dst(), self.a_s.at[step, w], self.a_r.at[step, w], (first, m)))
+            send(lambda w=w, src=src, dst=dst: remote(src(), dst(), self.b_s.at[step, 0, w], self.b_r.at[step, 0, w], (second, m)))
+            send(lambda w=w, src=src, dst=dst: remote(src(), dst(), self.c_s.at[step, 0, w], self.c_r.at[step, 0, w], (near, m)))
+
+    def from_first(self, step):
+        r, m, core, near, first, second, both, others = self.mail.pos
+        for w in range(len(self.ins)):
+            here = lambda w=w: self.at(w, first, step)
+            self.mail.arrived(here(), self.a_r.at[step, w])
+            self.mail.send(lambda w=w, here=here: remote(here(), here(), self.b_s.at[step, 1, w], self.b_r.at[step, 1, w], (second, m)))
+            self.mail.send(lambda w=w, here=here: remote(here(), here(), self.c_s.at[step, 1, w], self.c_r.at[step, 1, w], (near, m)))
+
+    def from_second(self, step):
+        r, m, core, near, first, second, both, others = self.mail.pos
+        for k, row in ((0, second), (1, both)):
+            for w in range(len(self.ins)):
+                here = lambda w=w, row=row: self.at(w, row, step)
+                self.mail.arrived(here(), self.b_r.at[step, k, w])
+                self.mail.send(lambda w=w, k=k, here=here: remote(here(), here(), self.c_s.at[step, 2 + k, w], self.c_r.at[step, 2 + k, w], (near, m)))
+
+    def finish(self):
+        others = self.mail.pos[7]
+        for step in range(4):
+            for k in range(4):
+                for w in range(len(self.ins)):
+                    self.mail.arrived(self.at(w, others[k], step), self.c_r.at[step, k, w])
+        for w in range(len(self.ins)):
+            self.own(w).wait()
+
+
+def gather_order(gather, more=()):
+    steps = [
+        (gather.ring, 0), (gather.ring, 1), (gather.from_first, 0), (gather.ring, 2), (gather.from_first, 1),
+        (gather.from_second, 0), (gather.ring, 3), (gather.from_first, 2), (gather.from_second, 1),
+        (gather.from_first, 3), (gather.from_second, 2), (gather.from_second, 3),
+    ]
+    return [functools.partial(*step) for step in steps]
+
+
+def token_sems(n):
+    return [dma(n, 2), dma(n, 2), dma(n)]
+
+
+class TokensIn:
+    def __init__(self, mail, pairs, sems):
+        self.mail, self.pairs = mail, pairs
+        self.t_s, self.t_r, self.t_l = sems
+
+    def start(self, n):
+        r, m, core, near = self.mail.pos[:4]
+        src, dst = self.pairs[n]
+        quarter = src.shape[1]
+        holder = lambda: lax.div(m * (3 - m), 2)
+        slot = lambda: lax.div(m, 2)
+        for i in (0, 1):
+            here = lambda i=i: jnp.logical_and(2 * core + i == m, holder() == core)
+            place = lambda: dst.at[pl.ds(pl.multiple_of(slot() * quarter, quarter), quarter)]
+            make = lambda i=i: remote(src.at[i], place(), self.t_s.at[n, i], self.t_r.at[n, slot()], (r - core + holder(), 2 * core + i))
+            keep = lambda i=i: pltpu.make_async_copy(src.at[i], place(), self.t_l.at[n])
+            self.mail.send_or_keep(here, make, keep)
+
+    def finish(self):
+        r, m, core, near = self.mail.pos[:4]
+        for n, (src, dst) in enumerate(self.pairs):
+            quarter = src.shape[1]
+            for li in (0, 1):
+                source = core if li == 0 else 3 - core
+                here = jnp.logical_and(lax.div(m, 2) == core, m == source)
+                place = lambda: dst.at[pl.ds(li * quarter, quarter)]
+                pl.when(here)(lambda: pltpu.make_async_copy(place(), place(), self.t_l.at[n]).wait())
+                pl.when(jnp.logical_not(here))(lambda: self.mail.arrived(place(), self.t_r.at[n, li]))
+
+
+class TokensOut:
+    def __init__(self, mail, pairs, sems):
+        self.mail, self.pairs = mail, pairs
+        self.t_s, self.t_r, self.t_l = sems
+
+    def start(self, n):
+        r, m, core, near = self.mail.pos[:4]
+        src, dst = self.pairs[n]
+        quarter = dst.shape[1]
+        row = lambda: lax.rem(m, 2)
+        for li in (0, 1):
+            to_mem = lambda li=li: core if li == 0 else 3 - core
+            here = lambda to_mem=to_mem: jnp.logical_and(to_mem() == m, lax.div(m, 2) == core)
+            place = lambda li=li: src.at[pl.ds(li * quarter, quarter)]
+            make = lambda li=li, to_mem=to_mem, place=place: remote(place(), dst.at[row()], self.t_s.at[n, li], self.t_r.at[n, row()], (r - core + lax.div(m, 2), to_mem()))
+            keep = lambda place=place: pltpu.make_async_copy(place(), dst.at[row()], self.t_l.at[n])
+            self.mail.send_or_keep(here, make, keep)
+
+    def finish(self):
+        r, m, core, near = self.mail.pos[:4]
+        holder = lax.div(m * (3 - m), 2)
+        for n, (src, dst) in enumerate(self.pairs):
+            for i in (0, 1):
+                here = jnp.logical_and(2 * core + i == m, holder == core)
+                pl.when(here)(lambda: pltpu.make_async_copy(dst.at[i], dst.at[i], self.t_l.at[n]).wait())
+                pl.when(jnp.logical_not(here))(lambda: self.mail.arrived(dst.at[i], self.t_r.at[n, i]))
+
+
+class NumbersIn:
+    def __init__(self, mail, seg_in, seg_out, ids_in, ids_out, sems):
+        self.mail, self.seg_in, self.seg_out, self.ids_in, self.ids_out = mail, seg_in, seg_out, ids_in, ids_out
+        self.i_s, self.i_r, self.i_l, self.n_s, self.n_r = sems
+
+    def start(self):
+        r, m, core, near = self.mail.pos[:4]
+        self.mail.send(lambda: remote(self.seg_in.at[lax.rem(m, 2)], self.seg_out, self.n_s, self.n_r, (near, m)))
+        for i in (0, 1):
+            make = lambda i=i, e=0, to=r: remote(self.ids_in.at[i], self.ids_out.at[m], self.i_s.at[i, e], self.i_r.at[m], (to, 2 * core + i))
+            self.mail.send(functools.partial(make, e=1, to=near))
+            here = lambda i=i: 2 * core + i == m
+            keep = lambda i=i: pltpu.make_async_copy(self.ids_in.at[i], self.ids_out.at[m], self.i_l)
+            self.mail.send_or_keep(here, make, keep)
+
+    def finish(self):
+        r, m, core, near = self.mail.pos[:4]
+        self.mail.arrived(self.seg_out, self.n_r)
+        for mem in range(4):
+            here = jnp.logical_and(lax.div(m, 2) == core, m == mem)
+            place = self.ids_out.at[mem]
+            pl.when(here)(lambda: pltpu.make_async_copy(place, place, self.i_l).wait())
+            pl.when(jnp.logical_not(here))(lambda: self.mail.arrived(place, self.i_r.at[mem]))
+
+
+def add_to(total, more):
+    def step(i, unused):
+        rows = pl.ds(pl.multiple_of(i * 32, 32), 32)
+        total[rows, :] = total[rows, :] + more[rows, :]
+        return unused
+
+    lax.fori_loop(0, total.shape[0] // 32, step, 0)
+
+
+def reduce_buffers(size):
+    block = lambda *lead: pltpu.VMEM(lead + (size, D), jnp.bfloat16)
+    return [block(4, 4), block(4, 4), block(4, 2), block(4), block(3)]
+
+
+def reduce_sems():
+    return [dma(4, 4), dma(4, 4), dma(4, 4), dma(4, 2), dma(4, 2), dma(4), dma(4), dma(3), dma(3), dma(1)]
+
+
+class Reduce:
+    def __init__(self, mail, source, out, buffers, sems):
+        self.mail, self.source, self.out = mail, source, out
+        self.held, self.rc, self.rb, self.ra, self.rz = buffers
+        self.l, self.c_s, self.c_r, self.b_s, self.b_r, self.a_s, self.a_r, self.z_s, self.z_r, self.o = sems
+
+    def at(self, row, j):
+        m = self.mail.pos[1]
+        size = self.out.shape[0]
+        mem = lax.rem(m + 7 - j, 4)
+        return self.source.at[pl.ds(pl.multiple_of((row * 4 + mem) * size, 32), size)]
+
+    def load(self, j, k):
+        r, m, core, near, first, second, both, others = self.mail.pos
+        return pltpu.make_async_copy(self.at((r, first, second, both)[k], j), self.held.at[j, k], self.l.at[j, k])
+
+    def start(self):
+        r, m, core, near, first, second, both, others = self.mail.pos
+        for j in range(4):
+            for k in (3, 2, 1, 0):
+                self.mail.send(lambda j=j, k=k: remote(self.at(others[k], j), self.rc.at[j, k], self.c_s.at[j, k], self.c_r.at[j, k], (near, m)))
+                self.load(j, k).start()
+
+    def from_core(self, j):
+        second, m = self.mail.pos[5], self.mail.pos[1]
+        for k in (3, 2, 1, 0):
+            self.load(j, k).wait()
+            self.mail.arrived(self.rc.at[j, k], self.c_r.at[j, k])
+            add_to(self.held.at[j, k], self.rc.at[j, k])
+            if k >= 2:
+                self.mail.send(lambda k=k: remote(self.held.at[j, k], self.rb.at[j, k - 2], self.b_s.at[j, k - 2], self.b_r.at[j, k - 2], (second, m)))
+
+    def from_second(self, j):
+        first, m = self.mail.pos[4], self.mail.pos[1]
+        for k in (1, 0):
+            self.mail.arrived(self.rb.at[j, k], self.b_r.at[j, k])
+            add_to(self.held.at[j, k], self.rb.at[j, k])
+            if k == 1:
+                self.mail.send(lambda: remote(self.held.at[j, 1], self.ra.at[j], self.a_s.at[j], self.a_r.at[j], (first, m)))
+
+    def result(self):
+        return pltpu.make_async_copy(self.held.at[3, 0], self.out, self.o.at[0])
+
+    def from_first(self, j):
+        r, m = self.mail.pos[:2]
+        self.mail.arrived(self.ra.at[j], self.a_r.at[j])
+        add_to(self.held.at[j, 0], self.ra.at[j])
+        if j > 0:
+            self.mail.arrived(self.rz.at[j - 1], self.z_r.at[j - 1])
+            add_to(self.held.at[j, 0], self.rz.at[j - 1])
+        if j < 3:
+            self.mail.send(lambda: remote(self.held.at[j, 0], self.rz.at[j], self.z_s.at[j], self.z_r.at[j], (r, lax.rem(m + 1, 4))))
+        else:
+            self.result().start()
+
+    def finish(self):
+        self.result().wait()
+
+
+def reduce_order(reduce):
+    steps = [
+        (reduce.from_core, 0), (reduce.from_core, 1), (reduce.from_second, 0), (reduce.from_core, 2),
+        (reduce.from_second, 1), (reduce.from_first, 0), (reduce.from_core, 3), (reduce.from_second, 2),
+        (reduce.from_first, 1), (reduce.from_second, 3), (reduce.from_first, 2), (reduce.from_first, 3),
+    ]
+    return [functools.partial(*step) for step in steps]
+
+
+class GainSums:
+    def __init__(self, mail, own, out, rg, gs, gz, sems):
+        self.mail, self.own, self.out, self.rg, self.gs, self.gz = mail, own, out, rg, gs, gz
+        self.g_s, self.g_r, self.gz_s, self.gz_r = sems
+
+    def hop(self, n):
+        r, m, core, near, first, second, both, others = self.mail.pos
+        x_near = first + core * (second - first)
+        y_near = second + core * (first - second)
+        if n > 0:
+            self.mail.arrived(self.rg.at[n - 1], self.g_r.at[n - 1])
+            before = self.own[...] if n == 1 else self.gs[n - 2]
+            self.gs[n - 1] = before + self.rg[n - 1]
+        if n < 3:
+            src = lambda: self.own if n == 0 else self.gs.at[n - 1]
+            to = (near, x_near, y_near)[n]
+            self.mail.send(lambda: remote(src(), self.rg.at[n], self.g_s.at[n], self.g_r.at[n], (to, m)))
+            return
+        self.gz[m] = self.gs[2]
+        for hop in (1, 2, 3):
+            self.mail.send(lambda hop=hop: remote(self.gs.at[2], self.gz.at[m], self.gz_s.at[hop - 1], self.gz_r.at[m], (r, lax.rem(m + hop, 4))))
+
+    def finish(self):
+        m = self.mail.pos[1]
+        for mem in range(4):
+            pl.when(m != mem)(lambda mem=mem: self.mail.arrived(self.gz.at[mem], self.gz_r.at[mem]))
+        self.out[...] = (self.gz[0] + self.gz[1]) + (self.gz[2] + self.gz[3])
+
+
+ANY = pl.BlockSpec(memory_space=pl.ANY)
+
+
+def shaped(shape, kind=jnp.bfloat16):
+    return jax.ShapeDtypeStruct(shape, kind)
+
+
+def gather_encoder_kernel(enc_in, q_in, seg_in, ids_in, enc_out, q_out, seg_out, ids_out, *sems):
+    mail = Mail(position())
+    gather = Gather(mail, (enc_in,), (enc_out,), sems[:9])
+    tokens = TokensIn(mail, ((q_in, q_out),), sems[9:12])
+    numbers = NumbersIn(mail, seg_in, seg_out, ids_in, ids_out, sems[12:])
+    greet(mail.pos)
+    numbers.start()
+    steps = gather_order(gather)
+    steps[0]()
+    tokens.start(0)
+    for step in steps[1:]:
+        step()
+    gather.finish()
+    tokens.finish()
+    numbers.finish()
+    mail.finish()
+
+
+def gather_encoder(enc_t, q, seg, ids):
+    return pl.pallas_call(
+        gather_encoder_kernel,
+        in_specs=[ANY] * 4,
+        out_specs=[ANY] * 4,
+        out_shape=[
+            shaped((32 * enc_t.shape[0], D)),
+            shaped((2 * q.shape[1], D)),
+            shaped(seg.shape[1:], jnp.int32),
+            shaped((4,) + ids.shape[1:], jnp.int32),
+        ],
+        scratch_shapes=gather_sems(1) + token_sems(1) + [dma(2, 2), dma(4), dma(), dma(), dma()],
+        compiler_params=pltpu.CompilerParams(collective_id=0, has_side_effects=True),
+        name="gather_encoder",
+    )(enc_t, q, seg, ids)
+
+
+def reduce_encoder_kernel(enc_in, q_in, gain_in, enc_out, q_out, gain_out, *rest):
+    mail = Mail(position())
+    reduce = Reduce(mail, enc_in, enc_out, rest[:5], rest[5:15])
+    tokens = TokensOut(mail, ((q_in, q_out),), rest[15:18])
+    gains = GainSums(mail, gain_in, gain_out, *rest[18:21], rest[21:])
+    greet(mail.pos)
+    gains.hop(0)
+    reduce.start()
+    steps = reduce_order(reduce)
+    steps[0]()
+    gains.hop(1)
+    tokens.start(0)
+    steps[1]()
+    gains.hop(2)
+    for step in steps[2:6]:
+        step()
+    gains.hop(3)
+    for step in steps[6:]:
+        step()
+    reduce.finish()
+    tokens.finish()
+    gains.finish()
+    mail.finish()
+
+
+def reduce_encoder(enc_g, q, gains):
+    vmem = pl.BlockSpec(memory_space=pltpu.VMEM)
+    size = enc_g.shape[0] // 32
+    small = lambda n: pltpu.VMEM((n,) + gains.shape, jnp.float32)
+    return pl.pallas_call(
+        reduce_encoder_kernel,
+        in_specs=[ANY, ANY, vmem],
+        out_specs=[ANY, ANY, vmem],
+        out_shape=[shaped((size, D)), shaped((2, q.shape[0] // 2, D)), shaped(gains.shape, jnp.float32)],
+        scratch_shapes=reduce_buffers(size) + reduce_sems() + token_sems(1) + [small(3), small(3), small(4)]
+        + [dma(3), dma(3), dma(3), dma(4)],
+        compiler_params=pltpu.CompilerParams(collective_id=3, has_side_effects=True, vmem_limit_bytes=40 * 1024 * 1024),
+        name="reduce_encoder",
+    )(enc_g, q, gains)
+
+
+PAIRS = H // 2
+CHUNKS = FF // CHUNK
+
+
+def encode_kernel(
+    fast, own_len, extra,
+    q_ref, qaug_ref, own_k, own_v, oth_k, oth_v, kaug_ref, x_ref, gains, wo_ref, w1_ref, w2_ref, *rest,
+):
+    i = pl.program_id(0)
+    if fast:
+        dec_in, a_in, g_in = rest[:3]
+        o_ref, lse_ref, h1_ref, nf1_ref, h2_ref, ne_ref, dec_out, a_out, g_out = rest[3:12]
+        s_ref, m_ref, l_ref, acc_ref, ff_ref = rest[12:17]
+        sems = rest[17:]
+        mail = Mail(position())
+        gather = Gather(mail, (dec_in,), (dec_out,), sems[:9])
+        tokens = TokensIn(mail, ((a_in, a_out), (g_in, g_out)), sems[9:12])
+        steps = gather_order(gather)
+        places = {2: (1, 2), 4: (3, 4), 5: (5,), 6: (6, 7), 7: (8,), 8: (9,), 10: (10,)}
+
+        @pl.when(i == 0)
+        def _():
+            greet(mail.pos)
+            steps[0]()
+            tokens.start(0)
+            tokens.start(1)
+
+        for at, which in places.items():
+
+            @pl.when(i == at)
+            def _(which=which):
+                for n in which:
+                    steps[n]()
+    else:
+        o_ref, lse_ref, h1_ref, nf1_ref, h2_ref, ne_ref = rest[:6]
+        s_ref, m_ref, l_ref, acc_ref, ff_ref = rest[6:]
+
+    @pl.when(i < PAIRS)
+    def _():
+        cols = pl.ds(pl.multiple_of(i * 128, 128), 128)
+        attend_pair(
+            False, own_len, extra, always, q_ref, qaug_ref, own_k, own_v, oth_k, oth_v, kaug_ref,
+            o_ref.at[:, cols], lse_ref, s_ref, m_ref, l_ref, acc_ref,
+        )
+
+    @pl.when(i == PAIRS)
+    def _():
+        h1_ref[...] = x_ref[...].astype(jnp.float32) + dot_nn(o_ref[...], wo_ref[...])
+        nf1_ref[...] = rms_norm(h1_ref[...], gains[1:2, :]).astype(jnp.bfloat16)
+        ff_ref[...] = h1_ref[...]
+
+    @pl.when(i >= PAIRS)
+    def _():
+        act = gelu_pair(dot_nt(nf1_ref[...], w1_ref[...]))[0].astype(jnp.bfloat16)
+        ff_ref[...] += dot_nn(act, w2_ref[...])
+
+    @pl.when(i == PAIRS + CHUNKS - 1)
+    def _():
+        h2_ref[...] = ff_ref[...]
+        ne_ref[...] = rms_norm(ff_ref[...], gains[5:6, :]).astype(jnp.bfloat16)
+        if fast:
+            steps[11]()
+            gather.finish()
+            tokens.finish()
+            mail.finish()
+
+
+def encode(fast, q, qaug, own_kv, oth_kv, kaug, x, gains, enc_w, dec_t, a, g):
+    t = q.shape[0]
+    nk = own_kv.shape[0]
+    pair = lambda i: jnp.minimum(i, PAIRS - 1)
+    chunk = lambda i: jnp.maximum(i - PAIRS, 0)
+    col = lambda first: pl.BlockSpec((nk, 128), lambda i: (0, first + pair(i)))
+    tok = whole_spec((t, D))
+    dims = lambda kind: jax.ShapeDtypeStruct((t, D), kind)
+    in_specs = [
+        pl.BlockSpec((t, 128), lambda i: (0, pair(i))), whole_spec((t, 128)),
+        col(0), col(PAIRS), col(0), col(PAIRS), whole_spec((2 * nk, 128)), tok, whole_spec(gains.shape),
+        pl.BlockSpec((D, D), lambda i: (3, 0)),
+        pl.BlockSpec((CHUNK, D), lambda i: (4 * D // CHUNK + chunk(i), 0)),
+        pl.BlockSpec((CHUNK, D), lambda i: (4 * D // CHUNK + CHUNKS + chunk(i), 0)),
+    ]
+    args = [q, qaug, own_kv, own_kv, oth_kv, oth_kv, kaug, x, gains, enc_w, enc_w, enc_w]
+    out_specs = [tok, pl.BlockSpec((t, 128), lambda i: (0, pair(i))), tok, tok, tok, tok]
+    out_shape = [dims(jnp.bfloat16), dims(jnp.float32), dims(jnp.float32), dims(jnp.bfloat16), dims(jnp.float32), dims(jnp.bfloat16)]
+    scratch = [
+        pltpu.VMEM((2 * nk, 2 * QB), jnp.float32), pltpu.VMEM((8, 2 * QB), jnp.float32),
+        pltpu.VMEM((8, 2 * QB), jnp.float32), pltpu.VMEM((QB, 128), jnp.float32), pltpu.VMEM((t, D), jnp.float32),
+    ]
+    params = dict(vmem_limit_bytes=48 * 1024 * 1024)
+    if fast:
+        in_specs += [ANY] * 3
+        args += [dec_t, a, g]
+        out_specs += [ANY] * 3
+        out_shape += [shaped((32 * dec_t.shape[0], D)), dims(jnp.bfloat16), dims(jnp.bfloat16)]
+        scratch += gather_sems(1) + token_sems(2)
+        params.update(collective_id=1, has_side_effects=True)
+    return pl.pallas_call(
+        functools.partial(encode_kernel, fast, t, nk - t),
+        grid=(PAIRS + CHUNKS,),
+        in_specs=in_specs,
+        out_specs=out_specs,
+        out_shape=out_shape,
+        scratch_shapes=scratch,
+        compiler_params=pltpu.CompilerParams(**params),
+        name="encode",
+    )(*args)
+
+
+def encode_back_kernel(
+    fast, own_len, extra,
+    grad_ref, nf1_ref, h1_ref, gains, wo_ref, w1_ref, w2_ref, o_ref,
+    q_ref, qaug_ref, own_k, own_v, oth_k, oth_v, kaug_ref, lse_ref, *rest,
+):
+    i = pl.program_id(0)
+    if fast:
+        dec_g, y_in, a_in = rest[:3]
+        rest = rest[3:]
+    whole, grad_h_ref, dgain_ref, dq_ref, dko_ref, dvo_ref, dkt_ref, dvt_ref = rest[:8]
+    rest = rest[8:]
+    if fast:
+        dec_out, y_out, a_out = rest[:3]
+        rest = rest[3:]
+    total_ref, grad_b, mix_ref, slots, dwo_ref, sems, sem_o, dk_acc, dv_acc, dq_acc = rest[:10]
+    store = ChunkStore(slots, whole, (4 * D, 4 * D + FF), sems)
+    store_o = lambda: pltpu.make_async_copy(dwo_ref, whole.at[pl.ds(3 * D, D)], sem_o)
+    if fast:
+        rest = rest[10:]
+        mail = Mail(position())
+        reduce = Reduce(mail, dec_g, dec_out, rest[:5], rest[5:15])
+        tokens = TokensOut(mail, ((y_in, y_out), (a_in, a_out)), rest[15:])
+        steps = reduce_order(reduce)
+        places = {1: (0,), 2: (1,), 4: (2, 3), 6: (4, 5, 6), 7: (7,), 8: (8,), 9: (9,), 11: (10,)}
+
+        @pl.when(i == 0)
+        def _():
+            greet(mail.pos)
+            reduce.start()
+            tokens.start(0)
+            tokens.start(1)
+
+        for at, which in places.items():
+
+            @pl.when(i == at)
+            def _(which=which):
+                for n in which:
+                    steps[n]()
+
+    @pl.when(i == 0)
+    def _():
+        grad_b[...] = grad_ref[...].astype(jnp.bfloat16)
+
+    @pl.when(i < CHUNKS)
+    def _():
+        pl.when(i >= 2)(lambda: store.wait(i - 2))
+        feed_back_chunk(
+            nf1_ref[...], grad_b[...], w1_ref[...], w2_ref[...], slots.at[lax.rem(i, 2)], total_ref, i == 0
+        )
+        store.start(i)
+
+    @pl.when(i == CHUNKS - 1)
+    def _():
+        grad_x, dgain = norm_back(h1_ref[...], gains[1:2, :], total_ref[...])
+        dgain_ref[...] = jnp.broadcast_to(dgain, dgain_ref.shape)
+        grad_h = grad_ref[...] + grad_x
+        grad_h_ref[...] = grad_h
+        top = grad_h.astype(jnp.bfloat16)
+        dwo_ref[...] = dot_tn(o_ref[...], top).astype(jnp.bfloat16)
+        store_o().start()
+        mix_ref[...] = dot_nt(top, wo_ref[...]).astype(jnp.bfloat16)
+        store.wait(i - 1)
+        store.wait(i)
+
+    @pl.when(i >= CHUNKS)
+    def _():
+        cols = pl.ds(pl.multiple_of((i - CHUNKS) * 128, 128), 128)
+        back_pair(
+            False, own_len, extra, always, q_ref, qaug_ref, own_k, own_v, oth_k, oth_v, kaug_ref,
+            o_ref.at[:, cols], lse_ref, mix_ref.at[:, cols],
+            dq_ref, dko_ref, dvo_ref, dkt_ref, dvt_ref, dk_acc, dv_acc, dq_acc,
+        )
+
+    @pl.when(i == PAIRS + CHUNKS - 1)
+    def _():
+        store_o().wait()
+        if fast:
+            steps[11]()
+            reduce.finish()
+            tokens.finish()
+            mail.finish()
+
+
+def encode_back(fast, grad, nf1, h1, gains, enc_w, o, q, qaug, own_kv, oth_kv, kaug, lse, dec_g, y, a):
+    t = q.shape[0]
+    nk = own_kv.shape[0]
+    pair = lambda i: jnp.maximum(i - CHUNKS, 0)
+    chunk = lambda i: jnp.minimum(i, CHUNKS - 1)
+    col = lambda first: pl.BlockSpec((nk, 128), lambda i: (0, first + pair(i)))
+    cols = pl.BlockSpec((t, 128), lambda i: (0, pair(i)))
+    tok = whole_spec((t, D))
+    dims = lambda kind, n=t: jax.ShapeDtypeStruct((n, D), kind)
+    in_specs = [
+        tok, tok, tok, whole_spec(gains.shape),
+        pl.BlockSpec((D, D), lambda i: (3, 0)),
+        pl.BlockSpec((CHUNK, D), lambda i: (4 * D // CHUNK + chunk(i), 0)),
+        pl.BlockSpec((CHUNK, D), lambda i: (4 * D // CHUNK + CHUNKS + chunk(i), 0)),
+        tok, cols, whole_spec((t, 128)), col(0), col(PAIRS), col(0), col(PAIRS), whole_spec((2 * nk, 128)), cols,
+    ]
+    args = [grad, nf1, h1, gains, enc_w, enc_w, enc_w, o, q, qaug, own_kv, own_kv, oth_kv, oth_kv, kaug, lse]
+    out_specs = [pl.BlockSpec(memory_space=pl.ANY), tok, whole_spec((8, D)), cols, col(0), col(0), col(0), col(0)]
+    out_shape = [
+        jax.ShapeDtypeStruct(enc_w.shape, jnp.bfloat16), dims(jnp.float32), dims(jnp.float32, 8), dims(jnp.bfloat16),
+        dims(jnp.float32, nk), dims(jnp.float32, nk), dims(jnp.bfloat16, nk), dims(jnp.bfloat16, nk),
+    ]
+    scratch = [
+        pltpu.VMEM((t, D), jnp.float32), pltpu.VMEM((t, D), jnp.bfloat16), pltpu.VMEM((t, D), jnp.bfloat16),
+        pltpu.VMEM((2, 2, CHUNK, D), jnp.bfloat16), pltpu.VMEM((D, D), jnp.bfloat16),
+        pltpu.SemaphoreType.DMA((2, 2)), pltpu.SemaphoreType.DMA,
+        pltpu.VMEM((2 * nk, 128), jnp.float32), pltpu.VMEM((2 * nk, 128), jnp.float32), pltpu.VMEM((QB, 128), jnp.float32),
+    ]
+    params = dict(vmem_limit_bytes=60 * 1024 * 1024)
+    if fast:
+        size = dec_g.shape[0] // 32
+        in_specs += [ANY] * 3
+        args += [dec_g, y, a]
+        out_specs += [ANY] * 3
+        out_shape += [shaped((size, D)), shaped((2, t // 2, D)), shaped((2, t // 2, D))]
+        scratch += reduce_buffers(size) + reduce_sems() + token_sems(2)
+        params.update(collective_id=2, has_side_effects=True)
+    return pl.pallas_call(
+        functools.partial(encode_back_kernel, fast, t, nk - t),
+        grid=(PAIRS + CHUNKS,),
+        in_specs=in_specs,
+        out_specs=out_specs,
+        out_shape=out_shape,
+        scratch_shapes=scratch,
+        compiler_params=pltpu.CompilerParams(**params),
+        name="encode_back",
+    )(*args)
 
 
 def project(left, weight_t):
@@ -244,15 +1077,6 @@
 def output_back(grad, mixed_b, w_out):
     grad_b = grad.astype(jnp.bfloat16)
     return (outer_sum(mixed_b, grad_b), project(grad_b, w_out).astype(jnp.bfloat16))
-
-
-def feed_back(grad, normed_b, pre_act, act_b, w_in, w_out):
-    grad_b = grad.astype(jnp.bfloat16)
-    grad_wout = outer_sum(act_b, grad_b)
-    grad_act = project(grad_b, w_out)
-    unused, pull = jax.vjp(jax.nn.gelu, pre_act)
-    grad_pre = pull(grad_act)[0].astype(jnp.bfloat16)
-    return (outer_sum(grad_pre, normed_b), grad_wout, project_back(grad_pre, w_in))
 
 
 def partner(values):
@@ -323,6 +1147,7 @@
 
 
 def on_device(
+    fast,
     questions,
     answers,
     q_segments,
@@ -339,29 +1164,30 @@
     core = lax.axis_index("rows") % 2
     per_row, slots = entry_alive_flags.shape[1], entry_alive_flags.shape[2]
     half = per_row // 2
-    enc_w = gather_weights(enc_params)
-    dec_w = gather_weights(dec_params)
-    all_ids = lax.all_gather(entry_ids, "mem", axis=2, tiled=True)
-    rows_here = questions.shape[0]
-    numbers = my_row(
-        jnp.concatenate(
-            [
-                q_segments,
-                a_segments,
-                entry_alive_flags.reshape(rows_here, -1),
-                all_ids.reshape(rows_here, -1),
-            ],
-            1,
-        )
-    )
-    row_len = q_segments.shape[1]
+    rows_here, row_len = q_segments.shape
+    segs = jnp.concatenate([q_segments, a_segments, entry_alive_flags.reshape(rows_here, -1)], 1)
+    if fast:
+        segs = jnp.pad(segs, ((0, 0), (0, -segs.shape[1] % 1024))).reshape(rows_here, -1, 128)
+        own_ids = entry_ids.reshape(rows_here, -1)
+        n_ids = own_ids.shape[1]
+        own_ids = jnp.pad(own_ids, ((0, 0), (0, 1024 - n_ids))).reshape(rows_here, 8, 128)
+        enc_w, x_question, other_segs, ids = gather_encoder(enc_params.T, questions, segs, own_ids)
+        mem = lax.axis_index("mem")
+        numbers = jnp.where(
+            mem // 2 == core, lax.dynamic_index_in_dim(segs, mem % 2, 0, keepdims=False), other_segs
+        ).reshape(-1)
+        ids = ids.reshape(ids.shape[0], -1)[:, :n_ids].reshape(ids.shape[0], per_row, -1)
+        ids = ids.transpose(1, 0, 2).reshape(-1)
+    else:
+        enc_w, dec_w = gather_weights(enc_params), gather_weights(dec_params)
+        ids = my_row(lax.all_gather(entry_ids, "mem", axis=2, tiled=True)).reshape(-1)
+        numbers = my_row(segs)
+        x_question, x_answer = to_rows(questions), to_rows(answers)
+        grad_top = to_rows(cotangent.astype(jnp.bfloat16))
+    gains = jnp.pad(norm_gains, ((0, 2), (0, 0)))
     q_row = numbers[:row_len]
     a_row = numbers[row_len : 2 * row_len]
     alive = numbers[2 * row_len : 2 * row_len + per_row * slots]
-    ids = numbers[2 * row_len + per_row * slots :]
-    x_question = to_rows(questions).astype(jnp.float32)
-    x_answer = to_rows(answers).astype(jnp.float32)
-    grad_top = to_rows(cotangent.astype(jnp.bfloat16)).astype(jnp.float32)
 
     own_ids = lax.dynamic_slice_in_dim(ids, core * half * slots, half * slots, 0)
     entry_vals = memory_table[own_ids].reshape(half * slots * 2, D).astype(jnp.float32)
@@ -390,24 +1216,23 @@
     self_act = flags_of(a_row, a_row, core, quarter, 0, True)
     cross_act = flags_of(a_row, q_row, core, quarter, 0, False)
 
-    enc_in = jnp.concatenate([x_question, jnp.pad(entry_vals, ((0, extra - n_prefix), (0, 0)))], 0)
+    enc_in = jnp.concatenate([x_question.astype(jnp.float32), jnp.pad(entry_vals, ((0, extra - n_prefix), (0, 0)))], 0)
     normed_q = rms_norm(enc_in, norm_gains[0]).astype(jnp.bfloat16)
     query_enc = project(normed_q[:tokens], enc_w[:D]).astype(jnp.bfloat16)
     enc_kv = project(normed_q, enc_w[D : 3 * D]).astype(jnp.bfloat16)
     enc_kv_other = partner(enc_kv)
 
+    mixed_enc, logsum_enc, hidden_one, normed_f1, hidden_two, encoded, *gathered = encode(
+        fast, query_enc, q_aug, enc_kv, enc_kv_other, enc_aug, x_question, gains, enc_w,
+        dec_params.T, answers, cotangent.astype(jnp.bfloat16),
+    )
+    if fast:
+        dec_w, x_answer, grad_top = gathered
+    x_answer = x_answer.astype(jnp.float32)
     normed_a = rms_norm(x_answer, norm_gains[2]).astype(jnp.bfloat16)
     qkv_self = project(normed_a, dec_w[: 3 * D]).astype(jnp.bfloat16)
     query_self, self_kv = qkv_self[:, :D], qkv_self[:, D:]
     self_kv_other = partner(self_kv)
-
-    mixed_enc, logsum_enc = attend(False, enc_act, query_enc, q_aug, enc_kv, enc_kv_other, enc_aug)
-    hidden_one = x_question + project_back(mixed_enc, enc_w[3 * D : 4 * D])
-    normed_f1 = rms_norm(hidden_one, norm_gains[1]).astype(jnp.bfloat16)
-    pre_enc = project(normed_f1, enc_w[4 * D : 4 * D + FF])
-    act_enc = jax.nn.gelu(pre_enc).astype(jnp.bfloat16)
-    hidden_two = hidden_one + project_back(act_enc, enc_w[4 * D + FF :])
-    encoded = rms_norm(hidden_two, norm_gains[5]).astype(jnp.bfloat16)
     cross_kv = project(encoded, dec_w[5 * D : 7 * D]).astype(jnp.bfloat16)
     cross_kv_other = partner(cross_kv)
 
@@ -418,19 +1243,9 @@
     mixed_cross, logsum_cross = attend(
         False, cross_act, query_cross, a_aug, cross_kv, cross_kv_other, cross_aug
     )
-    dec_two = dec_one + project_back(mixed_cross, dec_w[7 * D : 8 * D])
-    normed_f2 = rms_norm(dec_two, norm_gains[4]).astype(jnp.bfloat16)
-    pre_dec = project(normed_f2, dec_w[8 * D : 8 * D + FF])
-    act_dec = jax.nn.gelu(pre_dec).astype(jnp.bfloat16)
-    dec_three = dec_two + project_back(act_dec, dec_w[8 * D + FF :])
-    decoded = from_rows(dec_three.astype(jnp.bfloat16))
-
-    grad_w1d, grad_w2d, grad_nf2 = feed_back(
-        grad_top, normed_f2, pre_dec, act_dec, dec_w[8 * D : 8 * D + FF], dec_w[8 * D + FF :]
-    )
-    grad_x, grad_gain4 = norm_back(dec_two, norm_gains[4], grad_nf2)
-    grad_two = grad_top + grad_x
-    grad_woc, grad_mixc = output_back(grad_two, mixed_cross, dec_w[7 * D : 8 * D])
+    decoded, grad_two, grad_mixc, grad_gain4, dec_full = decode_top(
+        dec_one, mixed_cross, gains, grad_top, dec_w
+    )
     grad_qc, dk_own, dv_own, dk_other, dv_other = attend_back(
         False, cross_act, query_cross, a_aug, cross_kv, cross_kv_other, cross_aug,
         mixed_cross, logsum_cross, grad_mixc,
@@ -456,21 +1271,15 @@
     grad_self = jnp.concatenate([grad_qs, grad_skv], 1)
     grad_wself = outer_sum(grad_self, normed_a)
     grad_x, grad_gain2 = norm_back(x_answer, norm_gains[2], project_back(grad_self, dec_w[: 3 * D]))
-    grad_answers = from_rows((grad_one + grad_x).astype(jnp.bfloat16)).astype(jnp.float32)
-    dec_full = jnp.concatenate(
-        [grad_wself, grad_wos, grad_wqc, grad_wckv, grad_woc, grad_w1d, grad_w2d], 0
-    )
-    grad_decoder = reduce_weights(dec_full).astype(jnp.float32).T
-
-    grad_w1e, grad_w2e, grad_nf1 = feed_back(
-        grad_encoded, normed_f1, pre_enc, act_enc, enc_w[4 * D : 4 * D + FF], enc_w[4 * D + FF :]
-    )
-    grad_x, grad_gain1 = norm_back(hidden_one, norm_gains[1], grad_nf1)
-    grad_hidden = grad_encoded + grad_x
-    grad_woe, grad_mixe = output_back(grad_hidden, mixed_enc, enc_w[3 * D : 4 * D])
-    grad_qe, dk_own, dv_own, dk_other, dv_other = attend_back(
-        False, enc_act, query_enc, q_aug, enc_kv, enc_kv_other, enc_aug,
-        mixed_enc, logsum_enc, grad_mixe,
+    grad_answers = (grad_one + grad_x).astype(jnp.bfloat16)
+    dec_full = dec_full.at[: 3 * D].set(grad_wself)
+    dec_full = dec_full.at[3 * D : 4 * D].set(grad_wos)
+    dec_full = dec_full.at[4 * D : 5 * D].set(grad_wqc)
+    dec_full = dec_full.at[5 * D : 7 * D].set(grad_wckv)
+
+    enc_full, grad_hidden, grad_gain1, grad_qe, dk_own, dv_own, dk_other, dv_other, *reduced = encode_back(
+        fast, grad_encoded, normed_f1, hidden_one, gains, enc_w, mixed_enc, query_enc, q_aug,
+        enc_kv, enc_kv_other, enc_aug, logsum_enc, dec_full, decoded, grad_answers,
     )
     more = partner(jnp.concatenate([dk_other, dv_other], 1)).astype(jnp.float32)
     grad_ekv = (jnp.concatenate([dk_own, dv_own], 1) + more).astype(jnp.bfloat16)
@@ -479,19 +1288,38 @@
     grad_in = project_back(grad_ekv, enc_w[D : 3 * D])
     grad_in = grad_in + jnp.pad(project_back(grad_qe, enc_w[:D]), ((0, extra), (0, 0)))
     grad_x, grad_gain0 = norm_back(enc_in, norm_gains[0], grad_in)
-    grad_questions = from_rows((grad_hidden + grad_x[:tokens]).astype(jnp.bfloat16)).astype(jnp.float32)
-    enc_full = jnp.concatenate([grad_wqe, grad_wkve, grad_woe, grad_w1e, grad_w2e], 0)
-    gain_terms = jnp.stack(
-        [grad_gain0, grad_gain1, grad_gain2, grad_gain3, grad_gain4, grad_gain5]
-    )
-    grad_gains = lax.psum(gain_terms, ("rows", "mem"))
-    grad_encoder = reduce_weights(enc_full).astype(jnp.float32).T
-    return (decoded, grad_questions, grad_answers, grad_encoder, grad_decoder, grad_gains)
+    grad_questions = (grad_hidden + grad_x[:tokens]).astype(jnp.bfloat16)
+    enc_full = enc_full.at[:D].set(grad_wqe)
+    enc_full = enc_full.at[D : 3 * D].set(grad_wkve)
+    gain_terms = jnp.concatenate(
+        [grad_gain0, grad_gain1[:1], grad_gain2, grad_gain3, grad_gain4[:1], grad_gain5], 0
+    )
+    if fast:
+        grad_decoder, decoded, grad_answers = reduced
+        grad_encoder, grad_questions, grad_gains = reduce_encoder(
+            enc_full, grad_questions, jnp.pad(gain_terms, ((0, 2), (0, 0)))
+        )
+        grad_gains = grad_gains[:6]
+    else:
+        decoded, grad_questions, grad_answers = (
+            from_rows(values) for values in (decoded, grad_questions, grad_answers)
+        )
+        grad_gains = lax.psum(gain_terms, ("rows", "mem"))
+        grad_encoder, grad_decoder = reduce_weights(enc_full), reduce_weights(dec_full)
+    return (
+        decoded,
+        grad_questions.astype(jnp.float32),
+        grad_answers.astype(jnp.float32),
+        grad_encoder.astype(jnp.float32).T,
+        grad_decoder.astype(jnp.float32).T,
+        grad_gains,
+    )
 
 
 def solution(mesh):
+    fast = mesh.shape["rows"] == 8 and mesh.shape["mem"] == 4
     return jax.shard_map(
-        on_device,
+        functools.partial(on_device, fast),
         mesh=mesh,
         in_specs=(
             P("rows", "mem", None),

time: 1170 us -> 639 us (0.55)
  waiting for transfers between devices: 692 us -> 1.82 us
  Pallas kernels: 173 us -> 515 us
  matrix products: 158 us -> 58.5 us
  blocking collectives: 54.2 us -> 0 us
  between operations: 16.6 us -> 1.79 us
    pallas_call x0 -> x5, Pallas kernels: none -> 427 us  [the longest x1 126 us: encode_back(): pl.pallas_call(functools.partial(encode_back_kernel, fast, t, nk - t), gr...]
    all_gather x8 -> x0, waiting for transfers between devices: 357 us -> none  [the longest x3 164 us: to_rows(): row = my_row(lax.all_gather(values, 'mem', axis=1, tiled=True))]
    reduce_scatter x2 -> x0, waiting for transfers between devices: 330 us -> none  [reduce_weights(): lax.psum_scatter(grads, ('rows', 'mem'), scatter_dimension=0, tiled=True)]
    pallas_call x3 -> x2, Pallas kernels: 94.1 us -> 47.8 us  [attend_back(): pl.pallas_call(functools.partial(back_kernel, causal, t, nk - t), grid_sp...]
    psum x1 -> x0, blocking collectives: 39.4 us -> none  [on_device(): grad_gains = lax.psum(gain_terms, ('rows', 'mem'))]
    pallas_call x3 -> x2, Pallas kernels: 79.4 us -> 40.2 us  [attend(): pl.pallas_call(functools.partial(attend_kernel, causal, t, nk - t), grid_...]
    dot_general x12 -> x6, matrix products: 54.9 us -> 19.3 us  [project(): jnp.einsum('nd,ed->ne', left, weight_t, preferred_element_type=jnp.float32)]
    dot_general x12 -> x6, matrix products: 56.4 us -> 21.4 us  [project_back(): jnp.einsum('ne,ed->nd', left, weight_t, preferred_element_type=jnp.float32)]
  transfers between devices with their start and end apart: 23 -> 6, of which waited for: 10 -> 1; matrix products, arithmetic and copies ran while one was open for 16% -> 7% of each run, Pallas kernels for 13% -> 3%
where the time goes in v3:
time: 639 us; the launch traced here: 632 us
  Pallas kernels  515 us (81%)
  matrix products  58.5 us (9%)
  local copies, waits for them, and re-layouts  33.2 us (5%)
  other arithmetic  20.1 us (3%)
    pallas_call x1, Pallas kernels, encode_back(): pl.pallas_call(functools.partial(encode_back_kernel, fast, t, nk - t), gr...  126 us
    pallas_call x1, Pallas kernels, encode(): pl.pallas_call(functools.partial(encode_kernel, fast, t, nk - t), grid=(P...  115 us
    pallas_call x1, Pallas kernels, reduce_encoder(): pl.pallas_call(reduce_encoder_kernel, in_specs=[ANY, ANY, vmem], out_spec...  84.3 us
    pallas_call x1, Pallas kernels, gather_encoder(): pl.pallas_call(gather_encoder_kernel, in_specs=[ANY] * 4, out_specs=[ANY]...  73.6 us
    pallas_call x2, Pallas kernels, attend_back(): pl.pallas_call(functools.partial(back_kernel, causal, t, nk - t), grid_sp...  47.8 us
    pallas_call x2, Pallas kernels, attend(): pl.pallas_call(functools.partial(attend_kernel, causal, t, nk - t), grid_...  40.2 us
    pallas_call x1, Pallas kernels, decode_top(): pl.pallas_call(decode_top_kernel, grid=(n,), in_specs=[tok, tok, whole_sp...  28.7 us
    dot_general x6, matrix products, project_back(): jnp.einsum('ne,ed->nd', left, weight_t, preferred_element_type=jnp.float32)  21.4 us
  transfers between devices with their start and end apart: 6, of which 1 were waited for; matrix products, arithmetic and copies ran while one was open for 7% of the time, Pallas kernels for 3%

profile of v3, /device:TPU:0, one launch (start us, length us, event | category | flops | bytes accessed | tf_op | source)
XLA Modules:
  0.0 632.2 jit_solution(17507718029094972269)
XLA Ops:
  5.2 73.6 %gather_encoder.1 = (bf16[9216,768]{1,0:T(8,128)(2,1)}, bf16[512,768]{1,0:T(8,128)(2,1)}, s32[24,128]{1,0:T(8,128)}, s32[4,8,128]{2,1,0:T(8,128)}) custom-call(bf16[288,768]{1,0:T(8,128)(2,1)} %bitcast.55, bf16[2,256,768]{2,1,0:T(8,128)(2,1)} %q_in.1, s32[2,24,128]{2,1,0:T(8,128)} %bitcast.56, s32[2,8,128]{2,1,0:T(8,128)} %bitcast.60), custom_call_target="tpu_custom_call" | custom-call | tf_op jit(solution)/shard_map/gather_encoder/pallas_call | solution.py:767
  79.8 5.4 gather_fusion
  86.8 3.7 convolution_convert_fusion.4.own_k.own_v
  92.6 2.4 convert_element_type.125.rest_2_
  99.8 2.4 convolution_convert_fusion.11.q_ref
  102.6 115.2 %encode.1 = (bf16[512,768]{1,0:T(8,128)(2,1)S(1)}, f32[512,768]{1,0:T(8,128)}, f32[512,768]{1,0:T(8,128)}, bf16[512,768]{1,0:T(8,128)(2,1)S(1)}, f32[512,768]{1,...) custom-call(bf16[512,768]{1,0:T(8,128)(2,1)S(1)} %convolution_conver, ...), custom_call_target="tpu_custom_call" | custom-call | tf_op jit(solution)/shard_map/encode/pallas_call | solution.py:921
  218.0 4.9 convolution_convert_fusion.1
  229.6 3.4 convolution_convert_fusion.5.refs_2_.refs_3_
  234.8 20.8 %attend.2 = (bf16[512,768]{1,0:T(8,128)(2,1)S(1)}, f32[512,768]{1,0:T(8,128)S(1)}) custom-call(s32[2,4]{1,0:T(2,128)S(1)} %add_convert_fusion.1.act, bf16[512,768]{1,0:T(8,128)(2,1)S(1)} %slice.247.refs_0_, bf16[512,128]{1,0:T(8,128)(2,1)S(1)} %get-tuple-element.218.refs_1_, bf16[512,1536]{1,0:T(8,128)(2,1)S(1)} %slice.248.refs_2_.refs_3_, ...), custom_call_target="tpu_custom_call" | custom-call | flops 1610612736 | bytes 3145728 | tf_op jit(solution)/shard_map/attend/pallas_call | solution.py:99
  255.6 2.7 multiply_reduce_fusion.6
  258.3 2.7 convolution_convert_fusion.10.refs_0_
  261.1 19.5 %attend.3 = (bf16[512,768]{1,0:T(8,128)(2,1)S(1)}, f32[512,768]{1,0:T(8,128)S(1)}) custom-call(s32[2,4]{1,0:T(2,128)S(1)} %add_convert_fusion.act, bf16[512,768]{1,0:T(8,128)(2,1)S(1)} %convolution_convert_fusion.10.refs_0_, bf16[512,128]{1,0:T(8,128)(2,1)S(1)} %get-tuple-element.218.refs_1_, ...), custom_call_target="tpu_custom_call" | custom-call | flops 1610612736 | bytes 3145728 | tf_op jit(solution)/shard_map/attend/pallas_call | solution.py:99
  280.6 28.7 %decode_top.1 = (bf16[512,768]{1,0:T(8,128)(2,1)S(1)}, f32[512,768]{1,0:T(8,128)S(1)}, bf16[512,768]{1,0:T(8,128)(2,1)S(1)}, f32[8,768]{1,0:T(8,128)S(1)}, bf16[12288,768]{1,0:T(8,128)(2,1)}) custom-call(f32[512,768]{1,0:T(8,128)} %copy-done.26, bf16[512,768]{1,0:T(8,128)(2,1)S(1)} %get-tuple-element.133.mixed_ref.refs_7_, f32[8,768]{1,0:T(8,128)S(1)} %pad.48.gains, ...), custom_call_target="tpu_custom_call" | custom-call | flops 16911433728 | bytes 18874368 | tf_op jit(solution)/shard_map/decode_top/pallas_call | solution.py:363
  314.8 23.6 %attend_back.2 = (bf16[512,768]{1,0:T(8,128)(2,1)S(1)}, f32[512,768]{1,0:T(8,128)S(1)}, f32[512,768]{1,0:T(8,128)S(1)}, bf16[512,768]{1,0:T(8,128)(2,1)S(1)}, bf16[512,768]{1,0:T(8,128)(2,1)S(1)}) custom-call(s32[2,4]{1,0:T(2,128)S(1)} %add_convert_fusion.act, bf16[512,768]{1,0:T(8,128)(2,1)S(1)} %convolution_convert_fusion.10.refs_0_, ...), custom_call_target="tpu_custom_call" | custom-call | flops 4026531840 | bytes 9437184 | tf_op jit(solution)/shard_map/attend_back/pallas_call | solution.py:197
  338.4 2.8 multiply_reduce_fusion.3
  341.6 2.2 convolution_convert_fusion.9.refs_9_
  343.8 24.2 %attend_back.3 = (bf16[512,768]{1,0:T(8,128)(2,1)S(1)}, f32[512,768]{1,0:T(8,128)S(1)}, f32[512,768]{1,0:T(8,128)S(1)}, bf16[512,768]{1,0:T(8,128)(2,1)S(1)}, bf16[512,768]{1,0:T(8,128)(2,1)S(1)}) custom-call(s32[2,4]{1,0:T(2,128)S(1)} %add_convert_fusion.1.act, bf16[512,768]{1,0:T(8,128)(2,1)S(1)} %slice.247.refs_0_, ...), custom_call_target="tpu_custom_call" | custom-call | flops 4026531840 | bytes 9437184 | tf_op jit(solution)/shard_map/attend_back/pallas_call | solution.py:197
  369.8 1.8 collective-permute-done.4
  371.9 4.2 fusion.27
  376.1 4.0 fusion
  380.1 1.8 fusion.34
  381.9 2.0 fusion.33
  383.9 3.3 multiply_reduce_fusion.2
  390.0 3.0 fusion.2.rest_0_
  393.0 125.6 %encode_back.1 = (bf16[9216,768]{1,0:T(8,128)(2,1)}, f32[512,768]{1,0:T(8,128)}, f32[8,768]{1,0:T(8,128)}, bf16[512,768]{1,0:T(8,128)(2,1)}, f32[640,768]{1,0:T(...) custom-call(f32[512,768]{1,0:T(8,128)} %subtract_multiply_fusion.gra, ...), custom_call_target="tpu_custom_call" | custom-call | tf_op jit(solution)/shard_map/encode_back/pallas_call | solution.py:1053
  522.6 2.5 convert_element_type.154
  525.1 1.9 fusion.32
  527.0 2.2 fusion.42
  529.2 6.2 multiply_reduce_fusion
  535.6 2.4 fusion.31.q_in
  538.6 5.3 fusion.3.enc_in
  543.9 84.3 %reduce_encoder.1 = (bf16[288,768]{1,0:T(8,128)(2,1)S(1)}, bf16[2,256,768]{2,1,0:T(8,128)(2,1)S(1)}, f32[8,768]{1,0:T(8,128)S(1)}) custom-call(bf16[9216,768]{1,0:T(8,128)(2,1)} %fusion.3.enc_in, bf16[512,768]{1,0:T(8,128)(2,1)S(1)} %fusion.31.q_in, f32[8,768]{1,0:T(8,128)S(1)} %pad.50.gain_in), custom_call_target="tpu_custom_call" | custom-call | tf_op jit(solution)/shard_map/reduce_encoder/pallas_call | solution.py:812
  (218 shorter events, 41.9 us)
Async XLA Ops:
  85.3 5.2 copy-start.29
  86.8 4.3 copy-start.36
  90.5 7.7 %copy-start.21 = (bf16[640,1536]{1,0:T(8,128)(2,1)}, bf16[640,1536]{1,0:T(8,128)(2,1)S(1)}, u32[]{:S(2)}) copy-start(bf16[640,1536]{1,0:T(8,128)(2,1)S(1)} %convolution_convert_fusion.4.own_k.own_v) | copy-start | bytes 5898244
  90.5 4.4 copy-start.35
  90.5 4.4 copy-start.37
  90.5 12.0 %collective-permute-start = (bf16[640,1536]{1,0:T(8,128)(2,1)S(1)}, bf16[640,1536]{1,0:T(8,128)(2,1)}, u32[]{:S(2)}, u32[]{:S(2)}) collective-permute-start(bf16[640,1536]{1,0:T(8,128)(2,1)S(1)} %convolution_convert_fusion.4.own_k.own_v), channel_id=1, source_target_pairs={{0,4},{4,0},{8,12},{12,8},{16,20},{20,16},{24,28},{28,24},{1,5},{5... | collective-permute-start | bytes 5898248 | tf_op jit(solution)/shard_map/ppermute | solution.py:1084
  91.1 189.5 %copy-start.6 = (f32[8,768]{1,0:T(8,128)}, f32[8,768]{1,0:T(8,128)S(1)}, u32[]{:S(2)}) copy-start(f32[8,768]{1,0:T(8,128)S(1)} %pad.48.gains) | copy-start | bytes 73732
  91.1 7.4 %copy-start.22 = (bf16[512,768]{1,0:T(8,128)(2,1)S(1)}, bf16[512,768]{1,0:T(8,128)(2,1)}, u32[]{:S(2)}) copy-start(bf16[512,768]{1,0:T(8,128)(2,1)} %get-tuple-element.124.x_ref) | copy-start | bytes 2359300
  96.3 6.0 copy-start.44
  98.5 4.0 copy-start.2
  102.2 115.5 %copy-start = (bf16[512,768]{1,0:T(8,128)(2,1)}, bf16[512,768]{1,0:T(8,128)(2,1)S(1)}, u32[]{:S(2)}) copy-start(bf16[512,768]{1,0:T(8,128)(2,1)S(1)} %convolution_convert_fusion.11.q_ref) | copy-start | bytes 2359300
  102.5 115.2 %copy-start.1 = (bf16[1280,128]{1,0:T(8,128)(2,1)}, bf16[1280,128]{1,0:T(8,128)(2,1)S(1)}, u32[]{:S(2)}) copy-start(bf16[1280,128]{1,0:T(8,128)(2,1)S(1)} %select_convert_fusion.kaug_ref) | copy-start | bytes 983044
  217.7 5.2 copy-start.3
  217.8 5.2 copy-start.4
  217.8 5.2 copy-start.7
  217.8 5.2 copy-start.9
  224.5 10.3 %collective-permute-start.1 = (bf16[512,1536]{1,0:T(8,128)(2,1)S(1)}, bf16[512,1536]{1,0:T(8,128)(2,1)}, u32[]{:S(2)}, u32[]{:S(2)}) collective-permute-start(bf16[512,1536]{1,0:T(8,128)(2,1)S(1)} %slice.248.refs_2_.refs_3_), channel_id=1, source_target_pairs={{0,4},{4,0},{8,12},{12,8},{16,20},{20,16},{24,28},{28,24},{1,5},{5... | collective-permute-start | bytes 4718600 | tf_op jit(solution)/shard_map/ppermute | solution.py:1084
  229.5 3.7 copy-start.40
  229.5 3.7 copy-start.41
  229.5 3.7 copy-start.42
  229.5 3.7 copy-start.43
  229.5 3.7 copy-start.45
  232.9 28.1 %collective-permute-start.2 = (bf16[512,1536]{1,0:T(8,128)(2,1)S(1)}, bf16[512,1536]{1,0:T(8,128)(2,1)S(1)}, u32[]{:S(2)}, u32[]{:S(2)}) collective-permute-start(bf16[512,1536]{1,0:T(8,128)(2,1)S(1)} %convolution_convert_fusion.5.refs_2_.refs_3_), channel_id=1, source_target_pairs={{0,4},{4,0},{8,12},{12,8},{16,20},{20,16},{24,28},{28,24},{1,5},{5... | collective-permute-start | bytes 4718600 | tf_op jit(solution)/shard_map/ppermute | solution.py:1084
  261.0 19.5 %copy-start.10 = (bf16[512,768]{1,0:T(8,128)(2,1)S(1)}, bf16[512,768]{1,0:T(8,128)(2,1)}, u32[]{:S(2)}) copy-start(bf16[512,768]{1,0:T(8,128)(2,1)} %copy-done.9) | copy-start | bytes 2359300
  280.5 28.7 %copy-start.13 = (bf16[512,768]{1,0:T(8,128)(2,1)}, bf16[512,768]{1,0:T(8,128)(2,1)S(1)}, u32[]{:S(2)}) copy-start(bf16[512,768]{1,0:T(8,128)(2,1)S(1)} %get-tuple-element.133.mixed_ref.refs_7_) | copy-start | bytes 2359300
  280.5 28.7 %copy-start.19 = (f32[512,768]{1,0:T(8,128)}, f32[512,768]{1,0:T(8,128)S(1)}, u32[]{:S(2)}) copy-start(f32[512,768]{1,0:T(8,128)S(1)} %get-tuple-element.134.refs_8_) | copy-start | bytes 4718596
  314.8 23.6 %copy-start.27 = (f32[512,768]{1,0:T(8,128)S(1)}, f32[512,768]{1,0:T(8,128)}, u32[]{:S(2)}) copy-start(f32[512,768]{1,0:T(8,128)} %copy-done.26) | copy-start | bytes 4718596
  368.1 3.5 collective-permute-start.4
  369.7 14.2 %collective-permute-start.3 = (bf16[512,1536]{1,0:T(8,128)(2,1)S(1)}, bf16[512,1536]{1,0:T(8,128)(2,1)S(1)}, u32[]{:S(2)}, u32[]{:S(2)}) collective-permute-start(bf16[512,1536]{1,0:T(8,128)(2,1)S(1)} %pad_maximum_fusion.2), channel_id=1, source_target_pairs={{0,4},{4,0},{8,12},{12,8},{16,20},{20,16},{24,28},{28,24},{1,5},{5... | collective-permute-start | bytes 4718600 | tf_op jit(solution)/shard_map/ppermute | solution.py:1084
  520.2 8.9 %collective-permute-start.5 = (bf16[640,1536]{1,0:T(8,128)(2,1)S(1)}, bf16[640,1536]{1,0:T(8,128)(2,1)}, u32[]{:S(2)}, u32[]{:S(2)}) collective-permute-start(bf16[640,1536]{1,0:T(8,128)(2,1)S(1)} %pad_maximum_fusion.1), channel_id=1, source_target_pairs={{0,4},{4,0},{8,12},{12,8},{16,20},{20,16},{24,28},{28,24},{1,5},{5... | collective-permute-start | bytes 5898248 | tf_op jit(solution)/shard_map/ppermute | solution.py:1084
  525.1 4.1 copy-start.48
  529.2 6.3 copy-start.28
  (25 other events, 49.9 us)

commit v4 on v3

--- a/solution.py
+++ b/solution.py
@@ -24,7 +24,22 @@
     return chunks
 
 
-def attend_pair(causal, own_len, extra, when, q_ref, qaug_ref, own_k, own_v, oth_k, oth_v, kaug_ref, o_ref, lse_ref, s_ref, m_ref, l_ref, acc_ref):
+def chunk_sets(causal, own_len, extra):
+    chunks = key_chunks(own_len, extra)
+    if not causal:
+        return [[list(range(len(chunks)))] * (own_len // QB)]
+    quarters = ((0, 3), (1, 2))
+    sets = []
+    for core in (0, 1):
+        held = (quarters[core], quarters[1 - core])
+        sets.append([
+            [n for n, (side, at, size) in enumerate(chunks) if held[side][at // QB] <= held[0][qb]]
+            for qb in range(own_len // QB)
+        ])
+    return sets
+
+
+def attend_pair(causal, own_len, extra, use, q_ref, qaug_ref, own_k, own_v, oth_k, oth_v, kaug_ref, o_ref, lse_ref, s_ref):
     low = lax.broadcasted_iota(jnp.int32, (1, 128), 1) < HD
     chunks = key_chunks(own_len, extra)
     nk = own_len + extra
@@ -33,66 +48,61 @@
         q = q_ref[rows, :] * jnp.bfloat16(HD ** (-0.5))
         qaug = qaug_ref[rows, :]
         queries = (jnp.where(low, q, qaug), jnp.where(low, qaug, q))
-        m_ref[...] = jnp.full(m_ref.shape, -3e30, jnp.float32)
-        l_ref[...] = jnp.zeros(l_ref.shape, jnp.float32)
-        acc_ref[...] = jnp.zeros(acc_ref.shape, jnp.float32)
-        for ci, (side, at, size) in enumerate(chunks):
-
-            def score(side=side, at=at, size=size):
-                k = (own_k, oth_k)[side][at : at + size, :]
-                place = slice(side * nk + at, side * nk + at + size)
-                kaug = kaug_ref[place, :]
-                for h in (0, 1):
-                    cols = slice(h * QB, (h + 1) * QB)
-                    keys = jnp.where(low, k, kaug) if h == 0 else jnp.where(low, kaug, k)
-                    s = lax.dot_general(keys, queries[h], (((1,), (1,)), ((), ())), preferred_element_type=jnp.float32)
-                    if causal and side == 0 and at == qb * QB:
-                        tri = lax.broadcasted_iota(jnp.int32, (size, QB), 0) <= lax.broadcasted_iota(jnp.int32, (size, QB), 1)
-                        s = jnp.where(tri, s, masked_score)
-                    s_ref[place, cols] = s
-                    m_ref[:, cols] = jnp.maximum(m_ref[:, cols], jnp.max(s.reshape(size // 8, 8, QB), 0))
-
-            when(qb, ci)(score)
-        m = jnp.max(m_ref[...], 0, keepdims=True)
-        for ci, (side, at, size) in enumerate(chunks):
-
-            def mix(side=side, at=at, size=size):
-                v = (own_v, oth_v)[side][at : at + size, :]
-                zero = jnp.zeros_like(v)
-                place = slice(side * nk + at, side * nk + at + size)
-                p = jnp.exp(s_ref[place, :] - m)
-                l_ref[...] += jnp.sum(p.reshape(size // 8, 8, 2 * QB), 0)
-                pb = p.astype(jnp.bfloat16)
-                pb = jnp.concatenate([pb[:, :QB], pb[:, QB:]], 0)
-                v_split = jnp.concatenate([jnp.where(low, v, zero), jnp.where(low, zero, v)], 0)
-                acc_ref[...] += lax.dot_general(pb, v_split, (((0,), (0,)), ((), ())), preferred_element_type=jnp.float32)
-
-            when(qb, ci)(mix)
-        total = jnp.sum(l_ref[...], 0, keepdims=True)
+        tops = [None, None]
+        for ci in use[qb]:
+            side, at, size = chunks[ci]
+            k = (own_k, oth_k)[side][at : at + size, :]
+            place = slice(side * nk + at, side * nk + at + size)
+            kaug = kaug_ref[place, :]
+            for h in (0, 1):
+                keys = jnp.where(low, k, kaug) if h == 0 else jnp.where(low, kaug, k)
+                s = lax.dot_general(keys, queries[h], (((1,), (1,)), ((), ())), preferred_element_type=jnp.float32)
+                if causal and side == 0 and at == qb * QB:
+                    tri = lax.broadcasted_iota(jnp.int32, (size, QB), 0) <= lax.broadcasted_iota(jnp.int32, (size, QB), 1)
+                    s = jnp.where(tri, s, masked_score)
+                s_ref[qb, place, h * QB : (h + 1) * QB] = s
+                top = jnp.max(s.reshape(size // 8, 8, QB), 0)
+                tops[h] = top if tops[h] is None else jnp.maximum(tops[h], top)
+        m = jnp.max(jnp.concatenate(tops, 1), 0, keepdims=True)
+        total, acc = None, None
+        for ci in use[qb]:
+            side, at, size = chunks[ci]
+            v = (own_v, oth_v)[side][at : at + size, :]
+            zero = jnp.zeros_like(v)
+            place = slice(side * nk + at, side * nk + at + size)
+            p = jnp.exp(s_ref[qb, place, :] - m)
+            part = jnp.sum(p.reshape(size // 8, 8, 2 * QB), 0)
+            total = part if total is None else total + part
+            pb = p.astype(jnp.bfloat16)
+            pb = jnp.concatenate([pb[:, :QB], pb[:, QB:]], 0)
+            v_split = jnp.concatenate([jnp.where(low, v, zero), jnp.where(low, zero, v)], 0)
+            part = lax.dot_general(pb, v_split, (((0,), (0,)), ((), ())), preferred_element_type=jnp.float32)
+            acc = part if acc is None else acc + part
+        total = jnp.sum(total, 0, keepdims=True)
         lse = m + jnp.log(total)
         rec = 1.0 / total
         wide = lambda row, h: jnp.broadcast_to(row[:, h * QB : (h + 1) * QB], (HD, QB))
-        o_ref[rows, :] = (acc_ref[...] * jnp.concatenate([wide(rec, 0), wide(rec, 1)], 0).T).astype(jnp.bfloat16)
+        o_ref[rows, :] = (acc * jnp.concatenate([wide(rec, 0), wide(rec, 1)], 0).T).astype(jnp.bfloat16)
         lse_ref[rows, :] = jnp.concatenate([wide(lse, 1), wide(lse, 0)], 0).T
 
 
-def flagged(act):
-    return lambda qb, ci: pl.when(act[qb, ci] != 0)
-
-
-def always(qb, ci):
-    return lambda work: work()
-
-
-def attend_kernel(causal, own_len, extra, act, *refs):
-    attend_pair(causal, own_len, extra, flagged(act), *refs)
-
-
-def back_kernel(causal, own_len, extra, act, *refs):
-    back_pair(causal, own_len, extra, flagged(act), *refs)
-
-
-def attend(causal, act, q, qaug, own_kv, oth_kv, kaug):
+def by_core(core, sets, work):
+    if len(sets) == 1:
+        work(sets[0])
+        return
+    for n, use in enumerate(sets):
+        pl.when(core[0] == n)(functools.partial(work, use))
+
+
+def attend_kernel(causal, own_len, extra, core, *refs):
+    by_core(core, chunk_sets(causal, own_len, extra), lambda use: attend_pair(causal, own_len, extra, use, *refs))
+
+
+def back_kernel(causal, own_len, extra, core, *refs):
+    by_core(core, chunk_sets(causal, own_len, extra), lambda use: back_pair(causal, own_len, extra, use, *refs))
+
+
+def attend(causal, core, q, qaug, own_kv, oth_kv, kaug):
     t = q.shape[0]
     nk = own_kv.shape[0]
     col = lambda first: pl.BlockSpec((nk, 128), lambda i, a: (0, first + i))
@@ -108,13 +118,13 @@
                 pl.BlockSpec((2 * nk, 128), lambda i, a: (0, 0)),
             ],
             out_specs=[pl.BlockSpec((t, 128), lambda i, a: (0, i))] * 2,
-            scratch_shapes=[pltpu.VMEM((2 * nk, 2 * QB), jnp.float32), pltpu.VMEM((8, 2 * QB), jnp.float32), pltpu.VMEM((8, 2 * QB), jnp.float32), pltpu.VMEM((QB, 128), jnp.float32)],
+            scratch_shapes=[pltpu.VMEM((t // QB, 2 * nk, 2 * QB), jnp.float32)],
         ),
         out_shape=[jax.ShapeDtypeStruct((t, D), jnp.bfloat16), jax.ShapeDtypeStruct((t, D), jnp.float32)],
         compiler_params=pltpu.CompilerParams(vmem_limit_bytes=40 * 1024 * 1024),
         cost_estimate=pl.CostEstimate(flops=4 * t * 2 * nk * D, bytes_accessed=8 * nk * D, transcendentals=t * 2 * nk * H),
         name="attend",
-    )(act, q, qaug, own_kv, own_kv, oth_kv, oth_kv, kaug)
+    )(core.reshape(1), q, qaug, own_kv, own_kv, oth_kv, oth_kv, kaug)
 
 
 def three_parts(value):
@@ -128,14 +138,13 @@
     return jnp.where(lane64 == 8, hi, jnp.where(lane64 == 9, mid, jnp.where(lane64 == 10, lo, base)))
 
 
-def back_pair(causal, own_len, extra, when, q_ref, qaug_ref, own_k, own_v, oth_k, oth_v, kaug_ref, o_ref, lse_ref, g_ref, dq_ref, dko_ref, dvo_ref, dkt_ref, dvt_ref, dk_acc, dv_acc, dq_acc):
+def back_pair(causal, own_len, extra, use, q_ref, qaug_ref, own_k, own_v, oth_k, oth_v, kaug_ref, o_ref, lse_ref, g_ref, dq_ref, dko_ref, dvo_ref, dkt_ref, dvt_ref, dk_acc, dv_acc):
     lane = lax.broadcasted_iota(jnp.int32, (1, 128), 1)
     low = lane < HD
     lane64 = lane % HD
     chunks = key_chunks(own_len, extra)
     nk = own_len + extra
-    dk_acc[...] = jnp.zeros(dk_acc.shape, jnp.float32)
-    dv_acc[...] = jnp.zeros(dv_acc.shape, jnp.float32)
+    begun = set()
     ones_aug = jnp.where((lane64 >= 8) & (lane64 <= 10), 1.0, 0.0).astype(jnp.bfloat16)
     for qb in range(own_len // QB):
         rows = pl.ds(qb * QB, QB)
@@ -151,45 +160,53 @@
         zero = jnp.zeros_like(q)
         q_split = jnp.concatenate([jnp.where(low, q, zero), jnp.where(low, zero, q)], 0)
         g_split = jnp.concatenate([jnp.where(low, g, zero), jnp.where(low, zero, g)], 0)
-        dq_acc[...] = jnp.zeros(dq_acc.shape, jnp.float32)
-        for ci, (side, at, size) in enumerate(chunks):
-
-            def work(side=side, at=at, size=size):
-                k = (own_k, oth_k)[side][at : at + size, :]
-                v = (own_v, oth_v)[side][at : at + size, :]
-                place = slice(side * nk + at, side * nk + at + size)
-                kaug = kaug_ref[place, :]
-                vaug = jnp.broadcast_to(ones_aug, v.shape)
-                zk = jnp.zeros_like(k)
-                probs, dscores = [], []
-                for h in (0, 1):
-                    keys = jnp.where(low, k, kaug) if h == 0 else jnp.where(low, kaug, k)
-                    vals = jnp.where(low, v, vaug) if h == 0 else jnp.where(low, vaug, v)
-                    s = lax.dot_general(keys, queries[h], (((1,), (1,)), ((), ())), preferred_element_type=jnp.float32)
-                    if causal and side == 0 and at == qb * QB:
-                        tri = lax.broadcasted_iota(jnp.int32, (size, QB), 0) <= lax.broadcasted_iota(jnp.int32, (size, QB), 1)
-                        s = jnp.where(tri, s, masked_score)
-                    p = jnp.exp(s)
-                    dp = lax.dot_general(vals, grads[h], (((1,), (1,)), ((), ())), preferred_element_type=jnp.float32)
-                    dscores.append((p * dp).astype(jnp.bfloat16))
-                    probs.append(p.astype(jnp.bfloat16))
-                ds = jnp.concatenate(dscores, 1)
-                pb = jnp.concatenate(probs, 1)
-                dk_acc[place, :] += jnp.dot(ds, q_split, preferred_element_type=jnp.float32)
-                dv_acc[place, :] += jnp.dot(pb, g_split, preferred_element_type=jnp.float32)
-                k_split = jnp.concatenate([jnp.where(low, k, zk), jnp.where(low, zk, k)], 0)
-                dst = jnp.concatenate(dscores, 0)
-                dq_acc[...] += lax.dot_general(dst, k_split, (((0,), (0,)), ((), ())), preferred_element_type=jnp.float32)
-
-            when(qb, ci)(work)
-        dq_ref[rows, :] = (dq_acc[...] * HD ** (-0.5)).astype(jnp.bfloat16)
+        dq = None
+        for ci in use[qb]:
+            side, at, size = chunks[ci]
+            k = (own_k, oth_k)[side][at : at + size, :]
+            v = (own_v, oth_v)[side][at : at + size, :]
+            place = slice(side * nk + at, side * nk + at + size)
+            kaug = kaug_ref[place, :]
+            vaug = jnp.broadcast_to(ones_aug, v.shape)
+            zk = jnp.zeros_like(k)
+            probs, dscores = [], []
+            for h in (0, 1):
+                keys = jnp.where(low, k, kaug) if h == 0 else jnp.where(low, kaug, k)
+                vals = jnp.where(low, v, vaug) if h == 0 else jnp.where(low, vaug, v)
+                s = lax.dot_general(keys, queries[h], (((1,), (1,)), ((), ())), preferred_element_type=jnp.float32)
+                if causal and side == 0 and at == qb * QB:
+                    tri = lax.broadcasted_iota(jnp.int32, (size, QB), 0) <= lax.broadcasted_iota(jnp.int32, (size, QB), 1)
+                    s = jnp.where(tri, s, masked_score)
+                p = jnp.exp(s)
+                dp = lax.dot_general(vals, grads[h], (((1,), (1,)), ((), ())), preferred_element_type=jnp.float32)
+                dscores.append((p * dp).astype(jnp.bfloat16))
+                probs.append(p.astype(jnp.bfloat16))
+            dk = jnp.dot(jnp.concatenate(dscores, 1), q_split, preferred_element_type=jnp.float32)
+            dv = jnp.dot(jnp.concatenate(probs, 1), g_split, preferred_element_type=jnp.float32)
+            if ci in begun:
+                dk_acc[place, :] += dk
+                dv_acc[place, :] += dv
+            else:
+                begun.add(ci)
+                dk_acc[place, :] = dk
+                dv_acc[place, :] = dv
+            k_split = jnp.concatenate([jnp.where(low, k, zk), jnp.where(low, zk, k)], 0)
+            dst = jnp.concatenate(dscores, 0)
+            part = lax.dot_general(dst, k_split, (((0,), (0,)), ((), ())), preferred_element_type=jnp.float32)
+            dq = part if dq is None else dq + part
+        dq_ref[rows, :] = (dq * HD ** (-0.5)).astype(jnp.bfloat16)
+    for ci, (side, at, size) in enumerate(chunks):
+        if ci not in begun:
+            place = slice(side * nk + at, side * nk + at + size)
+            dk_acc[place, :] = jnp.zeros((size, 128), jnp.float32)
+            dv_acc[place, :] = jnp.zeros((size, 128), jnp.float32)
     dko_ref[...] = dk_acc[:nk, :]
     dvo_ref[...] = dv_acc[:nk, :]
     dkt_ref[...] = dk_acc[nk:, :].astype(jnp.bfloat16)
     dvt_ref[...] = dv_acc[nk:, :].astype(jnp.bfloat16)
 
 
-def attend_back(causal, act, q, qaug, own_kv, oth_kv, kaug, mixed, lse, grad):
+def attend_back(causal, core, q, qaug, own_kv, oth_kv, kaug, mixed, lse, grad):
     t = q.shape[0]
     nk = own_kv.shape[0]
     col = lambda first: pl.BlockSpec((nk, 128), lambda i, a: (0, first + i))
@@ -207,7 +224,7 @@
                 tok, tok, tok,
             ],
             out_specs=[tok, col(0), col(0), col(0), col(0)],
-            scratch_shapes=[pltpu.VMEM((2 * nk, 128), jnp.float32), pltpu.VMEM((2 * nk, 128), jnp.float32), pltpu.VMEM((QB, 128), jnp.float32)],
+            scratch_shapes=[pltpu.VMEM((2 * nk, 128), jnp.float32), pltpu.VMEM((2 * nk, 128), jnp.float32)],
         ),
         out_shape=[
             jax.ShapeDtypeStruct((t, D), jnp.bfloat16),
@@ -219,7 +236,7 @@
         compiler_params=pltpu.CompilerParams(vmem_limit_bytes=40 * 1024 * 1024),
         cost_estimate=pl.CostEstimate(flops=10 * t * 2 * nk * D, bytes_accessed=24 * nk * D, transcendentals=t * 2 * nk * H),
         name="attend_back",
-    )(act, q, qaug, own_kv, own_kv, oth_kv, oth_kv, kaug, mixed, lse, grad)
+    )(core.reshape(1), q, qaug, own_kv, own_kv, oth_kv, oth_kv, kaug, mixed, lse, grad)
 
 
 def seg_aug_q(seg):
@@ -833,8 +850,8 @@
     if fast:
         dec_in, a_in, g_in = rest[:3]
         o_ref, lse_ref, h1_ref, nf1_ref, h2_ref, ne_ref, dec_out, a_out, g_out = rest[3:12]
-        s_ref, m_ref, l_ref, acc_ref, ff_ref = rest[12:17]
-        sems = rest[17:]
+        s_ref, ff_ref = rest[12:14]
+        sems = rest[14:]
         mail = Mail(position())
         gather = Gather(mail, (dec_in,), (dec_out,), sems[:9])
         tokens = TokensIn(mail, ((a_in, a_out), (g_in, g_out)), sems[9:12])
@@ -845,25 +862,26 @@
         def _():
             greet(mail.pos)
             steps[0]()
-            tokens.start(0)
-            tokens.start(1)
 
         for at, which in places.items():
 
             @pl.when(i == at)
-            def _(which=which):
+            def _(at=at, which=which):
                 for n in which:
                     steps[n]()
+                if at == 6:
+                    tokens.start(0)
+                    tokens.start(1)
     else:
         o_ref, lse_ref, h1_ref, nf1_ref, h2_ref, ne_ref = rest[:6]
-        s_ref, m_ref, l_ref, acc_ref, ff_ref = rest[6:]
+        s_ref, ff_ref = rest[6:]
 
     @pl.when(i < PAIRS)
     def _():
         cols = pl.ds(pl.multiple_of(i * 128, 128), 128)
         attend_pair(
-            False, own_len, extra, always, q_ref, qaug_ref, own_k, own_v, oth_k, oth_v, kaug_ref,
-            o_ref.at[:, cols], lse_ref, s_ref, m_ref, l_ref, acc_ref,
+            False, own_len, extra, chunk_sets(False, own_len, extra)[0],
+            q_ref, qaug_ref, own_k, own_v, oth_k, oth_v, kaug_ref, o_ref.at[:, cols], lse_ref, s_ref,
         )
 
     @pl.when(i == PAIRS)
@@ -907,8 +925,7 @@
     out_specs = [tok, pl.BlockSpec((t, 128), lambda i: (0, pair(i))), tok, tok, tok, tok]
     out_shape = [dims(jnp.bfloat16), dims(jnp.float32), dims(jnp.float32), dims(jnp.bfloat16), dims(jnp.float32), dims(jnp.bfloat16)]
     scratch = [
-        pltpu.VMEM((2 * nk, 2 * QB), jnp.float32), pltpu.VMEM((8, 2 * QB), jnp.float32),
-        pltpu.VMEM((8, 2 * QB), jnp.float32), pltpu.VMEM((QB, 128), jnp.float32), pltpu.VMEM((t, D), jnp.float32),
+        pltpu.VMEM((t // QB, 2 * nk, 2 * QB), jnp.float32), pltpu.VMEM((t, D), jnp.float32),
     ]
     params = dict(vmem_limit_bytes=48 * 1024 * 1024)
     if fast:
@@ -944,16 +961,16 @@
     if fast:
         dec_out, y_out, a_out = rest[:3]
         rest = rest[3:]
-    total_ref, grad_b, mix_ref, slots, dwo_ref, sems, sem_o, dk_acc, dv_acc, dq_acc = rest[:10]
+    total_ref, grad_b, mix_ref, slots, dwo_ref, sems, sem_o, dk_acc, dv_acc = rest[:9]
     store = ChunkStore(slots, whole, (4 * D, 4 * D + FF), sems)
     store_o = lambda: pltpu.make_async_copy(dwo_ref, whole.at[pl.ds(3 * D, D)], sem_o)
     if fast:
-        rest = rest[10:]
+        rest = rest[9:]
         mail = Mail(position())
         reduce = Reduce(mail, dec_g, dec_out, rest[:5], rest[5:15])
         tokens = TokensOut(mail, ((y_in, y_out), (a_in, a_out)), rest[15:])
         steps = reduce_order(reduce)
-        places = {1: (0,), 2: (1,), 4: (2, 3), 6: (4, 5, 6), 7: (7,), 8: (8,), 9: (9,), 11: (10,)}
+        places = {1: (0,), 2: (1,), 4: (2, 3), 7: (4, 6), 8: (5,), 10: (7, 8)}
 
         @pl.when(i == 0)
         def _():
@@ -998,16 +1015,17 @@
     def _():
         cols = pl.ds(pl.multiple_of((i - CHUNKS) * 128, 128), 128)
         back_pair(
-            False, own_len, extra, always, q_ref, qaug_ref, own_k, own_v, oth_k, oth_v, kaug_ref,
+            False, own_len, extra, chunk_sets(False, own_len, extra)[0], q_ref, qaug_ref, own_k, own_v, oth_k, oth_v, kaug_ref,
             o_ref.at[:, cols], lse_ref, mix_ref.at[:, cols],
-            dq_ref, dko_ref, dvo_ref, dkt_ref, dvt_ref, dk_acc, dv_acc, dq_acc,
+            dq_ref, dko_ref, dvo_ref, dkt_ref, dvt_ref, dk_acc, dv_acc,
         )
 
     @pl.when(i == PAIRS + CHUNKS - 1)
     def _():
         store_o().wait()
         if fast:
-            steps[11]()
+            for n in (9, 10, 11):
+                steps[n]()
             reduce.finish()
             tokens.finish()
             mail.finish()
@@ -1039,7 +1057,7 @@
         pltpu.VMEM((t, D), jnp.float32), pltpu.VMEM((t, D), jnp.bfloat16), pltpu.VMEM((t, D), jnp.bfloat16),
         pltpu.VMEM((2, 2, CHUNK, D), jnp.bfloat16), pltpu.VMEM((D, D), jnp.bfloat16),
         pltpu.SemaphoreType.DMA((2, 2)), pltpu.SemaphoreType.DMA,
-        pltpu.VMEM((2 * nk, 128), jnp.float32), pltpu.VMEM((2 * nk, 128), jnp.float32), pltpu.VMEM((QB, 128), jnp.float32),
+        pltpu.VMEM((2 * nk, 128), jnp.float32), pltpu.VMEM((2 * nk, 128), jnp.float32),
     ]
     params = dict(vmem_limit_bytes=60 * 1024 * 1024)
     if fast:
@@ -1126,24 +1144,6 @@
 
 def reduce_weights(grads):
     return lax.psum_scatter(grads, ("rows", "mem"), scatter_dimension=0, tiled=True)
-
-
-def flags_of(q_row, k_row, core, quarter, extra, causal):
-    n = q_row.shape[0] // quarter
-    ends_q = q_row.reshape(n, quarter)
-    ends_k = k_row.reshape(n, quarter)
-    meets = (ends_k[None, :, 0] <= ends_q[:, None, -1]) & (ends_q[:, None, 0] <= ends_k[None, :, -1])
-    if causal:
-        meets &= jnp.arange(n)[None, :] <= jnp.arange(n)[:, None]
-    mine = jnp.stack(quarters_of(core))
-    others = jnp.stack(quarters_of(1 - core))
-    meets = meets[mine]
-    always = [jnp.ones((2, 1), bool)] if extra else []
-    return jnp.concatenate([meets[:, mine]] + always + [meets[:, others]] + always, 1).astype(jnp.int32)
-
-
-def both_parts(own, other):
-    return jnp.concatenate([own, other], 0)
 
 
 def on_device(
@@ -1212,9 +1212,6 @@
     )
     self_aug = seg_aug_k(jnp.concatenate([own_a, other_a]))
     cross_aug = seg_aug_k(jnp.concatenate([own_q, other_q]))
-    enc_act = flags_of(q_row, q_row, core, quarter, extra, False)
-    self_act = flags_of(a_row, a_row, core, quarter, 0, True)
-    cross_act = flags_of(a_row, q_row, core, quarter, 0, False)
 
     enc_in = jnp.concatenate([x_question.astype(jnp.float32), jnp.pad(entry_vals, ((0, extra - n_prefix), (0, 0)))], 0)
     normed_q = rms_norm(enc_in, norm_gains[0]).astype(jnp.bfloat16)
@@ -1236,18 +1233,18 @@
     cross_kv = project(encoded, dec_w[5 * D : 7 * D]).astype(jnp.bfloat16)
     cross_kv_other = partner(cross_kv)
 
-    mixed_self, logsum_self = attend(True, self_act, query_self, a_aug, self_kv, self_kv_other, self_aug)
+    mixed_self, logsum_self = attend(True, core, query_self, a_aug, self_kv, self_kv_other, self_aug)
     dec_one = x_answer + project_back(mixed_self, dec_w[3 * D : 4 * D])
     normed_c = rms_norm(dec_one, norm_gains[3]).astype(jnp.bfloat16)
     query_cross = project(normed_c, dec_w[4 * D : 5 * D]).astype(jnp.bfloat16)
     mixed_cross, logsum_cross = attend(
-        False, cross_act, query_cross, a_aug, cross_kv, cross_kv_other, cross_aug
+        False, core, query_cross, a_aug, cross_kv, cross_kv_other, cross_aug
     )
     decoded, grad_two, grad_mixc, grad_gain4, dec_full = decode_top(
         dec_one, mixed_cross, gains, grad_top, dec_w
     )
     grad_qc, dk_own, dv_own, dk_other, dv_other = attend_back(
-        False, cross_act, query_cross, a_aug, cross_kv, cross_kv_other, cross_aug,
+        False, core, query_cross, a_aug, cross_kv, cross_kv_other, cross_aug,
         mixed_cross, logsum_cross, grad_mixc,
     )
     more = partner(jnp.concatenate([dk_other, dv_other], 1)).astype(jnp.float32)
@@ -1263,7 +1260,7 @@
     )
     grad_wos, grad_mixs = output_back(grad_one, mixed_self, dec_w[3 * D : 4 * D])
     grad_qs, dk_own, dv_own, dk_other, dv_other = attend_back(
-        True, self_act, query_self, a_aug, self_kv, self_kv_other, self_aug,
+        True, core, query_self, a_aug, self_kv, self_kv_other, self_aug,
         mixed_self, logsum_self, grad_mixs,
     )
     more = partner(jnp.concatenate([dk_other, dv_other], 1)).astype(jnp.float32)

time: 639 us -> 569 us (0.89)
  Pallas kernels: 515 us -> 443 us
    pallas_call x1, Pallas kernels: 126 us -> 102 us  [encode_back(): pl.pallas_call(functools.partial(encode_back_kernel, fast, t, nk - t), gr...]
    pallas_call x1, Pallas kernels: 115 us -> 97.6 us  [encode(): pl.pallas_call(functools.partial(encode_kernel, fast, t, nk - t), grid=(P...]
    pallas_call x2, Pallas kernels: 40.2 us -> 22.8 us  [attend(): pl.pallas_call(functools.partial(attend_kernel, causal, t, nk - t), grid_...]
    pallas_call x2, Pallas kernels: 47.8 us -> 39.3 us  [attend_back(): pl.pallas_call(functools.partial(back_kernel, causal, t, nk - t), grid_sp...]
    unnamed x120 -> x104, local copies, waits for them, and re-layouts: 18.3 us -> 20.5 us
  transfers between devices with their start and end apart: 6 -> 6, of which waited for: 1 -> 1; matrix products, arithmetic and copies ran while one was open for 7% -> 9% of each run, Pallas kernels for 3% -> 2%
where the time goes in v4:
time: 569 us; the launch traced here: 563 us
  Pallas kernels  443 us (78%)
  matrix products  58.5 us (10%)
  local copies, waits for them, and re-layouts  33.8 us (6%)
  other arithmetic  22.8 us (4%)
    pallas_call x1, Pallas kernels, encode_back(): pl.pallas_call(functools.partial(encode_back_kernel, fast, t, nk - t), gr...  102 us
    pallas_call x1, Pallas kernels, encode(): pl.pallas_call(functools.partial(encode_kernel, fast, t, nk - t), grid=(P...  97.6 us
    pallas_call x1, Pallas kernels, reduce_encoder(): pl.pallas_call(reduce_encoder_kernel, in_specs=[ANY, ANY, vmem], out_spec...  78.9 us
    pallas_call x1, Pallas kernels, gather_encoder(): pl.pallas_call(gather_encoder_kernel, in_specs=[ANY] * 4, out_specs=[ANY]...  73.5 us
    pallas_call x2, Pallas kernels, attend_back(): pl.pallas_call(functools.partial(back_kernel, causal, t, nk - t), grid_sp...  39.3 us
    pallas_call x1, Pallas kernels, decode_top(): pl.pallas_call(decode_top_kernel, grid=(n,), in_specs=[tok, tok, whole_sp...  28.4 us
    pallas_call x2, Pallas kernels, attend(): pl.pallas_call(functools.partial(attend_kernel, causal, t, nk - t), grid_...  22.8 us
    dot_general x6, matrix products, project_back(): jnp.einsum('ne,ed->nd', left, weight_t, preferred_element_type=jnp.float32)  22 us
  transfers between devices with their start and end apart: 6, of which 1 were waited for; matrix products, arithmetic and copies ran while one was open for 9% of the time, Pallas kernels for 2%

profile of v4, /device:TPU:0, one launch (start us, length us, event | category | flops | bytes accessed | tf_op | source)
XLA Modules:
  0.0 563.5 jit_solution(9621014930144964414)
XLA Ops:
  5.7 73.5 %gather_encoder.1 = (bf16[9216,768]{1,0:T(8,128)(2,1)}, bf16[512,768]{1,0:T(8,128)(2,1)}, s32[24,128]{1,0:T(8,128)}, s32[4,8,128]{2,1,0:T(8,128)}) custom-call(bf16[288,768]{1,0:T(8,128)(2,1)} %bitcast.40, bf16[2,256,768]{2,1,0:T(8,128)(2,1)} %q_in.1, s32[2,24,128]{2,1,0:T(8,128)} %bitcast.41, s32[2,8,128]{2,1,0:T(8,128)} %bitcast.45), custom_call_target="tpu_custom_call" | custom-call | tf_op jit(solution)/shard_map/gather_encoder/pallas_call | solution.py:784
  80.3 5.4 gather_fusion
  87.3 3.7 convolution_convert_fusion.4.own_k.own_v
  93.6 2.4 convert_element_type.119.rest_2_
  109.6 2.4 convolution_convert_fusion.11.q_ref
  112.4 97.6 %encode.1 = (bf16[512,768]{1,0:T(8,128)(2,1)S(1)}, f32[512,768]{1,0:T(8,128)}, f32[512,768]{1,0:T(8,128)}, bf16[512,768]{1,0:T(8,128)(2,1)S(1)}, f32[512,768]{1,...) custom-call(bf16[512,768]{1,0:T(8,128)(2,1)S(1)} %convolution_conver, ...), custom_call_target="tpu_custom_call" | custom-call | tf_op jit(solution)/shard_map/encode/pallas_call | solution.py:938
  210.3 4.7 convolution_convert_fusion.1
  215.6 3.1 convolution_convert_fusion.5.refs_2_.refs_3_
  219.2 10.0 %attend.2 = (bf16[512,768]{1,0:T(8,128)(2,1)S(1)}, f32[512,768]{1,0:T(8,128)S(1)}) custom-call(s32[1]{0:T(128)} %bitcast.6.core, bf16[512,768]{1,0:T(8,128)(2,1)S(1)} %slice.210.refs_0_, bf16[512,128]{1,0:T(8,128)(2,1)S(1)} %get-tuple-element.212.refs_1_, bf16[512,1536]{1,0:T(8,128)(2,1)S(1)} %slice.212.refs_2_.refs_3_, ...), custom_call_target="tpu_custom_call" | custom-call | flops 1610612736 | bytes 3145728 | tf_op jit(solution)/shard_map/attend/pallas_call | solution.py:109
  229.3 2.7 multiply_reduce_fusion.6
  232.0 2.7 convolution_convert_fusion.10.refs_0_
  234.7 12.8 %attend.3 = (bf16[512,768]{1,0:T(8,128)(2,1)S(1)}, f32[512,768]{1,0:T(8,128)S(1)}) custom-call(s32[1]{0:T(128)} %bitcast.6.core, bf16[512,768]{1,0:T(8,128)(2,1)S(1)} %convolution_convert_fusion.10.refs_0_, bf16[512,128]{1,0:T(8,128)(2,1)S(1)} %get-tuple-element.212.refs_1_, bf16[512,1536]{1,0:T(8,128)(2,1)S(1)} %convolution_convert_fusion.5.refs_2_.refs_3_, ...), custom_call_target="tpu_custom_call" | custom-call | flops 1610612736 | bytes 3145728 | tf_op jit(solution)/shard_map/attend/pallas_call | solution.py:109
  247.6 28.4 %decode_top.1 = (bf16[512,768]{1,0:T(8,128)(2,1)S(1)}, f32[512,768]{1,0:T(8,128)S(1)}, bf16[512,768]{1,0:T(8,128)(2,1)S(1)}, f32[8,768]{1,0:T(8,128)S(1)}, bf16[12288,768]{1,0:T(8,128)(2,1)}) custom-call(f32[512,768]{1,0:T(8,128)} %copy-done.25, bf16[512,768]{1,0:T(8,128)(2,1)S(1)} %get-tuple-element.133.mixed_ref.refs_7_, f32[8,768]{1,0:T(8,128)S(1)} %pad.48.gains, ...), custom_call_target="tpu_custom_call" | custom-call | flops 16911433728 | bytes 18874368 | tf_op jit(solution)/shard_map/decode_top/pallas_call | solution.py:380
  282.6 23.1 %attend_back.2 = (bf16[512,768]{1,0:T(8,128)(2,1)S(1)}, f32[512,768]{1,0:T(8,128)S(1)}, f32[512,768]{1,0:T(8,128)S(1)}, bf16[512,768]{1,0:T(8,128)(2,1)S(1)}, bf16[512,768]{1,0:T(8,128)(2,1)S(1)}) custom-call(s32[1]{0:T(128)} %bitcast.6.core, bf16[512,768]{1,0:T(8,128)(2,1)S(1)} %convolution_convert_fusion.10.refs_0_, ...), custom_call_target="tpu_custom_call" | custom-call | flops 4026531840 | bytes 9437184 | tf_op jit(solution)/shard_map/attend_back/pallas_call | solution.py:214
  305.7 3.4 multiply_reduce_fusion.3
  309.6 2.2 convolution_convert_fusion.9.refs_9_
  311.8 16.2 %attend_back.3 = (bf16[512,768]{1,0:T(8,128)(2,1)S(1)}, f32[512,768]{1,0:T(8,128)S(1)}, f32[512,768]{1,0:T(8,128)S(1)}, bf16[512,768]{1,0:T(8,128)(2,1)S(1)}, bf16[512,768]{1,0:T(8,128)(2,1)S(1)}) custom-call(s32[1]{0:T(128)} %bitcast.6.core, bf16[512,768]{1,0:T(8,128)(2,1)S(1)} %slice.210.refs_0_, bf16[512,128]{1,0:T(8,128)(2,1)S(1)} %get-tuple-element.212.refs_1_, ...), custom_call_target="tpu_custom_call" | custom-call | flops 4026531840 | bytes 9437184 | tf_op jit(solution)/shard_map/attend_back/pallas_call | solution.py:214
  332.2 4.2 fusion.27
  336.4 3.9 fusion
  340.3 1.9 fusion.34
  342.2 2.0 fusion.33
  344.2 3.2 multiply_reduce_fusion.2
  350.2 2.9 fusion.2.rest_0_
  353.1 102.0 %encode_back.1 = (bf16[9216,768]{1,0:T(8,128)(2,1)}, f32[512,768]{1,0:T(8,128)}, f32[8,768]{1,0:T(8,128)}, bf16[512,768]{1,0:T(8,128)(2,1)}, f32[640,768]{1,0:T(...) custom-call(f32[512,768]{1,0:T(8,128)} %subtract_multiply_fusion.gra, ...), custom_call_target="tpu_custom_call" | custom-call | tf_op jit(solution)/shard_map/encode_back/pallas_call | solution.py:1071
  455.2 1.7 pad_maximum_fusion.1
  459.3 2.5 convert_element_type.146
  461.8 1.8 fusion.32
  463.6 2.2 fusion.42
  465.9 6.3 %multiply_reduce_fusion = (f32[768]{0:T(1024)S(1)}, f32[640]{0:T(1024)S(1)}, f32[640,768]{1,0:T(8,128)}, f32[640,768]{1,0:T(8,128)}) fusion(f32[640]{0:T(1024)S(1)} %add_rsqrt_fusion, bf16[96,768]{1,0:T(8,128)(2,1)S(1)} %copy-done.29, bf16[512,768]{1,0:T(8,128)(2,1)S(1)} %copy-done.23, f32[768]{0:T(1024)S(1)} %get-tuple-element.192, ...), kind=kOutput, calls=%fused_computation.38 | convolution fusion | flops 1520269952 | bytes 14707712 | tf_op jit(solution)/shard_map/ne,ed->nd/dot_general | solution.py:1088
  472.3 2.4 fusion.31.q_in
  475.3 5.3 fusion.3.enc_in
  480.6 78.9 %reduce_encoder.1 = (bf16[288,768]{1,0:T(8,128)(2,1)S(1)}, bf16[2,256,768]{2,1,0:T(8,128)(2,1)S(1)}, f32[8,768]{1,0:T(8,128)S(1)}) custom-call(bf16[9216,768]{1,0:T(8,128)(2,1)} %fusion.3.enc_in, bf16[512,768]{1,0:T(8,128)(2,1)S(1)} %fusion.31.q_in, f32[8,768]{1,0:T(8,128)S(1)} %pad.50.gain_in), custom_call_target="tpu_custom_call" | custom-call | tf_op jit(solution)/shard_map/reduce_encoder/pallas_call | solution.py:829
  (180 shorter events, 46.3 us)
Async XLA Ops:
  85.8 23.4 %copy-start.28 = (bf16[96,768]{1,0:T(8,128)(2,1)}, bf16[96,768]{1,0:T(8,128)(2,1)S(1)}, u32[]{:S(2)}) copy-start(bf16[96,768]{1,0:T(8,128)(2,1)S(1)} %convert_element_type.113) | copy-start | bytes 442372
  87.3 4.9 copy-start.35
  91.0 18.3 %copy-start.21 = (bf16[640,1536]{1,0:T(8,128)(2,1)}, bf16[640,1536]{1,0:T(8,128)(2,1)S(1)}, u32[]{:S(2)}) copy-start(bf16[640,1536]{1,0:T(8,128)(2,1)S(1)} %convolution_convert_fusion.4.own_k.own_v) | copy-start | bytes 5898244
  91.0 5.0 copy-start.34
  91.0 21.4 %collective-permute-start = (bf16[640,1536]{1,0:T(8,128)(2,1)S(1)}, bf16[640,1536]{1,0:T(8,128)(2,1)}, u32[]{:S(2)}, u32[]{:S(2)}) collective-permute-start(bf16[640,1536]{1,0:T(8,128)(2,1)S(1)} %convolution_convert_fusion.4.own_k.own_v), channel_id=1, source_target_pairs={{0,4},{4,0},{8,12},{12,8},{16,20},{20,16},{24,28},{28,24},{1,5},{5... | collective-permute-start | bytes 5898248 | tf_op jit(solution)/shard_map/ppermute | solution.py:1102
  92.2 155.4 %copy-start.6 = (f32[8,768]{1,0:T(8,128)}, f32[8,768]{1,0:T(8,128)S(1)}, u32[]{:S(2)}) copy-start(f32[8,768]{1,0:T(8,128)S(1)} %pad.48.gains) | copy-start | bytes 73732
  92.2 17.1 %copy-start.22 = (bf16[512,768]{1,0:T(8,128)(2,1)S(1)}, bf16[512,768]{1,0:T(8,128)(2,1)}, u32[]{:S(2)}) copy-start(bf16[512,768]{1,0:T(8,128)(2,1)} %get-tuple-element.124.x_ref) | copy-start | bytes 2359300
  109.3 3.1 copy-start.2
  112.1 97.9 %copy-start = (bf16[512,768]{1,0:T(8,128)(2,1)}, bf16[512,768]{1,0:T(8,128)(2,1)S(1)}, u32[]{:S(2)}) copy-start(bf16[512,768]{1,0:T(8,128)(2,1)S(1)} %convolution_convert_fusion.11.q_ref) | copy-start | bytes 2359300
  112.3 97.6 %copy-start.1 = (bf16[1280,128]{1,0:T(8,128)(2,1)}, bf16[1280,128]{1,0:T(8,128)(2,1)S(1)}, u32[]{:S(2)}) copy-start(bf16[1280,128]{1,0:T(8,128)(2,1)S(1)} %select_convert_fusion.kaug_ref) | copy-start | bytes 983044
  210.0 4.9 copy-start.3
  210.0 4.9 copy-start.4
  210.0 5.6 copy-start.11
  215.1 4.2 collective-permute-start.1
  218.7 16.1 %copy-start.7 = (bf16[512,1536]{1,0:T(8,128)(2,1)}, bf16[512,1536]{1,0:T(8,128)(2,1)S(1)}, u32[]{:S(2)}) copy-start(bf16[512,1536]{1,0:T(8,128)(2,1)S(1)} %convolution_convert_fusion.5.refs_2_.refs_3_) | copy-start | bytes 4718596
  218.7 16.1 %collective-permute-start.2 = (bf16[512,1536]{1,0:T(8,128)(2,1)S(1)}, bf16[512,1536]{1,0:T(8,128)(2,1)S(1)}, u32[]{:S(2)}, u32[]{:S(2)}) collective-permute-start(bf16[512,1536]{1,0:T(8,128)(2,1)S(1)} %convolution_convert_fusion.5.refs_2_.refs_3_), channel_id=1, source_target_pairs={{0,4},{4,0},{8,12},{12,8},{16,20},{20,16},{24,28},{28,24},{1,5},{5... | collective-permute-start | bytes 4718600 | tf_op jit(solution)/shard_map/ppermute | solution.py:1102
  229.2 2.8 copy-start.17
  229.3 2.8 copy-start.36
  232.0 2.7 copy-start.25
  234.7 12.9 %copy-start.9 = (bf16[512,1536]{1,0:T(8,128)(2,1)}, bf16[512,1536]{1,0:T(8,128)(2,1)S(1)}, u32[]{:S(2)}) copy-start(bf16[512,1536]{1,0:T(8,128)(2,1)S(1)} %collective-permute-done.2.refs_4_.refs_5_) | copy-start | bytes 4718596
  247.6 28.4 %copy-start.19 = (f32[512,768]{1,0:T(8,128)}, f32[512,768]{1,0:T(8,128)S(1)}, u32[]{:S(2)}) copy-start(f32[512,768]{1,0:T(8,128)S(1)} %get-tuple-element.134.refs_8_) | copy-start | bytes 4718596
  276.9 28.7 %copy-start.5 = (bf16[512,768]{1,0:T(8,128)(2,1)}, bf16[512,768]{1,0:T(8,128)(2,1)S(1)}, u32[]{:S(2)}) copy-start(bf16[512,768]{1,0:T(8,128)(2,1)S(1)} %get-tuple-element.154.rest_1_) | copy-start | bytes 2359300
  282.6 23.1 %copy-start.26 = (f32[512,768]{1,0:T(8,128)S(1)}, f32[512,768]{1,0:T(8,128)}, u32[]{:S(2)}) copy-start(f32[512,768]{1,0:T(8,128)} %copy-done.25) | copy-start | bytes 4718596
  305.7 3.4 copy-start.13
  328.1 3.8 collective-permute-start.4
  329.7 14.5 %collective-permute-start.3 = (bf16[512,1536]{1,0:T(8,128)(2,1)S(1)}, bf16[512,1536]{1,0:T(8,128)(2,1)S(1)}, u32[]{:S(2)}, u32[]{:S(2)}) collective-permute-start(bf16[512,1536]{1,0:T(8,128)(2,1)S(1)} %pad_maximum_fusion.2), channel_id=1, source_target_pairs={{0,4},{4,0},{8,12},{12,8},{16,20},{20,16},{24,28},{28,24},{1,5},{5... | collective-permute-start | bytes 4718600 | tf_op jit(solution)/shard_map/ppermute | solution.py:1102
  455.2 2.6 copy-start.33
  456.9 8.9 %collective-permute-start.5 = (bf16[640,1536]{1,0:T(8,128)(2,1)S(1)}, bf16[640,1536]{1,0:T(8,128)(2,1)}, u32[]{:S(2)}, u32[]{:S(2)}) collective-permute-start(bf16[640,1536]{1,0:T(8,128)(2,1)S(1)} %pad_maximum_fusion.1), channel_id=1, source_target_pairs={{0,4},{4,0},{8,12},{12,8},{16,20},{20,16},{24,28},{28,24},{1,5},{5... | collective-permute-start | bytes 5898248 | tf_op jit(solution)/shard_map/ppermute | solution.py:1102
  459.3 2.5 copy-start.44
  461.8 4.1 copy-start.42
  465.9 6.4 %copy-start.27 = (f32[512,768]{1,0:T(8,128)S(1)}, f32[512,768]{1,0:T(8,128)}, u32[]{:S(2)}) copy-start(f32[512,768]{1,0:T(8,128)} %get-tuple-element.162) | copy-start | bytes 4718596
  472.3 3.1 copy-start.43
  (19 other events, 36.8 us)

commit v5 on v4

--- a/solution.py
+++ b/solution.py
@@ -121,7 +121,7 @@
             scratch_shapes=[pltpu.VMEM((t // QB, 2 * nk, 2 * QB), jnp.float32)],
         ),
         out_shape=[jax.ShapeDtypeStruct((t, D), jnp.bfloat16), jax.ShapeDtypeStruct((t, D), jnp.float32)],
-        compiler_params=pltpu.CompilerParams(vmem_limit_bytes=40 * 1024 * 1024),
+        compiler_params=pltpu.CompilerParams(vmem_limit_bytes=32 * 1024 * 1024),
         cost_estimate=pl.CostEstimate(flops=4 * t * 2 * nk * D, bytes_accessed=8 * nk * D, transcendentals=t * 2 * nk * H),
         name="attend",
     )(core.reshape(1), q, qaug, own_kv, own_kv, oth_kv, oth_kv, kaug)
@@ -233,7 +233,7 @@
             jax.ShapeDtypeStruct((nk, D), jnp.bfloat16),
             jax.ShapeDtypeStruct((nk, D), jnp.bfloat16),
         ],
-        compiler_params=pltpu.CompilerParams(vmem_limit_bytes=40 * 1024 * 1024),
+        compiler_params=pltpu.CompilerParams(vmem_limit_bytes=32 * 1024 * 1024),
         cost_estimate=pl.CostEstimate(flops=10 * t * 2 * nk * D, bytes_accessed=24 * nk * D, transcendentals=t * 2 * nk * H),
         name="attend_back",
     )(core.reshape(1), q, qaug, own_kv, own_kv, oth_kv, oth_kv, kaug, mixed, lse, grad)
@@ -252,6 +252,7 @@
 
 epsilon = 1e-06
 CHUNK = 512
+TOP_CHUNK = 1024
 
 
 def dot_nt(left, right):
@@ -291,8 +292,9 @@
     act, slope = gelu_pair(dot_nt(normed, w1))
     act = act.astype(jnp.bfloat16)
     grad_pre = (dot_nt(grad_b, w2) * slope).astype(jnp.bfloat16)
-    dw[0] = dot_tn(grad_pre, normed).astype(jnp.bfloat16)
-    dw[1] = dot_tn(act, grad_b).astype(jnp.bfloat16)
+    size = w1.shape[0]
+    dw[:size, :] = dot_tn(grad_pre, normed).astype(jnp.bfloat16)
+    dw[size:, :] = dot_tn(act, grad_b).astype(jnp.bfloat16)
     part = dot_nn(grad_pre, w1)
 
     @pl.when(first)
@@ -312,8 +314,10 @@
 
     def copy(self, i, which):
         slot = lax.rem(i, 2)
-        rows = pl.ds(pl.multiple_of(self.places[which] + i * CHUNK, CHUNK), CHUNK)
-        return pltpu.make_async_copy(self.slots.at[slot, which], self.whole.at[rows], self.sems.at[slot, which])
+        size = self.slots.shape[1] // 2
+        rows = pl.ds(pl.multiple_of(self.places[which] + i * size, size), size)
+        source = self.slots.at[slot, pl.ds(which * size, size)]
+        return pltpu.make_async_copy(source, self.whole.at[rows], self.sems.at[slot, which])
 
     def start(self, i):
         for which in (0, 1):
@@ -356,7 +360,7 @@
     def _():
         acc_ref[...] += more
 
-    @pl.when(i == FF // CHUNK - 1)
+    @pl.when(i == FF // TOP_CHUNK - 1)
     def _():
         decoded_ref[...] = acc_ref[...].astype(jnp.bfloat16)
         grad_x, dgain = norm_back(d2_ref[...], gains[4:5, :], total_ref[...])
@@ -375,7 +379,7 @@
 
 def decode_top(d1, mixed, gains, grad_top, dec_w):
     t = d1.shape[0]
-    n = FF // CHUNK
+    n = FF // TOP_CHUNK
     tok = whole_spec((t, D))
     return pl.pallas_call(
         decode_top_kernel,
@@ -383,8 +387,8 @@
         in_specs=[
             tok, tok, whole_spec(gains.shape), tok,
             pl.BlockSpec((D, D), lambda i: (7, 0)),
-            pl.BlockSpec((CHUNK, D), lambda i: (8 * D // CHUNK + i, 0)),
-            pl.BlockSpec((CHUNK, D), lambda i: (8 * D // CHUNK + n + i, 0)),
+            pl.BlockSpec((TOP_CHUNK, D), lambda i: (8 * D // TOP_CHUNK + i, 0)),
+            pl.BlockSpec((TOP_CHUNK, D), lambda i: (8 * D // TOP_CHUNK + n + i, 0)),
         ],
         out_specs=[tok, tok, tok, whole_spec((8, D)), pl.BlockSpec(memory_space=pl.ANY)],
         out_shape=[
@@ -399,15 +403,91 @@
             pltpu.VMEM((t, D), jnp.bfloat16),
             pltpu.VMEM((t, D), jnp.float32),
             pltpu.VMEM((t, D), jnp.float32),
-            pltpu.VMEM((2, 2, CHUNK, D), jnp.bfloat16),
+            pltpu.VMEM((2, 2 * TOP_CHUNK, D), jnp.bfloat16),
             pltpu.VMEM((D, D), jnp.bfloat16),
             pltpu.SemaphoreType.DMA((2, 2)),
             pltpu.SemaphoreType.DMA,
         ],
-        compiler_params=pltpu.CompilerParams(vmem_limit_bytes=48 * 1024 * 1024),
+        compiler_params=pltpu.CompilerParams(vmem_limit_bytes=36 * 1024 * 1024),
         cost_estimate=pl.CostEstimate(flops=14 * t * FF * D, bytes_accessed=8 * FF * D, transcendentals=t * FF),
         name="decode_top",
     )(d1, mixed, gains, grad_top, dec_w, dec_w, dec_w)
+
+
+def decode_dense_kernel(
+    dqs_ref, dks_ref, dvs_ref, kvs_got, dqc_ref, dkc_ref, dvc_ref, kvc_got, na_ref, nc_ref, ne_ref, os_ref, one_ref,
+    x_ref, h2_ref, gains, w_ref, unused, dw_ref, answers_ref, encoded_ref, dgain2_ref, dgain5_ref, g_ref, sum_ref,
+):
+    i = pl.program_id(0)
+
+    def weight(n, wide, narrow):
+        @pl.when(i == n)
+        def _():
+            dw_ref[...] = dot_tn(wide(), narrow[...]).astype(jnp.bfloat16)
+
+    def total(own, got, which, slot):
+        g_ref[slot] = (own[...] + got[:, which * D : (which + 1) * D].astype(jnp.float32)).astype(jnp.bfloat16)
+        return g_ref[slot]
+
+    def gather_back(n, begin, grads, finish):
+        @pl.when(i == n)
+        def _():
+            part = dot_nn(grads(), w_ref[...])
+            if begin:
+                sum_ref[...] = part
+            else:
+                sum_ref[...] += part
+            if finish is not None:
+                finish()
+
+    def encoded_done():
+        grad, dgain = norm_back(h2_ref[...], gains[5:6, :], sum_ref[...])
+        encoded_ref[...] = grad
+        dgain5_ref[...] = jnp.broadcast_to(dgain, dgain5_ref.shape)
+
+    def answers_done():
+        grad, dgain = norm_back(x_ref[...].astype(jnp.float32), gains[2:3, :], sum_ref[...])
+        answers_ref[...] = (one_ref[...] + grad).astype(jnp.bfloat16)
+        dgain2_ref[...] = jnp.broadcast_to(dgain, dgain2_ref.shape)
+
+    weight(0, lambda: total(dkc_ref, kvc_got, 0, 0), ne_ref)
+    gather_back(0, True, lambda: g_ref[0], None)
+    weight(1, lambda: total(dvc_ref, kvc_got, 1, 1), ne_ref)
+    gather_back(1, False, lambda: g_ref[1], encoded_done)
+    weight(2, lambda: dqc_ref[...], nc_ref)
+
+    @pl.when(i == 3)
+    def _():
+        dw_ref[...] = dot_tn(os_ref[...], one_ref[...].astype(jnp.bfloat16)).astype(jnp.bfloat16)
+
+    weight(4, lambda: dqs_ref[...], na_ref)
+    gather_back(4, True, lambda: dqs_ref[...], None)
+    weight(5, lambda: total(dks_ref, kvs_got, 0, 0), na_ref)
+    gather_back(5, False, lambda: g_ref[0], None)
+    weight(6, lambda: total(dvs_ref, kvs_got, 1, 1), na_ref)
+    gather_back(6, False, lambda: g_ref[1], answers_done)
+
+
+def decode_dense(dqs, dks, dvs, kvs_got, dqc, dkc, dvc, kvc_got, na, nc, ne, os, one, x, h2, gains, dec_w, dec_g):
+    t = x.shape[0]
+    block = lambda i: jnp.where(i < 2, i + 5, jnp.where(i == 2, 4, jnp.where(i == 3, 3, i - 4)))
+    tok, wide = whole_spec((t, D)), whole_spec((t, 2 * D))
+    f32, bf = jnp.float32, jnp.bfloat16
+    dims = lambda kind, n=t: jax.ShapeDtypeStruct((n, D), kind)
+    return pl.pallas_call(
+        decode_dense_kernel,
+        grid=(7,),
+        in_specs=[tok, tok, tok, wide, tok, tok, tok, wide] + [tok] * 7 + [
+            whole_spec(gains.shape), pl.BlockSpec((D, D), lambda i: (block(i), 0)), pl.BlockSpec(memory_space=pl.ANY),
+        ],
+        out_specs=[pl.BlockSpec((D, D), lambda i: (block(i), 0)), tok, tok, whole_spec((8, D)), whole_spec((8, D))],
+        out_shape=[dims(bf, dec_g.shape[0]), dims(bf), dims(f32), dims(f32, 8), dims(f32, 8)],
+        scratch_shapes=[pltpu.VMEM((2, t, D), bf), pltpu.VMEM((t, D), f32)],
+        input_output_aliases={17: 0},
+        compiler_params=pltpu.CompilerParams(vmem_limit_bytes=40 * 1024 * 1024),
+        cost_estimate=pl.CostEstimate(flops=24 * t * D * D, bytes_accessed=50 * t * D, transcendentals=0),
+        name="decode_dense",
+    )(dqs, dks, dvs, kvs_got, dqc, dkc, dvc, kvc_got, na, nc, ne, os, one, x, h2, gains, dec_w, dec_g)
 
 
 MESH = pl.DeviceIdType.MESH
@@ -616,26 +696,28 @@
 
 
 class NumbersIn:
-    def __init__(self, mail, seg_in, seg_out, ids_in, ids_out, sems):
-        self.mail, self.seg_in, self.seg_out, self.ids_in, self.ids_out = mail, seg_in, seg_out, ids_in, ids_out
+    def __init__(self, mail, seg_ins, seg_outs, ent_in, ent_out, sems):
+        self.mail, self.seg_ins, self.seg_outs, self.ent_in, self.ent_out = mail, seg_ins, seg_outs, ent_in, ent_out
         self.i_s, self.i_r, self.i_l, self.n_s, self.n_r = sems
 
     def start(self):
         r, m, core, near = self.mail.pos[:4]
-        self.mail.send(lambda: remote(self.seg_in.at[lax.rem(m, 2)], self.seg_out, self.n_s, self.n_r, (near, m)))
+        for n, (src, dst) in enumerate(zip(self.seg_ins, self.seg_outs)):
+            self.mail.send(lambda n=n, src=src, dst=dst: remote(src, dst, self.n_s.at[n], self.n_r.at[n], (near, m)))
         for i in (0, 1):
-            make = lambda i=i, e=0, to=r: remote(self.ids_in.at[i], self.ids_out.at[m], self.i_s.at[i, e], self.i_r.at[m], (to, 2 * core + i))
-            self.mail.send(functools.partial(make, e=1, to=near))
+            make = lambda i=i, e=0, to=r, half=core: remote(self.ent_in.at[i, half], self.ent_out.at[m], self.i_s.at[i, e], self.i_r.at[m], (to, 2 * core + i))
+            self.mail.send(functools.partial(make, e=1, to=near, half=1 - core))
             here = lambda i=i: 2 * core + i == m
-            keep = lambda i=i: pltpu.make_async_copy(self.ids_in.at[i], self.ids_out.at[m], self.i_l)
+            keep = lambda i=i: pltpu.make_async_copy(self.ent_in.at[i, core], self.ent_out.at[m], self.i_l)
             self.mail.send_or_keep(here, make, keep)
 
     def finish(self):
         r, m, core, near = self.mail.pos[:4]
-        self.mail.arrived(self.seg_out, self.n_r)
+        for n, dst in enumerate(self.seg_outs):
+            self.mail.arrived(dst, self.n_r.at[n])
         for mem in range(4):
             here = jnp.logical_and(lax.div(m, 2) == core, m == mem)
-            place = self.ids_out.at[mem]
+            place = self.ent_out.at[mem]
             pl.when(here)(lambda: pltpu.make_async_copy(place, place, self.i_l).wait())
             pl.when(jnp.logical_not(here))(lambda: self.mail.arrived(place, self.i_r.at[mem]))
 
@@ -676,35 +758,34 @@
 
     def start(self):
         r, m, core, near, first, second, both, others = self.mail.pos
-        for j in range(4):
-            for k in (3, 2, 1, 0):
-                self.mail.send(lambda j=j, k=k: remote(self.at(others[k], j), self.rc.at[j, k], self.c_s.at[j, k], self.c_r.at[j, k], (near, m)))
-                self.load(j, k).start()
-
-    def from_core(self, j):
+        order = [(0, 3), (1, 3), (0, 1), (0, 2), (2, 3), (1, 1), (0, 0), (1, 2), (3, 3), (2, 1), (1, 0), (2, 2), (3, 1), (2, 0), (3, 2), (3, 0)]
+        for j, k in order:
+            self.mail.send(lambda j=j, k=k: remote(self.at(others[k], j), self.rc.at[j, k], self.c_s.at[j, k], self.c_r.at[j, k], (near, m)))
+            self.load(j, k).start()
+
+    def from_core(self, j, k):
         second, m = self.mail.pos[5], self.mail.pos[1]
-        for k in (3, 2, 1, 0):
-            self.load(j, k).wait()
-            self.mail.arrived(self.rc.at[j, k], self.c_r.at[j, k])
-            add_to(self.held.at[j, k], self.rc.at[j, k])
-            if k >= 2:
-                self.mail.send(lambda k=k: remote(self.held.at[j, k], self.rb.at[j, k - 2], self.b_s.at[j, k - 2], self.b_r.at[j, k - 2], (second, m)))
-
-    def from_second(self, j):
+        self.load(j, k).wait()
+        self.mail.arrived(self.rc.at[j, k], self.c_r.at[j, k])
+        add_to(self.held.at[j, k], self.rc.at[j, k])
+        if k >= 2:
+            self.mail.send(lambda: remote(self.held.at[j, k], self.rb.at[j, k - 2], self.b_s.at[j, k - 2], self.b_r.at[j, k - 2], (second, m)))
+
+    def to_first(self, j):
         first, m = self.mail.pos[4], self.mail.pos[1]
-        for k in (1, 0):
-            self.mail.arrived(self.rb.at[j, k], self.b_r.at[j, k])
-            add_to(self.held.at[j, k], self.rb.at[j, k])
-            if k == 1:
-                self.mail.send(lambda: remote(self.held.at[j, 1], self.ra.at[j], self.a_s.at[j], self.a_r.at[j], (first, m)))
+        self.mail.arrived(self.rb.at[j, 1], self.b_r.at[j, 1])
+        add_to(self.held.at[j, 1], self.rb.at[j, 1])
+        self.mail.send(lambda: remote(self.held.at[j, 1], self.ra.at[j], self.a_s.at[j], self.a_r.at[j], (first, m)))
 
     def result(self):
         return pltpu.make_async_copy(self.held.at[3, 0], self.out, self.o.at[0])
 
-    def from_first(self, j):
+    def ring(self, j):
         r, m = self.mail.pos[:2]
         self.mail.arrived(self.ra.at[j], self.a_r.at[j])
         add_to(self.held.at[j, 0], self.ra.at[j])
+        self.mail.arrived(self.rb.at[j, 0], self.b_r.at[j, 0])
+        add_to(self.held.at[j, 0], self.rb.at[j, 0])
         if j > 0:
             self.mail.arrived(self.rz.at[j - 1], self.z_r.at[j - 1])
             add_to(self.held.at[j, 0], self.rz.at[j - 1])
@@ -718,12 +799,24 @@
 
 
 def reduce_order(reduce):
-    steps = [
-        (reduce.from_core, 0), (reduce.from_core, 1), (reduce.from_second, 0), (reduce.from_core, 2),
-        (reduce.from_second, 1), (reduce.from_first, 0), (reduce.from_core, 3), (reduce.from_second, 2),
-        (reduce.from_first, 1), (reduce.from_second, 3), (reduce.from_first, 2), (reduce.from_first, 3),
+    core, first, ring = reduce.from_core, reduce.to_first, reduce.ring
+    groups = [
+        [(core, 0, 3), (core, 1, 3), (core, 0, 1)],
+        [(first, 0), (core, 0, 2), (core, 2, 3), (core, 1, 1), (core, 0, 0)],
+        [(first, 1), (core, 1, 2), (core, 3, 3), (core, 2, 1), (core, 1, 0)],
+        [(ring, 0)],
+        [(first, 2), (core, 2, 2), (core, 3, 1), (core, 2, 0)],
+        [(ring, 1)],
+        [(first, 3), (core, 3, 2), (core, 3, 0)],
+        [(ring, 2)],
+        [(ring, 3)],
     ]
-    return [functools.partial(*step) for step in steps]
+
+    def run(group):
+        for step in group:
+            step[0](*step[1:])
+
+    return [functools.partial(run, group) for group in groups]
 
 
 class GainSums:
@@ -762,17 +855,22 @@
     return jax.ShapeDtypeStruct(shape, kind)
 
 
-def gather_encoder_kernel(enc_in, q_in, seg_in, ids_in, enc_out, q_out, seg_out, ids_out, *sems):
+def gather_encoder_kernel(
+    enc_in, q_in, qs_in, as_in, al_in, ent_in, dec_ref, enc_out, q_out, qs_out, as_out, al_out, ent_out, dect_ref, *sems
+):
     mail = Mail(position())
     gather = Gather(mail, (enc_in,), (enc_out,), sems[:9])
     tokens = TokensIn(mail, ((q_in, q_out),), sems[9:12])
-    numbers = NumbersIn(mail, seg_in, seg_out, ids_in, ids_out, sems[12:])
+    numbers = NumbersIn(mail, (qs_in, as_in, al_in), (qs_out, as_out, al_out), ent_in, ent_out, sems[12:])
     greet(mail.pos)
     numbers.start()
     steps = gather_order(gather)
     steps[0]()
+    dect_ref[...] = dec_ref[...].T
+    for step in steps[1:4]:
+        step()
     tokens.start(0)
-    for step in steps[1:]:
+    for step in steps[4:]:
         step()
     gather.finish()
     tokens.finish()
@@ -780,215 +878,263 @@
     mail.finish()
 
 
-def gather_encoder(enc_t, q, seg, ids):
+def gather_encoder(enc_t, q, q_seg, a_seg, alive, entries, dec_params):
+    vmem = pl.BlockSpec(memory_space=pltpu.VMEM)
     return pl.pallas_call(
         gather_encoder_kernel,
-        in_specs=[ANY] * 4,
-        out_specs=[ANY] * 4,
+        in_specs=[ANY] * 6 + [vmem],
+        out_specs=[ANY] * 6 + [vmem],
         out_shape=[
             shaped((32 * enc_t.shape[0], D)),
             shaped((2 * q.shape[1], D)),
-            shaped(seg.shape[1:], jnp.int32),
-            shaped((4,) + ids.shape[1:], jnp.int32),
+            shaped(q_seg.shape, jnp.int32),
+            shaped(a_seg.shape, jnp.int32),
+            shaped(alive.shape, jnp.int32),
+            shaped((4,) + entries.shape[2:]),
+            shaped((dec_params.shape[1], D)),
         ],
-        scratch_shapes=gather_sems(1) + token_sems(1) + [dma(2, 2), dma(4), dma(), dma(), dma()],
-        compiler_params=pltpu.CompilerParams(collective_id=0, has_side_effects=True),
+        scratch_shapes=gather_sems(1) + token_sems(1) + [dma(2, 2), dma(4), dma(), dma(3), dma(3)],
+        compiler_params=pltpu.CompilerParams(collective_id=0, has_side_effects=True, vmem_limit_bytes=16 * 1024 * 1024),
         name="gather_encoder",
-    )(enc_t, q, seg, ids)
-
-
-def reduce_encoder_kernel(enc_in, q_in, gain_in, enc_out, q_out, gain_out, *rest):
+    )(enc_t, q, q_seg, a_seg, alive, entries, dec_params)
+
+
+def reduce_encoder_kernel(
+    enc_in, x_ref, pre_ref, dq_ref, dkv_ref, w_ref, grad_h_ref, gains, gain_in,
+    enc_out, q_out, gain_out, gq_ref, own_ref, *rest,
+):
     mail = Mail(position())
     reduce = Reduce(mail, enc_in, enc_out, rest[:5], rest[5:15])
-    tokens = TokensOut(mail, ((q_in, q_out),), rest[15:18])
-    gains = GainSums(mail, gain_in, gain_out, *rest[18:21], rest[21:])
+    tokens = TokensOut(mail, ((gq_ref, q_out),), rest[15:18])
+    sums = GainSums(mail, own_ref, gain_out, *rest[18:21], rest[21:])
     greet(mail.pos)
-    gains.hop(0)
     reduce.start()
     steps = reduce_order(reduce)
     steps[0]()
-    gains.hop(1)
+    steps[1]()
+    t = x_ref.shape[0]
+    back = dot_nn(dkv_ref[...], w_ref[D : 3 * D, :])
+    both = back[:t] + dot_nn(dq_ref[...], w_ref[:D, :])
+    grad_x, dgain = norm_back(x_ref[...].astype(jnp.float32), gains[0:1, :], both)
+    gq_ref[...] = (grad_h_ref[...] + grad_x).astype(jnp.bfloat16)
     tokens.start(0)
-    steps[1]()
-    gains.hop(2)
-    for step in steps[2:6]:
-        step()
-    gains.hop(3)
-    for step in steps[6:]:
-        step()
+    unused, more = norm_back(pre_ref[...].astype(jnp.float32), gains[0:1, :], back[t:])
+    own_ref[...] = gain_in[...]
+    own_ref[0:1, :] = dgain + more
+    sums.hop(0)
+    steps[2]()
+    sums.hop(1)
+    steps[3]()
+    steps[4]()
+    sums.hop(2)
+    steps[5]()
+    steps[6]()
+    sums.hop(3)
+    steps[7]()
+    steps[8]()
     reduce.finish()
     tokens.finish()
-    gains.finish()
+    sums.finish()
     mail.finish()
 
 
-def reduce_encoder(enc_g, q, gains):
+def reduce_encoder(enc_g, x, pre, dq, dkv, enc_w, grad_h, gains, gain_terms):
     vmem = pl.BlockSpec(memory_space=pltpu.VMEM)
     size = enc_g.shape[0] // 32
-    small = lambda n: pltpu.VMEM((n,) + gains.shape, jnp.float32)
+    t = x.shape[0]
+    small = lambda n: pltpu.VMEM((n, 8, D), jnp.float32)
     return pl.pallas_call(
         reduce_encoder_kernel,
-        in_specs=[ANY, ANY, vmem],
-        out_specs=[ANY, ANY, vmem],
-        out_shape=[shaped((size, D)), shaped((2, q.shape[0] // 2, D)), shaped(gains.shape, jnp.float32)],
-        scratch_shapes=reduce_buffers(size) + reduce_sems() + token_sems(1) + [small(3), small(3), small(4)]
+        grid=(1,),
+        in_specs=[ANY, whole_spec(x.shape), whole_spec(pre.shape), whole_spec(dq.shape), whole_spec(dkv.shape),
+                  pl.BlockSpec((3 * D, D), lambda i: (0, 0)), whole_spec(x.shape), whole_spec(gains.shape), whole_spec((8, D))],
+        out_specs=[ANY, ANY, whole_spec((8, D))],
+        out_shape=[shaped((size, D)), shaped((2, t // 2, D)), shaped((8, D), jnp.float32)],
+        scratch_shapes=[pltpu.VMEM(x.shape, jnp.bfloat16), pltpu.VMEM((8, D), jnp.float32)]
+        + reduce_buffers(size) + reduce_sems() + token_sems(1) + [small(3), small(3), small(4)]
         + [dma(3), dma(3), dma(3), dma(4)],
-        compiler_params=pltpu.CompilerParams(collective_id=3, has_side_effects=True, vmem_limit_bytes=40 * 1024 * 1024),
+        compiler_params=pltpu.CompilerParams(collective_id=3, has_side_effects=True, vmem_limit_bytes=52 * 1024 * 1024),
         name="reduce_encoder",
-    )(enc_g, q, gains)
+    )(enc_g, x, pre, dq, dkv, enc_w, grad_h, gains, gain_terms)
+
+
+def fetch_kernel(ids, table, out, sems):
+    n = out.shape[0]
+    copies = [pltpu.make_async_copy(table.at[ids[i]], out.at[i], sems.at[i]) for i in range(n)]
+    for copy in copies:
+        copy.start()
+    for copy in copies:
+        copy.wait()
+
+
+def fetch(ids, table):
+    n = ids.shape[0]
+    return pl.pallas_call(
+        fetch_kernel,
+        grid_spec=pltpu.PrefetchScalarGridSpec(
+            num_scalar_prefetch=1, grid=(1,), in_specs=[ANY], out_specs=ANY,
+            scratch_shapes=[dma(n)],
+        ),
+        out_shape=shaped((n,) + table.shape[1:], table.dtype),
+        name="fetch",
+    )(ids, table)
 
 
 PAIRS = H // 2
 CHUNKS = FF // CHUNK
 
 
+def once(shape):
+    return pl.BlockSpec(shape, lambda i: (0,) * len(shape), pipeline_mode=pl.Buffered(1))
+
+
+def column(refs, first, i):
+    return [ref.at[:, pl.ds(pl.multiple_of(first + i * 128, 128), 128)] for ref in refs]
+
+
 def encode_kernel(
-    fast, own_len, extra,
-    q_ref, qaug_ref, own_k, own_v, oth_k, oth_v, kaug_ref, x_ref, gains, wo_ref, w1_ref, w2_ref, *rest,
+    x_ref, pre_ref, qaug_ref, kaug_ref, gains, wqkv_ref, wo_ref, w1_ref, w2_ref, dec_in, a_in, g_ref,
+    nq_ref, q_ref, o_ref, lse_ref, h1_ref, nf1_ref, h2_ref, ne_ref, kvo_out, kvt_out, dec_out, a_out, g_out,
+    kvo_ref, kvt_ref, s_ref, ff_ref, g_in, kv_sems, *sems,
 ):
     i = pl.program_id(0)
-    if fast:
-        dec_in, a_in, g_in = rest[:3]
-        o_ref, lse_ref, h1_ref, nf1_ref, h2_ref, ne_ref, dec_out, a_out, g_out = rest[3:12]
-        s_ref, ff_ref = rest[12:14]
-        sems = rest[14:]
-        mail = Mail(position())
-        gather = Gather(mail, (dec_in,), (dec_out,), sems[:9])
-        tokens = TokensIn(mail, ((a_in, a_out), (g_in, g_out)), sems[9:12])
-        steps = gather_order(gather)
-        places = {2: (1, 2), 4: (3, 4), 5: (5,), 6: (6, 7), 7: (8,), 8: (9,), 10: (10,)}
-
-        @pl.when(i == 0)
-        def _():
-            greet(mail.pos)
-            steps[0]()
-
-        for at, which in places.items():
-
-            @pl.when(i == at)
-            def _(at=at, which=which):
-                for n in which:
-                    steps[n]()
-                if at == 6:
+    t, extra = x_ref.shape[0], pre_ref.shape[0]
+    mail = Mail(position())
+    gather = Gather(mail, (dec_in,), (dec_out,), sems[:9])
+    tokens = TokensIn(mail, ((a_in, a_out), (g_in, g_out)), sems[9:12])
+    steps = gather_order(gather)
+    places = {4: (1, 2), 9: (3, 4), 11: (5,)}
+    near, m = mail.pos[3], mail.pos[1]
+    keep_own = lambda: pltpu.make_async_copy(kvo_ref, kvo_out, kv_sems.at[2])
+    keep_other = lambda: pltpu.make_async_copy(kvt_ref, kvt_out, kv_sems.at[3])
+
+    @pl.when(i == 0)
+    def _():
+        greet(mail.pos)
+        steps[0]()
+        nq_ref[:t, :] = rms_norm(x_ref[...].astype(jnp.float32), gains[0:1, :]).astype(jnp.bfloat16)
+        nq_ref[t:, :] = rms_norm(pre_ref[...].astype(jnp.float32), gains[0:1, :]).astype(jnp.bfloat16)
+        for b in (1, 2):
+            kvo_ref[:, (b - 1) * D : b * D] = dot_nt(nq_ref[...], wqkv_ref[b * D : (b + 1) * D, :]).astype(jnp.bfloat16)
+        mail.send(lambda: remote(kvo_ref, kvt_ref, kv_sems.at[0], kv_sems.at[1], (near, m)))
+        keep_own().start()
+        q_ref[...] = dot_nt(nq_ref[:t, :], wqkv_ref[:D, :]).astype(jnp.bfloat16)
+
+    @pl.when(i == 1)
+    def _():
+        g_in[...] = g_ref[...].astype(jnp.bfloat16)
+        mail.arrived(kvt_ref, kv_sems.at[1])
+        keep_other().start()
+
+    for at, which in places.items():
+
+        @pl.when(i == at)
+        def _(which=which):
+            for n in which:
+                steps[n]()
+                if n == 3:
                     tokens.start(0)
                     tokens.start(1)
-    else:
-        o_ref, lse_ref, h1_ref, nf1_ref, h2_ref, ne_ref = rest[:6]
-        s_ref, ff_ref = rest[6:]
-
-    @pl.when(i < PAIRS)
-    def _():
-        cols = pl.ds(pl.multiple_of(i * 128, 128), 128)
+
+    @pl.when((i >= 1) & (i <= PAIRS))
+    def _():
+        pair = jnp.maximum(i - 1, 0)
+        own_k, oth_k = column((kvo_ref, kvt_ref), 0, pair)
+        own_v, oth_v = column((kvo_ref, kvt_ref), D, pair)
+        q, o, lse = column((q_ref, o_ref, lse_ref), 0, pair)
         attend_pair(
-            False, own_len, extra, chunk_sets(False, own_len, extra)[0],
-            q_ref, qaug_ref, own_k, own_v, oth_k, oth_v, kaug_ref, o_ref.at[:, cols], lse_ref, s_ref,
+            False, t, extra, chunk_sets(False, t, extra)[0], q, qaug_ref, own_k, own_v, oth_k, oth_v, kaug_ref, o, lse, s_ref
         )
 
-    @pl.when(i == PAIRS)
+    @pl.when(i == PAIRS + 1)
     def _():
         h1_ref[...] = x_ref[...].astype(jnp.float32) + dot_nn(o_ref[...], wo_ref[...])
         nf1_ref[...] = rms_norm(h1_ref[...], gains[1:2, :]).astype(jnp.bfloat16)
         ff_ref[...] = h1_ref[...]
 
-    @pl.when(i >= PAIRS)
+    @pl.when(i > PAIRS)
     def _():
         act = gelu_pair(dot_nt(nf1_ref[...], w1_ref[...]))[0].astype(jnp.bfloat16)
         ff_ref[...] += dot_nn(act, w2_ref[...])
 
-    @pl.when(i == PAIRS + CHUNKS - 1)
+    @pl.when(i == PAIRS + CHUNKS)
     def _():
         h2_ref[...] = ff_ref[...]
         ne_ref[...] = rms_norm(ff_ref[...], gains[5:6, :]).astype(jnp.bfloat16)
-        if fast:
-            steps[11]()
-            gather.finish()
-            tokens.finish()
-            mail.finish()
-
-
-def encode(fast, q, qaug, own_kv, oth_kv, kaug, x, gains, enc_w, dec_t, a, g):
-    t = q.shape[0]
-    nk = own_kv.shape[0]
-    pair = lambda i: jnp.minimum(i, PAIRS - 1)
-    chunk = lambda i: jnp.maximum(i - PAIRS, 0)
-    col = lambda first: pl.BlockSpec((nk, 128), lambda i: (0, first + pair(i)))
+        for n in range(6, 12):
+            steps[n]()
+        gather.finish()
+        tokens.finish()
+        keep_own().wait()
+        keep_other().wait()
+        mail.finish()
+
+
+def encode(x, pre, qaug, kaug, gains, enc_w, dec_t, a, g):
+    t, extra = x.shape[0], pre.shape[0]
+    nk = t + extra
+    chunk = lambda i: jnp.maximum(i - PAIRS - 1, 0)
     tok = whole_spec((t, D))
-    dims = lambda kind: jax.ShapeDtypeStruct((t, D), kind)
-    in_specs = [
-        pl.BlockSpec((t, 128), lambda i: (0, pair(i))), whole_spec((t, 128)),
-        col(0), col(PAIRS), col(0), col(PAIRS), whole_spec((2 * nk, 128)), tok, whole_spec(gains.shape),
-        pl.BlockSpec((D, D), lambda i: (3, 0)),
-        pl.BlockSpec((CHUNK, D), lambda i: (4 * D // CHUNK + chunk(i), 0)),
-        pl.BlockSpec((CHUNK, D), lambda i: (4 * D // CHUNK + CHUNKS + chunk(i), 0)),
-    ]
-    args = [q, qaug, own_kv, own_kv, oth_kv, oth_kv, kaug, x, gains, enc_w, enc_w, enc_w]
-    out_specs = [tok, pl.BlockSpec((t, 128), lambda i: (0, pair(i))), tok, tok, tok, tok]
-    out_shape = [dims(jnp.bfloat16), dims(jnp.float32), dims(jnp.float32), dims(jnp.bfloat16), dims(jnp.float32), dims(jnp.bfloat16)]
-    scratch = [
-        pltpu.VMEM((t // QB, 2 * nk, 2 * QB), jnp.float32), pltpu.VMEM((t, D), jnp.float32),
-    ]
-    params = dict(vmem_limit_bytes=48 * 1024 * 1024)
-    if fast:
-        in_specs += [ANY] * 3
-        args += [dec_t, a, g]
-        out_specs += [ANY] * 3
-        out_shape += [shaped((32 * dec_t.shape[0], D)), dims(jnp.bfloat16), dims(jnp.bfloat16)]
-        scratch += gather_sems(1) + token_sems(2)
-        params.update(collective_id=1, has_side_effects=True)
+    dims = lambda kind, n=t, width=D: jax.ShapeDtypeStruct((n, width), kind)
+    bf, f32 = jnp.bfloat16, jnp.float32
     return pl.pallas_call(
-        functools.partial(encode_kernel, fast, t, nk - t),
-        grid=(PAIRS + CHUNKS,),
-        in_specs=in_specs,
-        out_specs=out_specs,
-        out_shape=out_shape,
-        scratch_shapes=scratch,
-        compiler_params=pltpu.CompilerParams(**params),
+        encode_kernel,
+        grid=(1 + PAIRS + CHUNKS,),
+        in_specs=[
+            tok, whole_spec((extra, D)), whole_spec((t, 128)), whole_spec((2 * nk, 128)), whole_spec(gains.shape),
+            pl.BlockSpec((3 * D, D), lambda i: (0, 0)),
+            pl.BlockSpec((D, D), lambda i: (3, 0)),
+            pl.BlockSpec((CHUNK, D), lambda i: (4 * D // CHUNK + chunk(i), 0)),
+            pl.BlockSpec((CHUNK, D), lambda i: (4 * D // CHUNK + CHUNKS + chunk(i), 0)),
+            ANY, ANY, whole_spec(g.shape),
+        ],
+        out_specs=[whole_spec((nk, D)), tok, tok, tok, tok, tok, tok, tok] + [ANY] * 5,
+        out_shape=[
+            dims(bf, nk), dims(bf), dims(bf), dims(f32), dims(f32), dims(bf), dims(f32), dims(bf),
+            dims(bf, nk, 2 * D), dims(bf, nk, 2 * D), dims(bf, 32 * dec_t.shape[0]), dims(bf), dims(bf),
+        ],
+        scratch_shapes=[
+            pltpu.VMEM((nk, 2 * D), bf), pltpu.VMEM((nk, 2 * D), bf),
+            pltpu.VMEM((t // QB, 2 * nk, 2 * QB), f32), pltpu.VMEM((t, D), f32), pltpu.VMEM(g.shape, bf), dma(4),
+        ] + gather_sems(1) + token_sems(2),
+        compiler_params=pltpu.CompilerParams(collective_id=1, has_side_effects=True, vmem_limit_bytes=48 * 1024 * 1024),
         name="encode",
-    )(*args)
+    )(x, pre, qaug, kaug, gains, enc_w, enc_w, enc_w, enc_w, dec_t, a, g)
 
 
 def encode_back_kernel(
-    fast, own_len, extra,
-    grad_ref, nf1_ref, h1_ref, gains, wo_ref, w1_ref, w2_ref, o_ref,
-    q_ref, qaug_ref, own_k, own_v, oth_k, oth_v, kaug_ref, lse_ref, *rest,
+    grad_ref, nf1_ref, h1_ref, nq_ref, gains, wo_ref, w1_ref, w2_ref, o_ref,
+    q_ref, qaug_ref, own_k, own_v, oth_k, oth_v, kaug_ref, lse_ref, dec_g, y_in, a_in,
+    whole, grad_h_ref, dgain_ref, dq_ref, dkv_ref, dec_out, y_out, a_out,
+    total_ref, grad_b, mix_ref, slots, dwo_ref, sems, sem_o, dk_acc, dv_acc, dko_ref, dvo_ref, dkt_ref, dvt_ref,
+    dqp_ref, own_d, sent, got, x_s, x_r, sem_w, *rest,
 ):
     i = pl.program_id(0)
-    if fast:
-        dec_g, y_in, a_in = rest[:3]
-        rest = rest[3:]
-    whole, grad_h_ref, dgain_ref, dq_ref, dko_ref, dvo_ref, dkt_ref, dvt_ref = rest[:8]
-    rest = rest[8:]
-    if fast:
-        dec_out, y_out, a_out = rest[:3]
-        rest = rest[3:]
-    total_ref, grad_b, mix_ref, slots, dwo_ref, sems, sem_o, dk_acc, dv_acc = rest[:9]
+    t = q_ref.shape[0]
+    nk = own_k.shape[0]
     store = ChunkStore(slots, whole, (4 * D, 4 * D + FF), sems)
     store_o = lambda: pltpu.make_async_copy(dwo_ref, whole.at[pl.ds(3 * D, D)], sem_o)
-    if fast:
-        rest = rest[9:]
-        mail = Mail(position())
-        reduce = Reduce(mail, dec_g, dec_out, rest[:5], rest[5:15])
-        tokens = TokensOut(mail, ((y_in, y_out), (a_in, a_out)), rest[15:])
-        steps = reduce_order(reduce)
-        places = {1: (0,), 2: (1,), 4: (2, 3), 7: (4, 6), 8: (5,), 10: (7, 8)}
-
-        @pl.when(i == 0)
-        def _():
-            greet(mail.pos)
-            reduce.start()
-            tokens.start(0)
-            tokens.start(1)
-
-        for at, which in places.items():
-
-            @pl.when(i == at)
-            def _(which=which):
-                for n in which:
-                    steps[n]()
+    mail = Mail(position())
+    near, m = mail.pos[3], mail.pos[1]
+    reduce = Reduce(mail, dec_g, dec_out, rest[:5], rest[5:15])
+    tokens = TokensOut(mail, ((y_in, y_out), (a_in, a_out)), rest[15:])
+    steps = reduce_order(reduce)
+    places = {1: (0,), 2: (1,), 4: (2,), 7: (3,), 8: (4,), 10: (5,), 11: (6,)}
 
     @pl.when(i == 0)
     def _():
+        greet(mail.pos)
+        reduce.start()
+        tokens.start(0)
+        tokens.start(1)
         grad_b[...] = grad_ref[...].astype(jnp.bfloat16)
+
+    for at, which in places.items():
+
+        @pl.when(i == at)
+        def _(which=which):
+            for n in which:
+                steps[n]()
 
     @pl.when(i < CHUNKS)
     def _():
@@ -1011,73 +1157,91 @@
         store.wait(i - 1)
         store.wait(i)
 
+    def swap(n):
+        slot = lax.rem(n, 2)
+        return remote(sent.at[slot], got.at[n], x_s.at[slot], x_r.at[n], (near, m))
+
     @pl.when(i >= CHUNKS)
     def _():
-        cols = pl.ds(pl.multiple_of((i - CHUNKS) * 128, 128), 128)
+        n = jnp.maximum(i - CHUNKS, 0)
+        o, mix, dq = column((o_ref, mix_ref, dq_ref), 0, n)
         back_pair(
-            False, own_len, extra, chunk_sets(False, own_len, extra)[0], q_ref, qaug_ref, own_k, own_v, oth_k, oth_v, kaug_ref,
-            o_ref.at[:, cols], lse_ref, mix_ref.at[:, cols],
-            dq_ref, dko_ref, dvo_ref, dkt_ref, dvt_ref, dk_acc, dv_acc,
+            False, t, nk - t, chunk_sets(False, t, nk - t)[0], q_ref, qaug_ref, own_k, own_v, oth_k, oth_v, kaug_ref,
+            o, lse_ref, mix, dqp_ref, dko_ref, dvo_ref, dkt_ref, dvt_ref, dk_acc, dv_acc,
         )
+        dq[...] = dqp_ref[...]
+        own_d[n, 0] = dko_ref[...].astype(jnp.bfloat16)
+        own_d[n, 1] = dvo_ref[...].astype(jnp.bfloat16)
+        pl.when(n >= 2)(lambda: swap(n - 2).wait_send())
+        sent[lax.rem(n, 2), 0] = dkt_ref[...]
+        sent[lax.rem(n, 2), 1] = dvt_ref[...]
+        swap(n).start()
 
     @pl.when(i == PAIRS + CHUNKS - 1)
     def _():
         store_o().wait()
-        if fast:
-            for n in (9, 10, 11):
-                steps[n]()
-            reduce.finish()
-            tokens.finish()
-            mail.finish()
-
-
-def encode_back(fast, grad, nf1, h1, gains, enc_w, o, q, qaug, own_kv, oth_kv, kaug, lse, dec_g, y, a):
+        for n in range(PAIRS):
+            swap(n).wait_recv()
+            for b in (0, 1):
+                at = b * D + n * 128
+                dkv_ref[:, at : at + 128] = own_d[n, b] + got[n, b]
+        dwo_ref[...] = dot_tn(dq_ref[...], nq_ref[:t, :]).astype(jnp.bfloat16)
+        last = [pltpu.make_async_copy(dwo_ref, whole.at[pl.ds(0, D)], sem_w.at[0])]
+        for b in (1, 2):
+            slots[b - 1, :D, :] = dot_tn(dkv_ref[:, (b - 1) * D : b * D], nq_ref[...]).astype(jnp.bfloat16)
+            last.append(pltpu.make_async_copy(slots.at[b - 1, pl.ds(0, D)], whole.at[pl.ds(b * D, D)], sem_w.at[b]))
+        for copy in last:
+            copy.start()
+        for n in (7, 8):
+            steps[n]()
+        reduce.finish()
+        tokens.finish()
+        for copy in last:
+            copy.wait()
+        for n in (PAIRS - 2, PAIRS - 1):
+            swap(n).wait_send()
+        mail.finish()
+
+
+def encode_back(grad, nf1, h1, nq, gains, enc_w, o, q, qaug, own_kv, oth_kv, kaug, lse, dec_g, y, a):
     t = q.shape[0]
     nk = own_kv.shape[0]
+    size = dec_g.shape[0] // 32
     pair = lambda i: jnp.maximum(i - CHUNKS, 0)
     chunk = lambda i: jnp.minimum(i, CHUNKS - 1)
     col = lambda first: pl.BlockSpec((nk, 128), lambda i: (0, first + pair(i)))
     cols = pl.BlockSpec((t, 128), lambda i: (0, pair(i)))
     tok = whole_spec((t, D))
-    dims = lambda kind, n=t: jax.ShapeDtypeStruct((n, D), kind)
-    in_specs = [
-        tok, tok, tok, whole_spec(gains.shape),
-        pl.BlockSpec((D, D), lambda i: (3, 0)),
-        pl.BlockSpec((CHUNK, D), lambda i: (4 * D // CHUNK + chunk(i), 0)),
-        pl.BlockSpec((CHUNK, D), lambda i: (4 * D // CHUNK + CHUNKS + chunk(i), 0)),
-        tok, cols, whole_spec((t, 128)), col(0), col(PAIRS), col(0), col(PAIRS), whole_spec((2 * nk, 128)), cols,
-    ]
-    args = [grad, nf1, h1, gains, enc_w, enc_w, enc_w, o, q, qaug, own_kv, own_kv, oth_kv, oth_kv, kaug, lse]
-    out_specs = [pl.BlockSpec(memory_space=pl.ANY), tok, whole_spec((8, D)), cols, col(0), col(0), col(0), col(0)]
-    out_shape = [
-        jax.ShapeDtypeStruct(enc_w.shape, jnp.bfloat16), dims(jnp.float32), dims(jnp.float32, 8), dims(jnp.bfloat16),
-        dims(jnp.float32, nk), dims(jnp.float32, nk), dims(jnp.bfloat16, nk), dims(jnp.bfloat16, nk),
-    ]
-    scratch = [
-        pltpu.VMEM((t, D), jnp.float32), pltpu.VMEM((t, D), jnp.bfloat16), pltpu.VMEM((t, D), jnp.bfloat16),
-        pltpu.VMEM((2, 2, CHUNK, D), jnp.bfloat16), pltpu.VMEM((D, D), jnp.bfloat16),
-        pltpu.SemaphoreType.DMA((2, 2)), pltpu.SemaphoreType.DMA,
-        pltpu.VMEM((2 * nk, 128), jnp.float32), pltpu.VMEM((2 * nk, 128), jnp.float32),
-    ]
-    params = dict(vmem_limit_bytes=60 * 1024 * 1024)
-    if fast:
-        size = dec_g.shape[0] // 32
-        in_specs += [ANY] * 3
-        args += [dec_g, y, a]
-        out_specs += [ANY] * 3
-        out_shape += [shaped((size, D)), shaped((2, t // 2, D)), shaped((2, t // 2, D))]
-        scratch += reduce_buffers(size) + reduce_sems() + token_sems(2)
-        params.update(collective_id=2, has_side_effects=True)
+    bf, f32 = jnp.bfloat16, jnp.float32
+    dims = lambda kind, n=t, width=D: jax.ShapeDtypeStruct((n, width), kind)
     return pl.pallas_call(
-        functools.partial(encode_back_kernel, fast, t, nk - t),
+        encode_back_kernel,
         grid=(PAIRS + CHUNKS,),
-        in_specs=in_specs,
-        out_specs=out_specs,
-        out_shape=out_shape,
-        scratch_shapes=scratch,
-        compiler_params=pltpu.CompilerParams(**params),
+        in_specs=[
+            once((t, D)), once((t, D)), once((t, D)), once((nk, D)), whole_spec(gains.shape),
+            pl.BlockSpec((D, D), lambda i: (3, 0)),
+            pl.BlockSpec((CHUNK, D), lambda i: (4 * D // CHUNK + chunk(i), 0)),
+            pl.BlockSpec((CHUNK, D), lambda i: (4 * D // CHUNK + CHUNKS + chunk(i), 0)),
+            once((t, D)), cols, whole_spec((t, 128)), col(0), col(PAIRS), col(0), col(PAIRS), whole_spec((2 * nk, 128)), cols,
+            ANY, ANY, ANY,
+        ],
+        out_specs=[ANY, tok, whole_spec((8, D)), tok, whole_spec((nk, 2 * D)), ANY, ANY, ANY],
+        out_shape=[
+            dims(bf, enc_w.shape[0]), dims(f32), dims(f32, 8), dims(bf), dims(bf, nk, 2 * D),
+            shaped((size, D)), shaped((2, t // 2, D)), shaped((2, t // 2, D)),
+        ],
+        scratch_shapes=[
+            pltpu.VMEM((t, D), f32), pltpu.VMEM((t, D), bf), pltpu.VMEM((t, D), bf),
+            pltpu.VMEM((2, 2 * CHUNK, D), bf), pltpu.VMEM((D, D), bf), dma(2, 2), dma(),
+            pltpu.VMEM((2 * nk, 128), f32), pltpu.VMEM((2 * nk, 128), f32),
+            pltpu.VMEM((nk, 128), f32), pltpu.VMEM((nk, 128), f32), pltpu.VMEM((nk, 128), bf), pltpu.VMEM((nk, 128), bf),
+            pltpu.VMEM((t, 128), bf), pltpu.VMEM((PAIRS, 2, nk, 128), bf),
+            pltpu.VMEM((2, 2, nk, 128), bf), pltpu.VMEM((PAIRS, 2, nk, 128), bf), dma(2), dma(PAIRS),
+            dma(3),
+        ] + reduce_buffers(size) + reduce_sems() + token_sems(2),
+        compiler_params=pltpu.CompilerParams(collective_id=2, has_side_effects=True, vmem_limit_bytes=63 * 1024 * 1024),
         name="encode_back",
-    )(*args)
+    )(grad, nf1, h1, nq, gains, enc_w, enc_w, enc_w, o, q, qaug, own_kv, own_kv, oth_kv, oth_kv, kaug, lse, dec_g, y, a)
 
 
 def project(left, weight_t):
@@ -1095,6 +1259,15 @@
 def output_back(grad, mixed_b, w_out):
     grad_b = grad.astype(jnp.bfloat16)
     return (outer_sum(mixed_b, grad_b), project(grad_b, w_out).astype(jnp.bfloat16))
+
+
+def feed_back(grad, normed_b, pre_act, act_b, w_in, w_out):
+    grad_b = grad.astype(jnp.bfloat16)
+    grad_wout = outer_sum(act_b, grad_b)
+    grad_act = project(grad_b, w_out)
+    unused, pull = jax.vjp(jax.nn.gelu, pre_act)
+    grad_pre = pull(grad_act)[0].astype(jnp.bfloat16)
+    return (outer_sum(grad_pre, normed_b), grad_wout, project_back(grad_pre, w_in))
 
 
 def partner(values):
@@ -1146,8 +1319,7 @@
     return lax.psum_scatter(grads, ("rows", "mem"), scatter_dimension=0, tiled=True)
 
 
-def on_device(
-    fast,
+def on_device_general(
     questions,
     answers,
     q_segments,
@@ -1164,30 +1336,29 @@
     core = lax.axis_index("rows") % 2
     per_row, slots = entry_alive_flags.shape[1], entry_alive_flags.shape[2]
     half = per_row // 2
-    rows_here, row_len = q_segments.shape
-    segs = jnp.concatenate([q_segments, a_segments, entry_alive_flags.reshape(rows_here, -1)], 1)
-    if fast:
-        segs = jnp.pad(segs, ((0, 0), (0, -segs.shape[1] % 1024))).reshape(rows_here, -1, 128)
-        own_ids = entry_ids.reshape(rows_here, -1)
-        n_ids = own_ids.shape[1]
-        own_ids = jnp.pad(own_ids, ((0, 0), (0, 1024 - n_ids))).reshape(rows_here, 8, 128)
-        enc_w, x_question, other_segs, ids = gather_encoder(enc_params.T, questions, segs, own_ids)
-        mem = lax.axis_index("mem")
-        numbers = jnp.where(
-            mem // 2 == core, lax.dynamic_index_in_dim(segs, mem % 2, 0, keepdims=False), other_segs
-        ).reshape(-1)
-        ids = ids.reshape(ids.shape[0], -1)[:, :n_ids].reshape(ids.shape[0], per_row, -1)
-        ids = ids.transpose(1, 0, 2).reshape(-1)
-    else:
-        enc_w, dec_w = gather_weights(enc_params), gather_weights(dec_params)
-        ids = my_row(lax.all_gather(entry_ids, "mem", axis=2, tiled=True)).reshape(-1)
-        numbers = my_row(segs)
-        x_question, x_answer = to_rows(questions), to_rows(answers)
-        grad_top = to_rows(cotangent.astype(jnp.bfloat16))
-    gains = jnp.pad(norm_gains, ((0, 2), (0, 0)))
+    enc_w = gather_weights(enc_params)
+    dec_w = gather_weights(dec_params)
+    all_ids = lax.all_gather(entry_ids, "mem", axis=2, tiled=True)
+    rows_here = questions.shape[0]
+    numbers = my_row(
+        jnp.concatenate(
+            [
+                q_segments,
+                a_segments,
+                entry_alive_flags.reshape(rows_here, -1),
+                all_ids.reshape(rows_here, -1),
+            ],
+            1,
+        )
+    )
+    row_len = q_segments.shape[1]
     q_row = numbers[:row_len]
     a_row = numbers[row_len : 2 * row_len]
     alive = numbers[2 * row_len : 2 * row_len + per_row * slots]
+    ids = numbers[2 * row_len + per_row * slots :]
+    x_question = to_rows(questions).astype(jnp.float32)
+    x_answer = to_rows(answers).astype(jnp.float32)
+    grad_top = to_rows(cotangent.astype(jnp.bfloat16)).astype(jnp.float32)
 
     own_ids = lax.dynamic_slice_in_dim(ids, core * half * slots, half * slots, 0)
     entry_vals = memory_table[own_ids].reshape(half * slots * 2, D).astype(jnp.float32)
@@ -1213,23 +1384,24 @@
     self_aug = seg_aug_k(jnp.concatenate([own_a, other_a]))
     cross_aug = seg_aug_k(jnp.concatenate([own_q, other_q]))
 
-    enc_in = jnp.concatenate([x_question.astype(jnp.float32), jnp.pad(entry_vals, ((0, extra - n_prefix), (0, 0)))], 0)
+    enc_in = jnp.concatenate([x_question, jnp.pad(entry_vals, ((0, extra - n_prefix), (0, 0)))], 0)
     normed_q = rms_norm(enc_in, norm_gains[0]).astype(jnp.bfloat16)
     query_enc = project(normed_q[:tokens], enc_w[:D]).astype(jnp.bfloat16)
     enc_kv = project(normed_q, enc_w[D : 3 * D]).astype(jnp.bfloat16)
     enc_kv_other = partner(enc_kv)
 
-    mixed_enc, logsum_enc, hidden_one, normed_f1, hidden_two, encoded, *gathered = encode(
-        fast, query_enc, q_aug, enc_kv, enc_kv_other, enc_aug, x_question, gains, enc_w,
-        dec_params.T, answers, cotangent.astype(jnp.bfloat16),
-    )
-    if fast:
-        dec_w, x_answer, grad_top = gathered
-    x_answer = x_answer.astype(jnp.float32)
     normed_a = rms_norm(x_answer, norm_gains[2]).astype(jnp.bfloat16)
     qkv_self = project(normed_a, dec_w[: 3 * D]).astype(jnp.bfloat16)
     query_self, self_kv = qkv_self[:, :D], qkv_self[:, D:]
     self_kv_other = partner(self_kv)
+
+    mixed_enc, logsum_enc = attend(False, core, query_enc, q_aug, enc_kv, enc_kv_other, enc_aug)
+    hidden_one = x_question + project_back(mixed_enc, enc_w[3 * D : 4 * D])
+    normed_f1 = rms_norm(hidden_one, norm_gains[1]).astype(jnp.bfloat16)
+    pre_enc = project(normed_f1, enc_w[4 * D : 4 * D + FF])
+    act_enc = jax.nn.gelu(pre_enc).astype(jnp.bfloat16)
+    hidden_two = hidden_one + project_back(act_enc, enc_w[4 * D + FF :])
+    encoded = rms_norm(hidden_two, norm_gains[5]).astype(jnp.bfloat16)
     cross_kv = project(encoded, dec_w[5 * D : 7 * D]).astype(jnp.bfloat16)
     cross_kv_other = partner(cross_kv)
 
@@ -1240,9 +1412,19 @@
     mixed_cross, logsum_cross = attend(
         False, core, query_cross, a_aug, cross_kv, cross_kv_other, cross_aug
     )
-    decoded, grad_two, grad_mixc, grad_gain4, dec_full = decode_top(
-        dec_one, mixed_cross, gains, grad_top, dec_w
-    )
+    dec_two = dec_one + project_back(mixed_cross, dec_w[7 * D : 8 * D])
+    normed_f2 = rms_norm(dec_two, norm_gains[4]).astype(jnp.bfloat16)
+    pre_dec = project(normed_f2, dec_w[8 * D : 8 * D + FF])
+    act_dec = jax.nn.gelu(pre_dec).astype(jnp.bfloat16)
+    dec_three = dec_two + project_back(act_dec, dec_w[8 * D + FF :])
+    decoded = from_rows(dec_three.astype(jnp.bfloat16))
+
+    grad_w1d, grad_w2d, grad_nf2 = feed_back(
+        grad_top, normed_f2, pre_dec, act_dec, dec_w[8 * D : 8 * D + FF], dec_w[8 * D + FF :]
+    )
+    grad_x, grad_gain4 = norm_back(dec_two, norm_gains[4], grad_nf2)
+    grad_two = grad_top + grad_x
+    grad_woc, grad_mixc = output_back(grad_two, mixed_cross, dec_w[7 * D : 8 * D])
     grad_qc, dk_own, dv_own, dk_other, dv_other = attend_back(
         False, core, query_cross, a_aug, cross_kv, cross_kv_other, cross_aug,
         mixed_cross, logsum_cross, grad_mixc,
@@ -1268,15 +1450,21 @@
     grad_self = jnp.concatenate([grad_qs, grad_skv], 1)
     grad_wself = outer_sum(grad_self, normed_a)
     grad_x, grad_gain2 = norm_back(x_answer, norm_gains[2], project_back(grad_self, dec_w[: 3 * D]))
-    grad_answers = (grad_one + grad_x).astype(jnp.bfloat16)
-    dec_full = dec_full.at[: 3 * D].set(grad_wself)
-    dec_full = dec_full.at[3 * D : 4 * D].set(grad_wos)
-    dec_full = dec_full.at[4 * D : 5 * D].set(grad_wqc)
-    dec_full = dec_full.at[5 * D : 7 * D].set(grad_wckv)
-
-    enc_full, grad_hidden, grad_gain1, grad_qe, dk_own, dv_own, dk_other, dv_other, *reduced = encode_back(
-        fast, grad_encoded, normed_f1, hidden_one, gains, enc_w, mixed_enc, query_enc, q_aug,
-        enc_kv, enc_kv_other, enc_aug, logsum_enc, dec_full, decoded, grad_answers,
+    grad_answers = from_rows((grad_one + grad_x).astype(jnp.bfloat16)).astype(jnp.float32)
+    dec_full = jnp.concatenate(
+        [grad_wself, grad_wos, grad_wqc, grad_wckv, grad_woc, grad_w1d, grad_w2d], 0
+    )
+    grad_decoder = reduce_weights(dec_full).astype(jnp.float32).T
+
+    grad_w1e, grad_w2e, grad_nf1 = feed_back(
+        grad_encoded, normed_f1, pre_enc, act_enc, enc_w[4 * D : 4 * D + FF], enc_w[4 * D + FF :]
+    )
+    grad_x, grad_gain1 = norm_back(hidden_one, norm_gains[1], grad_nf1)
+    grad_hidden = grad_encoded + grad_x
+    grad_woe, grad_mixe = output_back(grad_hidden, mixed_enc, enc_w[3 * D : 4 * D])
+    grad_qe, dk_own, dv_own, dk_other, dv_other = attend_back(
+        False, core, query_enc, q_aug, enc_kv, enc_kv_other, enc_aug,
+        mixed_enc, logsum_enc, grad_mixe,
     )
     more = partner(jnp.concatenate([dk_other, dv_other], 1)).astype(jnp.float32)
     grad_ekv = (jnp.concatenate([dk_own, dv_own], 1) + more).astype(jnp.bfloat16)
@@ -1285,38 +1473,141 @@
     grad_in = project_back(grad_ekv, enc_w[D : 3 * D])
     grad_in = grad_in + jnp.pad(project_back(grad_qe, enc_w[:D]), ((0, extra), (0, 0)))
     grad_x, grad_gain0 = norm_back(enc_in, norm_gains[0], grad_in)
-    grad_questions = (grad_hidden + grad_x[:tokens]).astype(jnp.bfloat16)
-    enc_full = enc_full.at[:D].set(grad_wqe)
-    enc_full = enc_full.at[D : 3 * D].set(grad_wkve)
+    grad_questions = from_rows((grad_hidden + grad_x[:tokens]).astype(jnp.bfloat16)).astype(jnp.float32)
+    enc_full = jnp.concatenate([grad_wqe, grad_wkve, grad_woe, grad_w1e, grad_w2e], 0)
     gain_terms = jnp.concatenate(
-        [grad_gain0, grad_gain1[:1], grad_gain2, grad_gain3, grad_gain4[:1], grad_gain5], 0
-    )
-    if fast:
-        grad_decoder, decoded, grad_answers = reduced
-        grad_encoder, grad_questions, grad_gains = reduce_encoder(
-            enc_full, grad_questions, jnp.pad(gain_terms, ((0, 2), (0, 0)))
-        )
-        grad_gains = grad_gains[:6]
-    else:
-        decoded, grad_questions, grad_answers = (
-            from_rows(values) for values in (decoded, grad_questions, grad_answers)
-        )
-        grad_gains = lax.psum(gain_terms, ("rows", "mem"))
-        grad_encoder, grad_decoder = reduce_weights(enc_full), reduce_weights(dec_full)
+        [grad_gain0, grad_gain1, grad_gain2, grad_gain3, grad_gain4, grad_gain5], 0
+    )
+    grad_gains = lax.psum(gain_terms, ("rows", "mem"))
+    grad_encoder = reduce_weights(enc_full).astype(jnp.float32).T
+    return (decoded, grad_questions, grad_answers, grad_encoder, grad_decoder, grad_gains)
+
+
+def on_device_fast(
+    questions,
+    answers,
+    q_segments,
+    a_segments,
+    entry_ids,
+    entry_alive_flags,
+    memory_table,
+    enc_params,
+    dec_params,
+    norm_gains,
+    cotangent,
+):
+    quarter = questions.shape[1]
+    core = lax.axis_index("rows") % 2
+    mem = lax.axis_index("mem")
+    per_row, slots = entry_alive_flags.shape[1], entry_alive_flags.shape[2]
+    half = per_row // 2
+    rows_here, row_len = q_segments.shape
+    n_mem = slots // entry_ids.shape[2]
+    entries = fetch(entry_ids.reshape(-1), memory_table).reshape(rows_here, 2, -1, D)
+    n_entry = entries.shape[2]
+    piece = -(-n_entry // 32) * 32
+    entries = jnp.pad(entries, ((0, 0), (0, 0), (0, piece - n_entry), (0, 0)))
+    enc_w, x_question, *others, prefix, dec_t = gather_encoder(
+        enc_params.T, questions, q_segments, a_segments, entry_alive_flags, entries, dec_params
+    )
+    prefix = prefix.reshape(-1, D)
+    gains = norm_gains
+
+    def mine(own, other):
+        return lax.dynamic_index_in_dim(jnp.where(mem // 2 == core, own, other), mem % 2, 0, keepdims=False)
+
+    q_row, a_row, alive = (
+        mine(own, other) for own, other in zip((q_segments, a_segments, entry_alive_flags), others)
+    )
+    alive = alive.reshape(per_row, n_mem, -1)
+
+    def prefix_segments(which):
+        live = lax.dynamic_slice_in_dim(alive, which * half, half, 0)
+        question = which * half + jnp.arange(half, dtype=jnp.int32)[:, None, None]
+        found = jnp.where(live == 1, question, -1).transpose(1, 0, 2).reshape(n_mem, -1)
+        found = jnp.repeat(found, 2, axis=1)
+        return jnp.pad(found, ((0, 0), (0, piece - n_entry)), constant_values=-1).reshape(-1)
+
+    own_q = own_quarters(q_row, core, quarter)
+    other_q = own_quarters(q_row, 1 - core, quarter)
+    own_a = own_quarters(a_row, core, quarter)
+    other_a = own_quarters(a_row, 1 - core, quarter)
+    q_aug, a_aug = seg_aug_q(own_q), seg_aug_q(own_a)
+    enc_aug = seg_aug_k(
+        jnp.concatenate([own_q, prefix_segments(core), other_q, prefix_segments(1 - core)])
+    )
+    self_aug = seg_aug_k(jnp.concatenate([own_a, other_a]))
+    cross_aug = seg_aug_k(jnp.concatenate([own_q, other_q]))
+
+    (
+        normed_q, query_enc, mixed_enc, logsum_enc, hidden_one, normed_f1, hidden_two, encoded,
+        enc_kv, enc_kv_other, dec_w, x_answer, grad_top,
+    ) = encode(
+        x_question, prefix, q_aug, enc_aug, gains, enc_w, dec_t, answers, cotangent
+    )
+    normed_a = rms_norm(x_answer.astype(jnp.float32), norm_gains[2]).astype(jnp.bfloat16)
+    qkv_self = project(normed_a, dec_w[: 3 * D]).astype(jnp.bfloat16)
+    query_self, self_kv = qkv_self[:, :D], qkv_self[:, D:]
+    self_kv_other = partner(self_kv)
+    cross_kv = project(encoded, dec_w[5 * D : 7 * D]).astype(jnp.bfloat16)
+    cross_kv_other = partner(cross_kv)
+
+    mixed_self, logsum_self = attend(True, core, query_self, a_aug, self_kv, self_kv_other, self_aug)
+    dec_one = x_answer.astype(jnp.float32) + project_back(mixed_self, dec_w[3 * D : 4 * D])
+    normed_c = rms_norm(dec_one, norm_gains[3]).astype(jnp.bfloat16)
+    query_cross = project(normed_c, dec_w[4 * D : 5 * D]).astype(jnp.bfloat16)
+    mixed_cross, logsum_cross = attend(
+        False, core, query_cross, a_aug, cross_kv, cross_kv_other, cross_aug
+    )
+    decoded, grad_two, grad_mixc, grad_gain4, dec_full = decode_top(
+        dec_one, mixed_cross, gains, grad_top, dec_w
+    )
+    grad_qc, dk_own, dv_own, dk_other, dv_other = attend_back(
+        False, core, query_cross, a_aug, cross_kv, cross_kv_other, cross_aug,
+        mixed_cross, logsum_cross, grad_mixc,
+    )
+    cross_got = partner(jnp.concatenate([dk_other, dv_other], 1))
+    grad_x, grad_gain3 = norm_back(dec_one, norm_gains[3], project_back(grad_qc, dec_w[4 * D : 5 * D]))
+    grad_one = grad_two + grad_x
+    grad_mixs = project(grad_one.astype(jnp.bfloat16), dec_w[3 * D : 4 * D]).astype(jnp.bfloat16)
+    grad_qs, dk_self, dv_self, dk_other, dv_other = attend_back(
+        True, core, query_self, a_aug, self_kv, self_kv_other, self_aug,
+        mixed_self, logsum_self, grad_mixs,
+    )
+    self_got = partner(jnp.concatenate([dk_other, dv_other], 1))
+    dec_full, grad_answers, grad_encoded, grad_gain2, grad_gain5 = decode_dense(
+        grad_qs, dk_self, dv_self, self_got, grad_qc, dk_own, dv_own, cross_got, normed_a, normed_c, encoded,
+        mixed_self, grad_one, x_answer, hidden_two, gains, dec_w, dec_full,
+    )
+
+    enc_full, grad_hidden, grad_gain1, grad_qe, grad_ekv, grad_decoder, decoded, grad_answers = encode_back(
+        grad_encoded, normed_f1, hidden_one, normed_q, gains, enc_w, mixed_enc, query_enc, q_aug,
+        enc_kv, enc_kv_other, enc_aug, logsum_enc, dec_full, decoded, grad_answers,
+    )
+    gain_terms = jnp.concatenate(
+        [
+            jnp.zeros_like(grad_gain3), grad_gain1[:1], grad_gain2[:1], grad_gain3, grad_gain4[:1], grad_gain5[:1],
+            jnp.zeros((2, D), jnp.float32),
+        ],
+        0,
+    )
+    grad_encoder, grad_questions, grad_gains = reduce_encoder(
+        enc_full, x_question, prefix, grad_qe, grad_ekv, enc_w, grad_hidden, gains, gain_terms
+    )
     return (
         decoded,
         grad_questions.astype(jnp.float32),
         grad_answers.astype(jnp.float32),
         grad_encoder.astype(jnp.float32).T,
         grad_decoder.astype(jnp.float32).T,
-        grad_gains,
+        grad_gains[:6],
     )
 
 
 def solution(mesh):
     fast = mesh.shape["rows"] == 8 and mesh.shape["mem"] == 4
     return jax.shard_map(
-        functools.partial(on_device, fast),
+        on_device_fast if fast else on_device_general,
         mesh=mesh,
         in_specs=(
             P("rows", "mem", None),

time: 569 us -> 497 us (0.87)
  matrix products: 58.5 us -> 17.3 us
  other arithmetic: 22.8 us -> 5.77 us
  local copies, waits for them, and re-layouts: 33.8 us -> 17.6 us
    dot_general x6 -> x0, matrix products: 17.8 us -> none  [outer_sum(): jnp.einsum('ne,nd->ed', wide, narrow, preferred_element_type=jnp.float32)]
    dot_general x6 -> x2, matrix products: 22 us -> 5.48 us  [project_back(): jnp.einsum('ne,ed->nd', left, weight_t, preferred_element_type=jnp.float32)]
    convert_element_type x7 -> x4, other arithmetic: 10.5 us -> 2.95 us  [the longest x1 1.25 us: on_device_fast(): grad_questions.astype(jnp.float32)]
    unnamed x104 -> x63, local copies, waits for them, and re-layouts: 20.5 us -> 13.5 us
    dot_general x6 -> x4, matrix products: 18.7 us -> 11.9 us  [project(): jnp.einsum('nd,ed->ne', left, weight_t, preferred_element_type=jnp.float32)]
    pallas_call x4 -> x6, Pallas kernels: 352 us -> 358 us  [the longest x1 98.3 us: encode_back(): pl.pallas_call(encode_back_kernel, grid=(PAIRS + CHUNKS,), in_specs=[once...]
  transfers between devices with their start and end apart: 6 -> 4, of which waited for: 1 -> 2; matrix products, arithmetic and copies ran while one was open for 9% -> 2% of each run, Pallas kernels for 2% -> 2%
where the time goes in v5:
time: 497 us; the launch traced here: 494 us
  Pallas kernels  445 us (90%)
  local copies, waits for them, and re-layouts  17.6 us (4%)
  matrix products  17.3 us (3%)
  other arithmetic  5.77 us (1%)
  waiting for transfers between devices  5.07 us (1%)
    pallas_call x1, Pallas kernels, encode_back(): pl.pallas_call(encode_back_kernel, grid=(PAIRS + CHUNKS,), in_specs=[once...  98.3 us
    pallas_call x1, Pallas kernels, encode(): pl.pallas_call(encode_kernel, grid=(1 + PAIRS + CHUNKS,), in_specs=[tok,...  93.1 us
    pallas_call x1, Pallas kernels, reduce_encoder(): pl.pallas_call(reduce_encoder_kernel, grid=(1,), in_specs=[ANY, whole_spe...  75.2 us
    pallas_call x1, Pallas kernels, gather_encoder(): pl.pallas_call(gather_encoder_kernel, in_specs=[ANY] * 6 + [vmem], out_sp...  69.7 us
    pallas_call x2, Pallas kernels, attend_back(): pl.pallas_call(functools.partial(back_kernel, causal, t, nk - t), grid_sp...  39.1 us
    pallas_call x1, Pallas kernels, decode_top(): pl.pallas_call(decode_top_kernel, grid=(n,), in_specs=[tok, tok, whole_sp...  24.9 us
    pallas_call x2, Pallas kernels, attend(): pl.pallas_call(functools.partial(attend_kernel, causal, t, nk - t), grid_...  22.7 us
    pallas_call x1, Pallas kernels, decode_dense(): pl.pallas_call(decode_dense_kernel, grid=(7,), in_specs=[tok, tok, tok, w...  15.3 us
  transfers between devices with their start and end apart: 4, of which 2 were waited for; matrix products, arithmetic and copies ran while one was open for 2% of the time, Pallas kernels for 2%

profile of v5, /device:TPU:0, one launch (start us, length us, event | category | flops | bytes accessed | tf_op | source)
XLA Modules:
  0.0 493.9 jit_solution(14914778765118390381)
XLA Ops:
  0.8 0.8 copy.27
  2.2 0.8 slice_reduce_fusion
  3.1 6.8 %fetch.1 = bf16[48,2,768]{2,1,0:T(2,128)(2,1)} custom-call(s32[48]{0:T(128)} %reshape.123.ids, bf16[4096,2,768]{2,1,0:T(2,128)(2,1)} %table.1), custom_call_target="tpu_custom_call" | custom-call | tf_op jit(solution)/shard_map/fetch/pallas_call | solution.py:972
  9.9 1.0 reshape.124
  11.0 69.7 %gather_encoder.1 = (bf16[9216,768]{1,0:T(8,128)(2,1)S(1)}, bf16[512,768]{1,0:T(8,128)(2,1)S(1)}, s32[2,1024]{1,0:T(2,128)S(1)}, s32[2,1024]{1,0:T(2,128)S(1)}, ...) custom-call(bf16[288,768]{1,0:T(8,128)(2,1)S(1)} %bitcast.35, ...), custom_call_target="tpu_custom_call" | custom-call | tf_op jit(solution)/shard_map/gather_encoder/pallas_call | solution.py:883
  80.7 5.0 %copy-done = bf16[9216,768]{1,0:T(8,128)(2,1)} copy-done((bf16[9216,768]{1,0:T(8,128)(2,1)}, bf16[9216,768]{1,0:T(8,128)(2,1)S(1)}, u32[]{:S(2)}) %copy-start) | copy-done | bytes 14155800
  85.7 0.9 copy-done.1
  88.2 93.1 %encode.1 = (bf16[640,768]{1,0:T(8,128)(2,1)}, bf16[512,768]{1,0:T(8,128)(2,1)S(1)}, bf16[512,768]{1,0:T(8,128)(2,1)S(1)}, f32[512,768]{1,0:T(8,128)}, f32[512,7...) custom-call(bf16[512,768]{1,0:T(8,128)(2,1)} %copy-done.1, ...), custom_call_target="tpu_custom_call" | custom-call | tf_op jit(solution)/shard_map/encode/pallas_call | solution.py:1080
  182.2 4.0 convolution_convert_fusion
  186.8 3.1 convolution_convert_fusion.1.refs_2_.refs_3_
  190.6 9.9 %attend.2 = (bf16[512,768]{1,0:T(8,128)(2,1)S(1)}, f32[512,768]{1,0:T(8,128)S(1)}) custom-call(s32[1]{0:T(128)} %bitcast.core, bf16[512,768]{1,0:T(8,128)(2,1)S(1)} %slice.55.refs_0_, bf16[512,128]{1,0:T(8,128)(2,1)S(1)} %get-tuple-element.144.refs_1_, bf16[512,1536]{1,0:T(8,128)(2,1)S(1)} %slice.56.refs_2_.refs_3_, ...), custom_call_target="tpu_custom_call" | custom-call | flops 1610612736 | bytes 3145728 | tf_op jit(solution)/shard_map/attend/pallas_call | solution.py:109
  200.4 2.7 multiply_reduce_fusion.2
  203.4 2.1 convolution_convert_fusion.3.refs_0_
  205.5 12.8 %attend.3 = (bf16[512,768]{1,0:T(8,128)(2,1)S(1)}, f32[512,768]{1,0:T(8,128)S(1)}) custom-call(s32[1]{0:T(128)} %bitcast.core, bf16[512,768]{1,0:T(8,128)(2,1)S(1)} %convolution_convert_fusion.3.refs_0_, bf16[512,128]{1,0:T(8,128)(2,1)S(1)} %get-tuple-element.144.refs_1_, bf16[512,1536]{1,0:T(8,128)(2,1)S(1)} %convolution_convert_fusion.1.refs_2_.refs_3_, ...), custom_call_target="tpu_custom_call" | custom-call | flops 1610612736 | bytes 3145728 | tf_op jit(solution)/shard_map/attend/pallas_call | solution.py:109
  218.3 24.9 %decode_top.1 = (bf16[512,768]{1,0:T(8,128)(2,1)S(1)}, f32[512,768]{1,0:T(8,128)S(1)}, bf16[512,768]{1,0:T(8,128)(2,1)S(1)}, f32[8,768]{1,0:T(8,128)S(1)}, bf16[12288,768]{1,0:T(8,128)(2,1)}) custom-call(f32[512,768]{1,0:T(8,128)S(1)} %get-tuple-element.147.d1_ref, bf16[512,768]{1,0:T(8,128)(2,1)S(1)} %get-tuple-element.73.mixed_ref.refs_7_, ...), custom_call_target="tpu_custom_call" | custom-call | flops 16911433728 | bytes 18874368 | tf_op jit(solution)/shard_map/decode_top/pallas_call | solution.py:384
  243.2 23.2 %attend_back.2 = (bf16[512,768]{1,0:T(8,128)(2,1)S(1)}, f32[512,768]{1,0:T(8,128)S(1)}, f32[512,768]{1,0:T(8,128)S(1)}, bf16[512,768]{1,0:T(8,128)(2,1)S(1)}, bf16[512,768]{1,0:T(8,128)(2,1)S(1)}) custom-call(s32[1]{0:T(128)} %bitcast.core, bf16[512,768]{1,0:T(8,128)(2,1)S(1)} %convolution_convert_fusion.3.refs_0_, ...), custom_call_target="tpu_custom_call" | custom-call | flops 4026531840 | bytes 9437184 | tf_op jit(solution)/shard_map/attend_back/pallas_call | solution.py:214
  266.4 2.8 multiply_reduce_fusion
  269.6 2.7 convolution_convert_fusion.2.refs_9_
  272.3 15.9 %attend_back.3 = (bf16[512,768]{1,0:T(8,128)(2,1)S(1)}, f32[512,768]{1,0:T(8,128)S(1)}, f32[512,768]{1,0:T(8,128)S(1)}, bf16[512,768]{1,0:T(8,128)(2,1)S(1)}, bf16[512,768]{1,0:T(8,128)(2,1)S(1)}) custom-call(s32[1]{0:T(128)} %bitcast.core, bf16[512,768]{1,0:T(8,128)(2,1)S(1)} %slice.55.refs_0_, bf16[512,128]{1,0:T(8,128)(2,1)S(1)} %get-tuple-element.144.refs_1_, ...), custom_call_target="tpu_custom_call" | custom-call | flops 4026531840 | bytes 9437184 | tf_op jit(solution)/shard_map/attend_back/pallas_call | solution.py:214
  289.2 2.8 collective-permute-done.2.kvs_got
  292.0 2.2 collective-permute-done.3.kvc_got
  294.3 1.1 copy-done.22
  295.4 15.3 %decode_dense.1 = (bf16[12288,768]{1,0:T(8,128)(2,1)}, bf16[512,768]{1,0:T(8,128)(2,1)S(1)}, f32[512,768]{1,0:T(8,128)S(1)}, f32[8,768]{1,0:T(8,128)S(1)}, f32[8,768]{1,0:T(8,128)S(1)}) custom-call(bf16[512,768]{1,0:T(8,128)(2,1)S(1)} %get-tuple-element.79.dqs_ref, f32[512,768]{1,0:T(8,128)S(1)} %get-tuple-element.80.dks_ref, ...), custom_call_target="tpu_custom_call", output_to_operand_aliasing={{0}: (17, {})} | custom-call | flops 7247757312 | bytes 19660800 | tf_op jit(solution)/shard_map/decode_dense/pallas_call | solution.py:477
  310.7 1.1 copy-done.4
  311.8 0.9 copy-done.10
  312.7 98.3 %encode_back.1 = (bf16[9216,768]{1,0:T(8,128)(2,1)}, f32[512,768]{1,0:T(8,128)}, f32[8,768]{1,0:T(8,128)}, bf16[512,768]{1,0:T(8,128)(2,1)}, bf16[640,1536]{1,0:...) custom-call(f32[512,768]{1,0:T(8,128)} %copy-done.4, ...), custom_call_target="tpu_custom_call" | custom-call | tf_op jit(solution)/shard_map/encode_back/pallas_call | solution.py:1217
  411.8 75.2 %reduce_encoder.1 = (bf16[288,768]{1,0:T(8,128)(2,1)S(1)}, bf16[2,256,768]{2,1,0:T(8,128)(2,1)S(1)}, f32[8,768]{1,0:T(8,128)S(1)}) custom-call(bf16[9216,768]{1,0:T(8,128)(2,1)} %get-tuple-element.103.enc_in, bf16[512,768]{1,0:T(8,128)(2,1)} %copy-done.1, bf16[128,768]{1,0:T(8,128)(2,1)S(1)} %bitcast.34, bf16[512,768]{1,0:T(8,128)(2,1)} %get-tuple-element.104.dq_ref, ...), custom_call_target="tpu_custom_call" | custom-call | tf_op jit(solution)/shard_map/reduce_encoder/pallas_call | solution.py:946
  487.1 1.3 convert_element_type.63
  488.3 1.0 convert_bitcast_fusion.1
  489.4 1.4 copy.35
  490.8 1.3 convert_element_type.64
  492.2 0.9 copy.51
  (113 shorter events, 7.4 us)
Async XLA Ops:
  3.0 7.9 %copy-start.11 = (bf16[2,256,768]{2,1,0:T(8,128)(2,1)S(1)}, bf16[2,256,768]{2,1,0:T(8,128)(2,1)}, u32[]{:S(2)}) copy-start(bf16[2,256,768]{2,1,0:T(8,128)(2,1)} %q_in.1) | copy-start | bytes 2359300
  3.0 7.9 %copy-start.12 = (bf16[768,384]{1,0:T(8,128)(2,1)S(1)}, bf16[768,384]{1,0:T(8,128)(2,1)}, u32[]{:S(2)}) copy-start(bf16[768,384]{1,0:T(8,128)(2,1)} %dec_ref.1) | copy-start | bytes 1769476
  3.0 7.9 %copy-start.15 = (bf16[768,288]{0,1:T(8,128)(2,1)S(1)}, bf16[768,288]{0,1:T(8,128)(2,1)}, u32[]{:S(2)}) copy-start(bf16[768,288]{0,1:T(8,128)(2,1)} %param.18) | copy-start | bytes 1327108
  3.0 7.9 %copy-start.16 = (s32[2,1024]{1,0:T(2,128)S(1)}, s32[2,1024]{1,0:T(2,128)}, u32[]{:S(2)}) copy-start(s32[2,1024]{1,0:T(2,128)} %qs_in.1) | copy-start | bytes 24580
  3.1 7.9 %copy-start.17 = (s32[2,1024]{1,0:T(2,128)S(1)}, s32[2,1024]{1,0:T(2,128)}, u32[]{:S(2)}) copy-start(s32[2,1024]{1,0:T(2,128)} %as_in.1) | copy-start | bytes 24580
  3.1 7.9 %copy-start.18 = (s32[2,8,12]{2,1,0:T(8,128)S(1)}, s32[2,8,12]{2,1,0:T(8,128)}, u32[]{:S(2)}) copy-start(s32[2,8,12]{2,1,0:T(8,128)} %al_in.1) | copy-start | bytes 2308
  10.9 77.2 %copy-start.13 = (f32[6,768]{1,0:T(8,128)S(1)}, f32[6,768]{1,0:T(8,128)}, u32[]{:S(2)}) copy-start(f32[6,768]{1,0:T(8,128)} %gains.9) | copy-start | bytes 55300
  80.6 5.0 %copy-start = (bf16[9216,768]{1,0:T(8,128)(2,1)}, bf16[9216,768]{1,0:T(8,128)(2,1)S(1)}, u32[]{:S(2)}) copy-start(bf16[9216,768]{1,0:T(8,128)(2,1)S(1)} %get-tuple-element.65.wqkv_ref.wo_ref.w1_ref.w2_ref.w_ref) | copy-start | bytes 42467332
  85.7 0.9 copy-start.1
  87.9 93.4 %copy-start.5 = (bf16[512,128]{1,0:T(8,128)(2,1)}, bf16[512,128]{1,0:T(8,128)(2,1)S(1)}, u32[]{:S(2)}) copy-start(bf16[512,128]{1,0:T(8,128)(2,1)S(1)} %get-tuple-element.145.qaug_ref) | copy-start | bytes 393220
  88.1 93.2 %copy-start.2 = (bf16[1280,128]{1,0:T(8,128)(2,1)}, bf16[1280,128]{1,0:T(8,128)(2,1)S(1)}, u32[]{:S(2)}) copy-start(bf16[1280,128]{1,0:T(8,128)(2,1)S(1)} %select_convert_fusion.kaug_ref) | copy-start | bytes 983044
  181.3 0.9 copy-start.6
  181.3 4.9 copy-start.7
  181.3 4.9 copy-start.8
  186.4 4.2 collective-permute-start
  189.9 15.5 %collective-permute-start.1 = (bf16[512,1536]{1,0:T(8,128)(2,1)S(1)}, bf16[512,1536]{1,0:T(8,128)(2,1)S(1)}, u32[]{:S(2)}, u32[]{:S(2)}) collective-permute-start(bf16[512,1536]{1,0:T(8,128)(2,1)S(1)} %convolution_convert_fusion.1.refs_2_.refs_3_), channel_id=1, source_target_pairs={{0,4},{4,0},{8,12},{12,8},{16,20},{20,16},{24,28},{28,24},{1,5},{5... | collective-permute-start | bytes 4718600 | tf_op jit(solution)/shard_map/ppermute | solution.py:1275
  200.4 2.7 copy-start.19
  243.2 23.2 %copy-start.9 = (bf16[512,768]{1,0:T(8,128)(2,1)}, bf16[512,768]{1,0:T(8,128)(2,1)S(1)}, u32[]{:S(2)}) copy-start(bf16[512,768]{1,0:T(8,128)(2,1)S(1)} %get-tuple-element.100.y_in) | copy-start | bytes 2359300
  266.4 2.8 copy-start.3
  269.6 2.7 copy-start.21
  269.6 2.7 copy-start.20
  288.4 3.7 collective-permute-start.2
  289.1 5.2 %collective-permute-start.3 = (bf16[512,1536]{1,0:T(8,128)(2,1)S(1)}, bf16[512,1536]{1,0:T(8,128)(2,1)S(1)}, u32[]{:S(2)}, u32[]{:S(2)}) collective-permute-start(bf16[512,1536]{1,0:T(8,128)(2,1)S(1)} %pad_maximum_fusion.1), channel_id=1, source_target_pairs={{0,4},{4,0},{8,12},{12,8},{16,20},{20,16},{24,28},{28,24},{1,5},{5... | collective-permute-start | bytes 4718600 | tf_op jit(solution)/shard_map/ppermute | solution.py:1275
  294.3 1.1 copy-start.22
  310.7 1.1 copy-start.4
  311.8 0.9 copy-start.10
  312.7 99.1 %copy-start.14 = (f32[6,768]{1,0:T(8,128)S(1)}, f32[6,768]{1,0:T(8,128)}, u32[]{:S(2)}) copy-start(f32[6,768]{1,0:T(8,128)} %gains.9) | copy-start | bytes 55300
  487.1 2.2 copy-start.25
  489.4 1.4 copy-start.24
  490.8 1.4 copy-start.23
